TPU v7x, 512 devices: a whole 4x8x8 slice. The times are simulated.
512 devices in a mesh: tm: 16 (over y_hi, z), space: 8 (over x, core), dp: 4 (over y_lo).
Axes of the slice: x: 4, y: 8 (y_hi: 2, y_lo: 4; y = y_hi * 4 + y_lo), z: 8, core: 2. Of those that a mesh axis runs over, the one named last changes fastest.
Arguments:
- time_query: bfloat16 [4, 128, 128, 768], P('dp', 'tm', 'space'), may hold values from -36 to 36
- time_key: bfloat16 [4, 128, 128, 768], P('dp', 'tm', 'space'), may hold values from -37 to 37
- time_value: bfloat16 [4, 128, 128, 768], P('dp', 'tm', 'space'), may hold values from -6 to 6
- residual_in: bfloat16 [4, 128, 128, 1024], P('dp', 'tm', 'space'), may hold values from -6 to 6
- fc_weight: bfloat16 [768, 1024], P(('tm', 'space')), may hold values from -0.21875 to 0.21875
- norm_gain: float32 [1024], replicated, may hold values from 0.25 to 1.75
- qkv_weight: bfloat16 [1024, 2304], P(('tm', 'space')), may hold values from -0.640625 to 0.640625
- out_weight: bfloat16 [768, 1024], P(('tm', 'space')), may hold values from -0.21875 to 0.21875
- bias_slope: float32 [12], replicated, may hold values from 0.01 to 0.3
- visible: int32 [4, 128], P('dp'), may hold values from 0 to 1023, as said below
- cotangent: bfloat16 [4, 128, 128, 1024], P('dp', 'tm', 'space'), may hold values from -6 to 6
Outputs:
- grad_residual: bfloat16 [4, 128, 128, 1024], P('dp', 'tm', 'space')
- grad_query: bfloat16 [4, 128, 128, 768], P('dp', 'tm', 'space')
- grad_key: bfloat16 [4, 128, 128, 768], P('dp', 'tm', 'space')
- grad_value: bfloat16 [4, 128, 128, 768], P('dp', 'tm', 'space')
Inputs may be any that keep to these rules, and one draw needn't show every extreme that they name: `visible`: each clip's 128 entries are distinct positions of a 32 x 32 grid; the same for all time steps.
All inputs are finite; a program needn't handle non-finite values.
Results may differ from a plain program's by a relative error of at most 0.018.
Values may be sent and summed in bfloat16 or wider, within the bound.
No kernel may reach another device: no remote copies, remote signals or barrier semaphores. Data moves between devices by JAX's collectives and lax.ppermute only.
A program may use at most 64 MiB of HBM per device.

v0:
```python
import jax
import jax.numpy as jnp
from jax import lax
from jax.sharding import PartitionSpec as P

HEADS = 12
HD = 64
GRID = 32


epsilon = 1e-05


def rounded(values):
    return lax.optimization_barrier(values.astype(jnp.bfloat16)).astype(jnp.float32)


def split_heads(block):
    return block.reshape(block.shape[:-1] + (HEADS, HD)).astype(jnp.float32)


def softmax_rows(scores):
    row_top = jnp.max(scores, axis=-1, keepdims=True)
    exponent = jnp.exp(scores - row_top)
    return exponent / jnp.sum(exponent, axis=-1, keepdims=True)


def temporal_probs(queries, key_rows):
    scores = jnp.einsum("tshd,ushd->shtu", split_heads(queries), split_heads(key_rows)) * HD ** (
        -0.5
    )
    return softmax_rows(scores)


def temporal_forward(queries, key_rows, value_rows):
    attend = temporal_probs(queries, key_rows)
    mixed_out = jnp.einsum("shtu,ushd->tshd", rounded(attend), split_heads(value_rows))
    return mixed_out.reshape(queries.shape).astype(jnp.bfloat16)


def temporal_backward(queries, key_rows, value_rows, grad_out):
    attend = temporal_probs(queries, key_rows)
    grad_attend = jnp.einsum("tshd,ushd->shtu", split_heads(grad_out), split_heads(value_rows))
    inner_sum = jnp.sum(attend * grad_attend, axis=-1, keepdims=True)
    grad_scores = rounded(attend * (grad_attend - inner_sum))
    score_scale = HD ** (-0.5)
    grad_q = jnp.einsum("shtu,ushd->tshd", grad_scores, split_heads(key_rows)) * score_scale
    grad_k = jnp.einsum("shtu,tshd->ushd", grad_scores, split_heads(queries)) * score_scale
    grad_v = jnp.einsum("shtu,tshd->ushd", rounded(attend), split_heads(grad_out))
    return (
        grad_q.reshape(queries.shape).astype(jnp.bfloat16),
        grad_k.reshape(queries.shape).astype(jnp.bfloat16),
        grad_v.reshape(queries.shape).astype(jnp.bfloat16),
    )


def distance_bias(tube_ids, bias_slope):
    tube_rows = tube_ids // GRID
    tube_cols = tube_ids % GRID
    distance = jnp.abs(tube_rows[:, None] - tube_rows[None, :]) + jnp.abs(
        tube_cols[:, None] - tube_cols[None, :]
    )
    return -bias_slope[:, None, None] * distance.astype(jnp.float32)[None]


def spatial_backward(queries, key_rows, value_rows, grad_out, pair_bias):
    score_scale = HD ** (-0.5)
    scores = (
        jnp.einsum("tihd,tjhd->thij", split_heads(queries), split_heads(key_rows)) * score_scale
    )
    attend = softmax_rows(scores + pair_bias[None])
    grad_attend = jnp.einsum("tihd,tjhd->thij", split_heads(grad_out), split_heads(value_rows))
    inner_sum = jnp.sum(attend * grad_attend, axis=-1, keepdims=True)
    grad_scores = rounded(attend * (grad_attend - inner_sum))
    grad_q = jnp.einsum("thij,tjhd->tihd", grad_scores, split_heads(key_rows)) * score_scale
    grad_k = jnp.einsum("thij,tihd->tjhd", grad_scores, split_heads(queries)) * score_scale
    grad_v = jnp.einsum("thij,tihd->tjhd", rounded(attend), split_heads(grad_out))
    return (
        grad_q.reshape(queries.shape).astype(jnp.bfloat16),
        grad_k.reshape(queries.shape).astype(jnp.bfloat16),
        grad_v.reshape(queries.shape).astype(jnp.bfloat16),
    )


def normalize(hidden):
    row_mean = jnp.mean(hidden, axis=-1, keepdims=True)
    centred = hidden - row_mean
    row_var = jnp.mean(centred * centred, axis=-1, keepdims=True)
    inv_std = lax.rsqrt(row_var + epsilon)
    return (centred * inv_std, inv_std)


def norm_backward(grad_normed, normed, inv_std, norm_gain, cot_rows):
    scaled_grad = grad_normed.astype(jnp.float32) * norm_gain
    first_mean = jnp.mean(scaled_grad, axis=-1, keepdims=True)
    second_mean = jnp.mean(scaled_grad * normed, axis=-1, keepdims=True)
    term = inv_std * (scaled_grad - first_mean - normed * second_mean)
    return (cot_rows.astype(jnp.float32) + term).astype(jnp.bfloat16)


def body(
    time_query,
    time_key,
    time_value,
    residual_in,
    fc_weight,
    norm_gain,
    qkv_weight,
    out_weight,
    bias_slope,
    visible,
    cotangent,
):
    fc_full, qkv_full, out_full = (
        lax.all_gather(fc_weight, ("tm", "space"), axis=0, tiled=True),
        lax.all_gather(qkv_weight, ("tm", "space"), axis=0, tiled=True),
        lax.all_gather(out_weight, ("tm", "space"), axis=0, tiled=True),
    )
    step_count, tube_count, inner_width = time_query.shape[1:]
    model_width = residual_in.shape[-1]
    local_shape = (1, step_count, tube_count, inner_width)
    tube_query, tube_key, tube_value = (
        lax.all_to_all(time_query, "tm", split_axis=2, concat_axis=1, tiled=True),
        lax.all_to_all(time_key, "tm", split_axis=2, concat_axis=1, tiled=True),
        lax.all_to_all(time_value, "tm", split_axis=2, concat_axis=1, tiled=True),
    )
    mixed_tube = temporal_forward(tube_query[0], tube_key[0], tube_value[0])
    mixed_out = lax.all_to_all(mixed_tube[None], "tm", split_axis=1, concat_axis=2, tiled=True)
    hidden = residual_in.reshape(-1, model_width).astype(jnp.float32) + jnp.dot(
        mixed_out.reshape(-1, inner_width), fc_full, preferred_element_type=jnp.float32
    )
    normed, inv_std = normalize(hidden)
    normed_in = (normed * norm_gain).astype(jnp.bfloat16)
    flat_cot = cotangent.reshape(-1, model_width)
    grad_mixed = jnp.dot(flat_cot, out_full.T, preferred_element_type=jnp.float32).astype(
        jnp.bfloat16
    )
    pair_bias = distance_bias(visible[0], bias_slope)
    projected = jnp.dot(normed_in, qkv_full, preferred_element_type=jnp.float32).astype(
        jnp.bfloat16
    )
    query_local = projected[:, :inner_width].reshape(local_shape)
    key_local = projected[:, inner_width : 2 * inner_width].reshape(local_shape)
    value_local = projected[:, 2 * inner_width :].reshape(local_shape)
    space_query, space_key, space_value, space_grad = (
        lax.all_to_all(query_local, "space", split_axis=1, concat_axis=2, tiled=True),
        lax.all_to_all(key_local, "space", split_axis=1, concat_axis=2, tiled=True),
        lax.all_to_all(value_local, "space", split_axis=1, concat_axis=2, tiled=True),
        lax.all_to_all(
            grad_mixed.reshape(local_shape), "space", split_axis=1, concat_axis=2, tiled=True
        ),
    )
    grad_list = spatial_backward(
        space_query[0], space_key[0], space_value[0], space_grad[0], pair_bias
    )
    back_query, back_key, back_value = (
        lax.all_to_all(grad_list[0][None], "space", split_axis=2, concat_axis=1, tiled=True),
        lax.all_to_all(grad_list[1][None], "space", split_axis=2, concat_axis=1, tiled=True),
        lax.all_to_all(grad_list[2][None], "space", split_axis=2, concat_axis=1, tiled=True),
    )
    joined = jnp.concatenate(
        [
            back_query.reshape(-1, inner_width),
            back_key.reshape(-1, inner_width),
            back_value.reshape(-1, inner_width),
        ],
        axis=-1,
    )
    grad_normed = jnp.dot(joined, qkv_full.T, preferred_element_type=jnp.float32).astype(
        jnp.bfloat16
    )
    grad_resid = norm_backward(grad_normed, normed, inv_std, norm_gain, flat_cot)
    grad_time = jnp.dot(grad_resid, fc_full.T, preferred_element_type=jnp.float32).astype(
        jnp.bfloat16
    )
    tube_grad = lax.all_to_all(
        grad_time.reshape(local_shape), "tm", split_axis=2, concat_axis=1, tiled=True
    )
    grad_q, grad_k, grad_v = temporal_backward(
        tube_query[0], tube_key[0], tube_value[0], tube_grad[0]
    )
    grad_query, grad_key, grad_value = (
        lax.all_to_all(grad_q[None], "tm", split_axis=1, concat_axis=2, tiled=True),
        lax.all_to_all(grad_k[None], "tm", split_axis=1, concat_axis=2, tiled=True),
        lax.all_to_all(grad_v[None], "tm", split_axis=1, concat_axis=2, tiled=True),
    )
    return (grad_resid.reshape(residual_in.shape), grad_query, grad_key, grad_value)


def solution(mesh):
    in_specs = (
        P("dp", "tm", "space", None),
        P("dp", "tm", "space", None),
        P("dp", "tm", "space", None),
        P("dp", "tm", "space", None),
        P(("tm", "space"), None),
        P(),
        P(("tm", "space"), None),
        P(("tm", "space"), None),
        P(),
        P("dp", None),
        P("dp", "tm", "space", None),
    )
    out_specs = (
        P("dp", "tm", "space", None),
        P("dp", "tm", "space", None),
        P("dp", "tm", "space", None),
        P("dp", "tm", "space", None),
    )
    return jax.shard_map(body, mesh=mesh, in_specs=in_specs, out_specs=out_specs, check_vma=False)
```

profile of v0, /device:TPU:16, one launch (start us, length us, event | category | flops | bytes accessed | tf_op | source)
XLA Modules:
  0.0 580.9 jit_solution(6431588132030807175)
XLA Ops:
  11.1 13.9 %all-to-all-start.1 = ((bf16[1,8,16,768]{3,1,0,2:T(8,128)(2,1)}), bf16[1,8,16,768]{3,1,0,2:T(8,128)(2,1)S(1)}, u32[]{:S(2)}, u32[]{:S(2)}) async-start(bf16[1,8,16,768]{3,1,0,2:T(8,128)(2,1)} %copy.106), calls=%async_computation.1 | async-start | bytes 393216 | tf_op jit(solution)/shard_map/all_to_all | solution.py:124
  26.6 12.7 %all-to-all-done.1 = bf16[1,8,16,768]{3,1,0,2:T(8,128)(2,1)S(1)} async-done(((bf16[1,8,16,768]{3,1,0,2:T(8,128)(2,1)}), bf16[1,8,16,768]{3,1,0,2:T(8,128)(2,1)S(1)}, u32[]{:S(2)}, u32[]{:S(2)}) %all-to-all-start.1) | async-done | bytes 196640 | tf_op jit(solution)/shard_map/all_to_all | solution.py:124
  43.6 13.1 %all-to-all-done.2 = bf16[1,8,16,768]{3,1,0,2:T(8,128)(2,1)S(1)} async-done(((bf16[1,8,16,768]{3,1,0,2:T(8,128)(2,1)}), bf16[1,8,16,768]{3,1,0,2:T(8,128)(2,1)S(1)}, u32[]{:S(2)}, u32[]{:S(2)}) %all-to-all-start.2) | async-done | bytes 196640 | tf_op jit(solution)/shard_map/all_to_all | solution.py:125
  61.7 11.7 %all-to-all-done = bf16[1,8,16,768]{3,1,0,2:T(8,128)(2,1)S(1)} async-done(((bf16[1,8,16,768]{3,1,0,2:T(8,128)(2,1)}), bf16[1,8,16,768]{3,1,0,2:T(8,128)(2,1)S(1)}, u32[]{:S(2)}, u32[]{:S(2)}) %all-to-all-start) | async-done | bytes 196640 | tf_op jit(solution)/shard_map/all_to_all | solution.py:123
  82.1 14.2 %all-to-all-done.3 = bf16[16,2,3072]{2,1,0:T(2,128)(2,1)S(1)} async-done(((bf16[16,2,3072]{2,1,0:T(2,128)(2,1)}), bf16[16,2,3072]{2,1,0:T(2,128)(2,1)S(1)}, u32[]{:S(2)}, u32[]{:S(2)}) %all-to-all-start.3) | async-done | bytes 196640 | tf_op jit(solution)/shard_map/all_to_all | solution.py:128
  96.5 49.7 %all-gather.10.cloned.1.call-done = bf16[128,6,1024]{2,1,0:T(8,128)(2,1)} async-done(((bf16[1,6,1024]{2,1,0:T(8,128)(2,1)}), bf16[128,6,1024]{2,1,0:T(8,128)(2,1)}) %all-gather.10.cloned.1.call-update) | async-done | bytes 1572880 | tf_op jit(solution)/shard_map/all_gather | solution.py:117
  150.2 4.3 all-to-all-start.6
  154.4 118.5 %all-gather.8.cloned.1.call-done = bf16[128,6,1024]{2,1,0:T(8,128)(2,1)} async-done(((bf16[1,6,1024]{2,1,0:T(8,128)(2,1)}), bf16[128,6,1024]{2,1,0:T(8,128)(2,1)}) %all-gather.8.cloned.1.call-update) | async-done | bytes 1572880 | tf_op jit(solution)/shard_map/all_gather | solution.py:115
  276.3 135.2 %all-gather.6.cloned.1.call-done = bf16[1024,2304]{1,0:T(8,128)(2,1)} async-done(((bf16[8,2304]{1,0:T(8,128)(2,1)}), bf16[1024,2304]{1,0:T(8,128)(2,1)}) %all-gather.6.cloned.1.call-update) | async-done | bytes 4718608 | tf_op jit(solution)/shard_map/all_gather | solution.py:116
  415.5 4.5 all-to-all-start.4
  420.0 6.8 %all-to-all-done.4 = bf16[1,8,16,768]{3,2,0,1:T(8,128)(2,1)S(1)} async-done(((bf16[1,8,16,768]{3,2,0,1:T(8,128)(2,1)}), bf16[1,8,16,768]{3,2,0,1:T(8,128)(2,1)S(1)}, u32[]{:S(2)}, u32[]{:S(2)}) %all-to-all-start.4) | async-done | bytes 196640 | tf_op jit(solution)/shard_map/all_to_all | solution.py:147
  426.8 4.0 all-to-all-start.5
  437.6 4.2 all-to-all-start.7
  459.9 4.0 all-to-all-start.10
  471.3 4.7 all-to-all-start.9
  489.4 3.6 all-to-all-done.8
  493.2 4.2 fusion.57
  498.4 19.0 %all_to_all.192 = bf16[1,8,16,768]{3,1,0,2:T(8,128)(2,1)S(1)} all-to-all(bf16[1,8,16,768]{3,1,0,2:T(8,128)(2,1)S(1)} %copy.131), channel_id=1, replica_groups=mesh['tm'=16,'space'=8,'dp'=4] {'tm'}, dimensions={2} | all-to-all | bytes 393216 | tf_op jit(solution)/shard_map/all_to_all | solution.py:176
  521.5 3.8 all-to-all-start.14
  529.1 9.5 %all-to-all-done.14 = bf16[16,2,3072]{2,1,0:T(2,128)(2,1)S(1)} async-done(((bf16[16,2,3072]{2,1,0:T(2,128)(2,1)}), bf16[16,2,3072]{2,1,0:T(2,128)(2,1)S(1)}, u32[]{:S(2)}, u32[]{:S(2)}) %all-to-all-start.14) | async-done | bytes 196640 | tf_op jit(solution)/shard_map/all_to_all | solution.py:185
  538.5 4.3 all-to-all-start.13
  546.0 9.9 %all-to-all-done.13 = bf16[16,2,3072]{2,1,0:T(2,128)(2,1)S(1)} async-done(((bf16[16,2,3072]{2,1,0:T(2,128)(2,1)}), bf16[16,2,3072]{2,1,0:T(2,128)(2,1)S(1)}, u32[]{:S(2)}, u32[]{:S(2)}) %all-to-all-start.13) | async-done | bytes 196640 | tf_op jit(solution)/shard_map/all_to_all | solution.py:184
  555.8 4.5 all-to-all-start.12
  562.1 11.4 %all-to-all-done.12 = bf16[16,2,3072]{2,1,0:T(2,128)(2,1)S(1)} async-done(((bf16[16,2,3072]{2,1,0:T(2,128)(2,1)}), bf16[16,2,3072]{2,1,0:T(2,128)(2,1)S(1)}, u32[]{:S(2)}, u32[]{:S(2)}) %all-to-all-start.12) | async-done | bytes 196640 | tf_op jit(solution)/shard_map/all_to_all | solution.py:183
  (142 shorter events, 94.9 us)
Async XLA Ops:
  7.2 35.7 %copy-start.14 = (bf16[1,8,16,768]{3,2,1,0:T(8,128)(2,1)S(1)}, bf16[1,8,16,768]{3,2,1,0:T(8,128)(2,1)}, u32[]{:S(2)}) copy-start(bf16[1,8,16,768]{3,2,1,0:T(8,128)(2,1)} %param.11) | copy-start | bytes 589828
  7.2 139.0 %all-gather.10.cloned.1.call-start = ((), (), s32[]{:S(2)}) async-start(), calls=%async_computation.17 | async-start | bytes 2113536 | tf_op jit(solution)/shard_map/all_gather | solution.py:117
  7.9 265.1 %all-gather.8.cloned.1.call-start = ((), (), s32[]{:S(2)}) async-start(), calls=%async_computation.16 | async-start | bytes 2113536 | tf_op jit(solution)/shard_map/all_gather | solution.py:115
  8.7 402.8 %all-gather.6.cloned.1.call-start = ((), (), s32[]{:S(2)}) async-start(), calls=%async_computation.15 | async-start | bytes 4755456 | tf_op jit(solution)/shard_map/all_gather | solution.py:116
  11.1 28.3 %all-to-all-start.1 = ((bf16[1,8,16,768]{3,1,0,2:T(8,128)(2,1)}), bf16[1,8,16,768]{3,1,0,2:T(8,128)(2,1)S(1)}, u32[]{:S(2)}, u32[]{:S(2)}) async-start(bf16[1,8,16,768]{3,1,0,2:T(8,128)(2,1)} %copy.106), calls=%async_computation.1 | async-start | bytes 393216 | tf_op jit(solution)/shard_map/all_to_all | solution.py:124
  39.3 17.4 %all-to-all-start.2 = ((bf16[1,8,16,768]{3,1,0,2:T(8,128)(2,1)}), bf16[1,8,16,768]{3,1,0,2:T(8,128)(2,1)S(1)}, u32[]{:S(2)}, u32[]{:S(2)}) async-start(bf16[1,8,16,768]{3,1,0,2:T(8,128)(2,1)} %copy.109), calls=%async_computation.2 | async-start | bytes 393216 | tf_op jit(solution)/shard_map/all_to_all | solution.py:125
  56.7 16.7 %all-to-all-start = ((bf16[1,8,16,768]{3,1,0,2:T(8,128)(2,1)}), bf16[1,8,16,768]{3,1,0,2:T(8,128)(2,1)S(1)}, u32[]{:S(2)}, u32[]{:S(2)}) async-start(bf16[1,8,16,768]{3,1,0,2:T(8,128)(2,1)} %copy.105), calls=%async_computation | async-start | bytes 393216 | tf_op jit(solution)/shard_map/all_to_all | solution.py:123
  61.7 12.9 %copy-start.9 = (bf16[128,12,64]{0,2,1:T(8,128)(2,1)}, bf16[128,12,64]{0,2,1:T(8,128)(2,1)S(1)}, u32[]{:S(2)}) copy-start(bf16[128,12,64]{0,2,1:T(8,128)(2,1)S(1)} %copy.108) | copy-start | bytes 589828
  78.5 17.7 %all-to-all-start.3 = ((bf16[16,2,3072]{2,1,0:T(2,128)(2,1)}), bf16[16,2,3072]{2,1,0:T(2,128)(2,1)S(1)}, u32[]{:S(2)}, u32[]{:S(2)}) async-start(bf16[16,2,3072]{2,1,0:T(2,128)(2,1)} %reshape.480), calls=%async_computation.3 | async-start | bytes 393216 | tf_op jit(solution)/shard_map/all_to_all | solution.py:128
  96.5 52.4 %copy-start.5 = (bf16[1,8,16,1024]{3,2,1,0:T(8,128)(2,1)S(1)}, bf16[1,8,16,1024]{3,2,1,0:T(8,128)(2,1)}, u32[]{:S(2)}) copy-start(bf16[1,8,16,1024]{3,2,1,0:T(8,128)(2,1)} %param.21) | copy-start | bytes 786436
  150.2 265.3 %all-to-all-start.6 = ((bf16[1,8,16,768]{3,2,0,1:T(8,128)(2,1)}), bf16[1,8,16,768]{3,2,0,1:T(8,128)(2,1)S(1)}, u32[]{:S(2)}, u32[]{:S(2)}) async-start(bf16[1,8,16,768]{3,2,0,1:T(8,128)(2,1)} %bitcast.26), calls=%async_computation.6 | async-start | bytes 393216 | tf_op jit(solution)/shard_map/all_to_all | solution.py:149
  154.4 121.2 %copy-start.13 = (bf16[1,8,16,1024]{3,2,1,0:T(8,128)(2,1)S(1)}, bf16[1,8,16,1024]{3,2,1,0:T(8,128)(2,1)}, u32[]{:S(2)}) copy-start(bf16[1,8,16,1024]{3,2,1,0:T(8,128)(2,1)} %param.14) | copy-start | bytes 786436
  275.6 135.9 %copy-start.16 = (f32[1024]{0:T(1024)S(1)}, f32[1024]{0:T(1024)}, u32[]{:S(2)}) copy-start(f32[1024]{0:T(1024)} %param.16) | copy-start | bytes 12292
  415.5 11.3 %all-to-all-start.4 = ((bf16[1,8,16,768]{3,2,0,1:T(8,128)(2,1)}), bf16[1,8,16,768]{3,2,0,1:T(8,128)(2,1)S(1)}, u32[]{:S(2)}, u32[]{:S(2)}) async-start(bf16[1,8,16,768]{3,2,0,1:T(8,128)(2,1)} %bitcast.18), calls=%async_computation.4 | async-start | bytes 393216 | tf_op jit(solution)/shard_map/all_to_all | solution.py:147
  426.8 10.9 %all-to-all-start.5 = ((bf16[1,8,16,768]{3,2,0,1:T(8,128)(2,1)}), bf16[1,8,16,768]{3,2,0,1:T(8,128)(2,1)}, u32[]{:S(2)}, u32[]{:S(2)}) async-start(bf16[1,8,16,768]{3,2,0,1:T(8,128)(2,1)} %bitcast.20), calls=%async_computation.5 | async-start | bytes 393216 | tf_op jit(solution)/shard_map/all_to_all | solution.py:146
  437.6 10.9 %all-to-all-start.7 = ((bf16[1,8,16,768]{3,2,0,1:T(8,128)(2,1)}), bf16[1,8,16,768]{3,2,0,1:T(8,128)(2,1)}, u32[]{:S(2)}, u32[]{:S(2)}) async-start(bf16[1,8,16,768]{3,2,0,1:T(8,128)(2,1)} %bitcast.28), calls=%async_computation.7 | async-start | bytes 393216 | tf_op jit(solution)/shard_map/all_to_all | solution.py:148
  459.9 11.3 %all-to-all-start.10 = ((bf16[8,2,6144]{2,1,0:T(2,128)(2,1)}), bf16[8,2,6144]{2,1,0:T(2,128)(2,1)}, u32[]{:S(2)}, u32[]{:S(2)}) async-start(bf16[8,2,6144]{2,1,0:T(2,128)(2,1)} %reshape.482), calls=%async_computation.10 | async-start | bytes 393216 | tf_op jit(solution)/shard_map/all_to_all | solution.py:159
  471.3 11.5 %all-to-all-start.9 = ((bf16[8,2,6144]{2,1,0:T(2,128)(2,1)}), bf16[8,2,6144]{2,1,0:T(2,128)(2,1)S(1)}, u32[]{:S(2)}, u32[]{:S(2)}) async-start(bf16[8,2,6144]{2,1,0:T(2,128)(2,1)} %reshape.484), calls=%async_computation.9 | async-start | bytes 393216 | tf_op jit(solution)/shard_map/all_to_all | solution.py:158
  482.8 10.2 %all-to-all-start.8 = ((bf16[8,2,6144]{2,1,0:T(2,128)(2,1)}), bf16[8,2,6144]{2,1,0:T(2,128)(2,1)S(1)}, u32[]{:S(2)}, u32[]{:S(2)}) async-start(bf16[8,2,6144]{2,1,0:T(2,128)(2,1)} %reshape.486), calls=%async_computation.8 | async-start | bytes 393216 | tf_op jit(solution)/shard_map/all_to_all | solution.py:157
  497.7 20.1 %copy-start.7 = (bf16[128,1024]{1,0:T(8,128)(2,1)}, bf16[128,1024]{1,0:T(8,128)(2,1)S(1)}, u32[]{:S(2)}) copy-start(bf16[128,1024]{1,0:T(8,128)(2,1)S(1)} %add_convert_fusion) | copy-start | bytes 786436
  521.5 17.0 %all-to-all-start.14 = ((bf16[16,2,3072]{2,1,0:T(2,128)(2,1)}), bf16[16,2,3072]{2,1,0:T(2,128)(2,1)S(1)}, u32[]{:S(2)}, u32[]{:S(2)}) async-start(bf16[16,2,3072]{2,1,0:T(2,128)(2,1)} %reshape.492), calls=%async_computation.14 | async-start | bytes 393216 | tf_op jit(solution)/shard_map/all_to_all | solution.py:185
  525.8 17.0 %copy-start.10 = (bf16[128,12,64]{0,2,1:T(8,128)(2,1)S(1)}, bf16[128,12,64]{0,2,1:T(8,128)(2,1)}, u32[]{:S(2)}) copy-start(bf16[128,12,64]{0,2,1:T(8,128)(2,1)} %copy-done.9) | copy-start | bytes 589828
  538.5 17.3 %all-to-all-start.13 = ((bf16[16,2,3072]{2,1,0:T(2,128)(2,1)}), bf16[16,2,3072]{2,1,0:T(2,128)(2,1)S(1)}, u32[]{:S(2)}, u32[]{:S(2)}) async-start(bf16[16,2,3072]{2,1,0:T(2,128)(2,1)} %reshape.490), calls=%async_computation.13 | async-start | bytes 393216 | tf_op jit(solution)/shard_map/all_to_all | solution.py:184
  555.8 17.6 %all-to-all-start.12 = ((bf16[16,2,3072]{2,1,0:T(2,128)(2,1)}), bf16[16,2,3072]{2,1,0:T(2,128)(2,1)S(1)}, u32[]{:S(2)}, u32[]{:S(2)}) async-start(bf16[16,2,3072]{2,1,0:T(2,128)(2,1)} %reshape.488), calls=%async_computation.12 | async-start | bytes 393216 | tf_op jit(solution)/shard_map/all_to_all | solution.py:183
  (12 other events, 56.0 us)
Sparse Core Ops, SparseCore 0:
  12.6 133.5 all-gather.9
  150.8 122.1 all-gather.7
  277.7 133.7 all-gather.5
where the time goes:
time: 583 us; the launch traced here: 581 us
  waiting for transfers between devices  406 us (70%)
  starting transfers between devices  66.1 us (11%)
  local copies, waits for them, and re-layouts  39.8 us (7%)
  matrix products  19 us (3%)
  blocking collectives  19 us (3%)
  other arithmetic  16.5 us (3%)
  between operations  14.5 us (2%)
    all_gather x1, waiting for transfers between devices, body(): lax.all_gather(qkv_weight, ('tm', 'space'), axis=0, tiled=True)  135 us
    all_gather x1, waiting for transfers between devices, body(): lax.all_gather(fc_weight, ('tm', 'space'), axis=0, tiled=True)  119 us
    all_gather x1, waiting for transfers between devices, body(): lax.all_gather(out_weight, ('tm', 'space'), axis=0, tiled=True)  49.7 us
    unnamed x68, local copies, waits for them, and re-layouts  23.3 us
    all_to_all x1, blocking collectives, body(): lax.all_to_all(grad_time.reshape(local_shape), 'tm', split_axis=2, concat...  19 us
    all_to_all x1, waiting for transfers between devices, body(): lax.all_to_all(mixed_tube[None], 'tm', split_axis=1, concat_axis=2, tiled...  14.2 us
    all_to_all x1, starting transfers between devices, body(): lax.all_to_all(time_key, 'tm', split_axis=2, concat_axis=1, tiled=True)  13.9 us
    unnamed x7, other arithmetic  13.4 us
  transfers between devices with their start and end apart: 17, of which 15 were waited for; matrix products, arithmetic and copies ran while one was open for 9% of the time, Pallas kernels for 0%

commit v1 on v0

v1 whole, which is shorter than its diff:
```python
import jax
import jax.numpy as jnp
from jax import lax
from jax.sharding import PartitionSpec as P

HEADS = 12
HD = 64
GRID = 32


epsilon = 1e-05


def rounded(values):
    return lax.optimization_barrier(values.astype(jnp.bfloat16)).astype(jnp.float32)


def split_heads(block):
    return block.reshape(block.shape[:-1] + (HEADS, HD)).astype(jnp.float32)


def softmax_rows(scores):
    row_top = jnp.max(scores, axis=-1, keepdims=True)
    exponent = jnp.exp(scores - row_top)
    return exponent / jnp.sum(exponent, axis=-1, keepdims=True)


def probs_of(queries, key_rows, pair_bias=None):
    scores = jnp.einsum("thd,uhd->htu", split_heads(queries), split_heads(key_rows)) * HD ** (-0.5)
    if pair_bias is not None:
        scores = scores + pair_bias
    return softmax_rows(scores)


def attention_forward(queries, key_rows, value_rows):
    attend = probs_of(queries, key_rows)
    mixed_out = jnp.einsum("htu,uhd->thd", rounded(attend), split_heads(value_rows))
    return mixed_out.reshape(queries.shape).astype(jnp.bfloat16)


def attention_backward(queries, key_rows, value_rows, grad_out, pair_bias=None):
    attend = probs_of(queries, key_rows, pair_bias)
    grad_attend = jnp.einsum("thd,uhd->htu", split_heads(grad_out), split_heads(value_rows))
    inner_sum = jnp.sum(attend * grad_attend, axis=-1, keepdims=True)
    grad_scores = rounded(attend * (grad_attend - inner_sum))
    score_scale = HD ** (-0.5)
    grad_q = jnp.einsum("htu,uhd->thd", grad_scores, split_heads(key_rows)) * score_scale
    grad_k = jnp.einsum("htu,thd->uhd", grad_scores, split_heads(queries)) * score_scale
    grad_v = jnp.einsum("htu,thd->uhd", rounded(attend), split_heads(grad_out))
    return tuple(g.reshape(queries.shape).astype(jnp.bfloat16) for g in (grad_q, grad_k, grad_v))


def distance_bias(tube_ids, bias_slope):
    tube_rows = tube_ids // GRID
    tube_cols = tube_ids % GRID
    distance = jnp.abs(tube_rows[:, None] - tube_rows[None, :]) + jnp.abs(
        tube_cols[:, None] - tube_cols[None, :]
    )
    return -bias_slope[:, None, None] * distance.astype(jnp.float32)[None]


def normalize(hidden):
    row_mean = jnp.mean(hidden, axis=-1, keepdims=True)
    centred = hidden - row_mean
    row_var = jnp.mean(centred * centred, axis=-1, keepdims=True)
    inv_std = lax.rsqrt(row_var + epsilon)
    return (centred * inv_std, inv_std)


def norm_backward(grad_normed, normed, inv_std, norm_gain, cot_rows):
    scaled_grad = grad_normed.astype(jnp.float32) * norm_gain
    first_mean = jnp.mean(scaled_grad, axis=-1, keepdims=True)
    second_mean = jnp.mean(scaled_grad * normed, axis=-1, keepdims=True)
    term = inv_std * (scaled_grad - first_mean - normed * second_mean)
    return (cot_rows.astype(jnp.float32) + term).astype(jnp.bfloat16)


def middle(mixed, resid, cot, fc_full, qkv_full, out_full, norm_gain, pair_bias):
    inner = mixed.shape[-1]
    f32 = jnp.float32
    hidden = resid.astype(f32) + jnp.dot(mixed, fc_full, preferred_element_type=f32)
    normed, inv_std = normalize(hidden)
    normed_in = (normed * norm_gain).astype(jnp.bfloat16)
    grad_mixed = jnp.dot(cot, out_full.T, preferred_element_type=f32).astype(jnp.bfloat16)
    projected = jnp.dot(normed_in, qkv_full, preferred_element_type=f32).astype(jnp.bfloat16)
    grads = attention_backward(
        projected[:, :inner],
        projected[:, inner : 2 * inner],
        projected[:, 2 * inner :],
        grad_mixed,
        pair_bias,
    )
    joined = jnp.concatenate(grads, axis=-1)
    grad_normed = jnp.dot(joined, qkv_full.T, preferred_element_type=f32).astype(jnp.bfloat16)
    grad_resid = norm_backward(grad_normed, normed, inv_std, norm_gain, cot)
    grad_time = jnp.dot(grad_resid, fc_full.T, preferred_element_type=f32).astype(jnp.bfloat16)
    return grad_resid, grad_time


def body(
    time_query,
    time_key,
    time_value,
    residual_in,
    fc_weight,
    norm_gain,
    qkv_weight,
    out_weight,
    bias_slope,
    visible,
    cotangent,
):
    tm, sp = lax.axis_size("tm"), lax.axis_size("space")
    steps, tubes, inner = time_query.shape[1:]
    width = residual_in.shape[-1]
    fc_rows, qkv_rows = fc_weight.shape[0], qkv_weight.shape[0]
    total = tm * steps
    both = ("tm", "space")

    pieces = [x[0].transpose(1, 0, 2) for x in (time_query, time_key, time_value)]
    shard = jnp.concatenate(
        [qkv_weight.reshape(-1, inner), fc_weight.reshape(-1, inner), out_weight.reshape(-1, inner)]
    )
    send = jnp.concatenate(
        pieces + [jnp.broadcast_to(shard[None], (tm,) + shard.shape)], axis=1
    )
    got = lax.all_to_all(send, "tm", split_axis=0, concat_axis=0, tiled=True)
    queries, keys, values = (
        got[:, i * steps : (i + 1) * steps].reshape(total, inner) for i in range(3)
    )
    at = 3 * steps
    cut = at + qkv_weight.size // inner
    mid = cut + fc_weight.size // inner
    qkv_part = got[:, at:cut].reshape(tm * qkv_rows, 3 * inner)
    fc_part = got[:, cut:mid].reshape(tm * fc_rows, width)
    out_part = got[:, mid:].reshape(tm * fc_rows, width)
    qkv_all = lax.all_gather(qkv_part, "space", axis=0)
    fo_all = lax.all_gather(jnp.concatenate([fc_part, out_part]), "space", axis=0)

    def natural(block, rows):
        block = block.reshape((sp, tm, rows) + block.shape[-1:])
        return block.transpose(1, 0, 2, 3).reshape(sp * tm * rows, -1)

    mixed = attention_forward(queries, keys, values)
    mixed = lax.all_to_all(mixed, both, split_axis=0, concat_axis=0, tiled=True)

    rest = jnp.concatenate([residual_in[0], cotangent[0]], axis=-1)
    rest, mixed = lax.optimization_barrier((rest, mixed))
    rest = lax.all_to_all(rest, "space", split_axis=0, concat_axis=0, tiled=True)
    rest = rest.reshape(sp, tm, 2 * width).transpose(1, 0, 2).reshape(sp * tm, 2 * width)
    tube_ids = visible[0].reshape(sp, tm).T.reshape(-1)
    pair_bias = distance_bias(tube_ids, bias_slope)

    qkv_full = natural(qkv_all, qkv_rows)
    fc_full = natural(fo_all[:, : tm * fc_rows], fc_rows)
    out_full = natural(fo_all[:, tm * fc_rows :], fc_rows)
    grad_resid, grad_time = middle(
        mixed, rest[:, :width], rest[:, width:], fc_full, qkv_full, out_full, norm_gain, pair_bias
    )
    grad_time = lax.all_to_all(grad_time, both, split_axis=0, concat_axis=0, tiled=True)
    grad_resid, grad_time = lax.optimization_barrier((grad_resid, grad_time))
    grad_resid = grad_resid.reshape(tm, sp, width).transpose(1, 0, 2)
    grad_resid = lax.all_to_all(grad_resid, "space", split_axis=0, concat_axis=0, tiled=True)

    grads = attention_backward(queries, keys, values, grad_time)
    back = jnp.concatenate([g.reshape(tm, steps, inner) for g in grads], axis=1)
    back = lax.all_to_all(back, "tm", split_axis=0, concat_axis=0, tiled=True)
    outs = [
        back[:, i * steps : (i + 1) * steps].transpose(1, 0, 2)[None] for i in range(3)
    ]
    return (grad_resid.reshape(residual_in.shape), *outs)


def solution(mesh):
    token = P("dp", "tm", "space", None)
    row = P(("tm", "space"), None)
    in_specs = (token, token, token, token, row, P(), row, row, P(), P("dp", None), token)
    return jax.shard_map(
        body, mesh=mesh, in_specs=in_specs, out_specs=(token,) * 4, check_vma=False
    )
```

time: 583 us -> 245 us (0.42)
  the two profiles are of different devices: /device:TPU:16 before, /device:TPU:8 now
where the time goes in v1:
time: 245 us; the launch traced here: 244 us
  blocking collectives  90.5 us (37%)
  waiting for transfers between devices  53.4 us (22%)
  local copies, waits for them, and re-layouts  40.7 us (17%)
  starting transfers between devices  20 us (8%)
  matrix products  17.7 us (7%)
  between operations  14.7 us (6%)
  other arithmetic  7.17 us (3%)
    all_to_all x1, blocking collectives, body(): got = lax.all_to_all(send, 'tm', split_axis=0, concat_axis=0, tiled=True)  58.9 us
    all_to_all x1, blocking collectives, body(): lax.all_to_all(grad_time, both, split_axis=0, concat_axis=0, tiled=True)  31.6 us
    all_to_all x1, waiting for transfers between devices, body(): back = lax.all_to_all(back, 'tm', split_axis=0, concat_axis=0, tiled=True)  22 us
    all_to_all x1, waiting for transfers between devices, body(): mixed = lax.all_to_all(mixed, both, split_axis=0, concat_axis=0, tiled=True)  14.7 us
    all_to_all x1, starting transfers between devices, body(): mixed = lax.all_to_all(mixed, both, split_axis=0, concat_axis=0, tiled=True)  9.27 us
    unnamed x49, local copies, waits for them, and re-layouts  8.45 us
    all_to_all x1, waiting for transfers between devices, body(): lax.all_to_all(rest, 'space', split_axis=0, concat_axis=0, tiled=True)  7.89 us
    transpose x3, local copies, waits for them, and re-layouts, natural(): return block.transpose(1, 0, 2, 3).reshape(sp * tm * rows, -1)  7.73 us
  transfers between devices with their start and end apart: 6, of which 5 were waited for; matrix products, arithmetic and copies ran while one was open for 14% of the time, Pallas kernels for 0%

profile of v1, /device:TPU:8, one launch (start us, length us, event | category | flops | bytes accessed | tf_op | source)
XLA Modules:
  0.0 244.2 jit_solution(13888973346628949000)
XLA Ops:
  12.7 58.9 %all_to_all.41 = bf16[16,64,768]{2,1,0:T(8,128)(2,1)S(1)} all-to-all(bf16[16,64,768]{2,1,0:T(8,128)(2,1)S(1)} %pad_maximum_fusion), channel_id=1, replica_groups=mesh['tm'=16,'space'=8,'dp'=4] {'tm'}, dimensions={0} | all-to-all | bytes 3145728 | tf_op jit(solution)/shard_map/all_to_all | solution.py:127
  79.2 9.3 %all-to-all-start.1 = ((bf16[128,2,384]{2,1,0:T(2,128)(2,1)}), bf16[128,2,384]{2,1,0:T(2,128)(2,1)S(1)}, u32[]{:S(2)}, u32[]{:S(2)}) async-start(bf16[128,2,384]{2,1,0:T(2,128)(2,1)} %reshape.322), calls=%async_computation.1 | async-start | bytes 393216 | tf_op jit(solution)/shard_map/all_to_all | solution.py:145
  89.3 14.7 %all-to-all-done.1 = bf16[128,2,384]{2,1,0:T(2,128)(2,1)S(1)} async-done(((bf16[128,2,384]{2,1,0:T(2,128)(2,1)}), bf16[128,2,384]{2,1,0:T(2,128)(2,1)S(1)}, u32[]{:S(2)}, u32[]{:S(2)}) %all-to-all-start.1) | async-done | bytes 196640 | tf_op jit(solution)/shard_map/all_to_all | solution.py:145
  104.9 3.7 %all-to-all-start.2 = ((bf16[8,16,2048]{2,1,0:T(8,128)(2,1)}), bf16[8,16,2048]{2,1,0:T(8,128)(2,1)S(1)}, u32[]{:S(2)}, u32[]{:S(2)}) async-start(bf16[8,16,2048]{2,1,0:T(8,128)(2,1)} %pad_maximum_fusion.2), calls=%async_computation.2 | async-start | bytes 1048576 | tf_op jit(solution)/shard_map/all_to_all | solution.py:149
  110.8 7.9 %all-to-all-done.2 = bf16[8,16,2048]{2,1,0:T(8,128)(2,1)S(1)} async-done(((bf16[8,16,2048]{2,1,0:T(8,128)(2,1)}), bf16[8,16,2048]{2,1,0:T(8,128)(2,1)S(1)}, u32[]{:S(2)}, u32[]{:S(2)}) %all-to-all-start.2) | async-done | bytes 524320 | tf_op jit(solution)/shard_map/all_to_all | solution.py:149
  119.7 2.7 %fusion.48 = (bf16[8,96,1024]{2,1,0:T(8,128)(2,1)S(1)}, bf16[8,96,1024]{2,1,0:T(8,128)(2,1)S(1)}) fusion(bf16[8,192,1024]{2,1,0:T(8,128)(2,1)} %bitcast.114), kind=kLoop, calls=%fused_computation.90 | loop fusion | bytes 6291456 | tf_op jit(solution)/shard_map/slice | solution.py:155
  123.3 2.5 %copy.122 = bf16[16,8,6,1024]{3,2,1,0:T(8,128)(2,1)} copy(bf16[16,8,6,1024]{3,1,2,0:T(8,128)(2,1)S(1)} %bitcast.108) | data formatting | bytes 3145728 | tf_op jit(solution)/shard_map/transpose | solution.py:142
  125.8 2.6 %reshape.299 = bf16[768,1024]{1,0:T(8,128)(2,1)S(1)} reshape(bf16[16,8,6,1024]{3,2,1,0:T(8,128)(2,1)} %copy.122) | data formatting | bytes 3145728 | tf_op jit(solution)/shard_map/reshape | solution.py:142
  129.3 2.5 %copy.128 = bf16[16,8,6,1024]{3,2,1,0:T(8,128)(2,1)} copy(bf16[16,8,6,1024]{3,1,2,0:T(8,128)(2,1)S(1)} %bitcast.109) | data formatting | bytes 3145728 | tf_op jit(solution)/shard_map/transpose | solution.py:142
  131.8 2.6 %reshape.306 = bf16[768,1024]{1,0:T(8,128)(2,1)S(1)} reshape(bf16[16,8,6,1024]{3,2,1,0:T(8,128)(2,1)} %copy.128) | data formatting | bytes 3145728 | tf_op jit(solution)/shard_map/reshape | solution.py:142
  134.4 2.3 convolution_convert_fusion.5
  137.8 1.5 fusion.52
  139.5 4.7 %all-gather.4.cloned.1.call-done = bf16[8,128,2304]{2,1,0:T(8,128)(2,1)} async-done(((bf16[1,128,2304]{2,1,0:T(8,128)(2,1)}), bf16[8,128,2304]{2,1,0:T(8,128)(2,1)}) %all-gather.4.cloned.1.call-update) | async-done | bytes 4718608 | tf_op jit(solution)/shard_map/all_gather | solution.py:137
  144.2 2.8 %copy.123 = bf16[16,8,8,2304]{3,2,1,0:T(8,128)(2,1)S(1)} copy(bf16[16,8,8,2304]{3,2,0,1:T(8,128)(2,1)} %bitcast.110) | data formatting | bytes 9437184 | tf_op jit(solution)/shard_map/transpose | solution.py:142
  147.9 1.2 copy-done
  150.3 1.3 fusion.53
  152.9 2.0 fusion.13
  154.9 1.3 fusion.18
  157.8 4.2 %fusion.47 = (f32[128]{0:T(128)S(1)}, f32[128]{0:T(128)S(1)}, f32[128,1024]{1,0:T(8,128)S(1)}) fusion(f32[128]{0:T(128)S(1)} %add_rsqrt_fusion, f32[128,1024]{1,0:T(8,128)S(1)} %get-tuple-element.44, f32[128]{0:T(128)S(1)} %broadcast_multiply_fusion.2, f32[1024]{0:T(1024)S(1)} %copy-done.15, bf16[1024,2304]{1,0:T(8,128)(2,1)} %bitcast.107, ...), kind=kOutput, calls=%fused_computation.89 | convolution fusion | flops 606797568 | bytes 6363136 | tf_op jit(solution)/shard_map/dot_general | solution.py:94
  163.7 31.6 %all_to_all.42 = bf16[128,2,384]{2,1,0:T(2,128)(2,1)S(1)} all-to-all(bf16[128,2,384]{2,1,0:T(2,128)(2,1)S(1)} %reshape.324), channel_id=1, replica_groups=mesh['tm'=16,'space'=8,'dp'=4] {'tm','space'}, dimensions={0} | all-to-all | bytes 393216 | tf_op jit(solution)/shard_map/all_to_all | solution.py:160
  198.0 3.4 %all-to-all-start.4 = ((bf16[8,16,1024]{2,1,0:T(8,128)(2,1)}), bf16[8,16,1024]{2,1,0:T(8,128)(2,1)S(1)}, u32[]{:S(2)}, u32[]{:S(2)}) async-start(bf16[8,16,1024]{2,1,0:T(8,128)(2,1)} %bitcast.104), calls=%async_computation.4 | async-start | bytes 524288 | tf_op jit(solution)/shard_map/all_to_all | solution.py:163
  204.7 4.1 %all-to-all-done.4 = bf16[8,16,1024]{2,1,0:T(8,128)(2,1)S(1)} async-done(((bf16[8,16,1024]{2,1,0:T(8,128)(2,1)}), bf16[8,16,1024]{2,1,0:T(8,128)(2,1)S(1)}, u32[]{:S(2)}, u32[]{:S(2)}) %all-to-all-start.4) | async-done | bytes 262176 | tf_op jit(solution)/shard_map/all_to_all | solution.py:163
  208.9 3.6 %all-to-all-start.5 = ((bf16[16,24,768]{2,1,0:T(8,128)(2,1)}), bf16[16,24,768]{2,1,0:T(8,128)(2,1)S(1)}, u32[]{:S(2)}, u32[]{:S(2)}) async-start(bf16[16,24,768]{2,1,0:T(8,128)(2,1)} %pad_maximum_fusion.1), calls=%async_computation.5 | async-start | bytes 1179648 | tf_op jit(solution)/shard_map/all_to_all | solution.py:167
  212.5 22.0 %all-to-all-done.5 = bf16[16,24,768]{2,1,0:T(8,128)(2,1)S(1)} async-done(((bf16[16,24,768]{2,1,0:T(8,128)(2,1)}), bf16[16,24,768]{2,1,0:T(8,128)(2,1)S(1)}, u32[]{:S(2)}, u32[]{:S(2)}) %all-to-all-start.5) | async-done | bytes 589856 | tf_op jit(solution)/shard_map/all_to_all | solution.py:167
  (118 shorter events, 36.2 us)
Async XLA Ops:
  7.2 112.6 %all-gather.6.cloned.1.call-start = ((), (), s32[]{:S(2)}) async-start(), calls=%async_computation.7 | async-start | bytes 3538944 | tf_op jit(solution)/shard_map/all_gather | solution.py:138
  72.8 71.3 %all-gather.4.cloned.1.call-start = ((), (), s32[]{:S(2)}) async-start(), calls=%async_computation.6 | async-start | bytes 5308416 | tf_op jit(solution)/shard_map/all_gather | solution.py:137
  74.8 1.9 copy-start.6
  75.6 1.2 copy-start.8
  76.3 0.8 copy-start.10
  76.8 2.4 copy-start.2
  76.8 11.7 %copy-start.12 = (bf16[1,8,16,1024]{3,2,1,0:T(8,128)(2,1)S(1)}, bf16[1,8,16,1024]{3,2,1,0:T(8,128)(2,1)}, u32[]{:S(2)}) copy-start(bf16[1,8,16,1024]{3,2,1,0:T(8,128)(2,1)} %param.21) | copy-start | bytes 786436
  76.8 11.7 %copy-start.13 = (bf16[1,8,16,1024]{3,2,1,0:T(8,128)(2,1)S(1)}, bf16[1,8,16,1024]{3,2,1,0:T(8,128)(2,1)}, u32[]{:S(2)}) copy-start(bf16[1,8,16,1024]{3,2,1,0:T(8,128)(2,1)} %param.14) | copy-start | bytes 786436
  79.2 24.9 %all-to-all-start.1 = ((bf16[128,2,384]{2,1,0:T(2,128)(2,1)}), bf16[128,2,384]{2,1,0:T(2,128)(2,1)S(1)}, u32[]{:S(2)}, u32[]{:S(2)}) async-start(bf16[128,2,384]{2,1,0:T(2,128)(2,1)} %reshape.322), calls=%async_computation.1 | async-start | bytes 393216 | tf_op jit(solution)/shard_map/all_to_all | solution.py:145
  88.5 20.1 %copy-start.16 = (f32[12]{0:T(128)S(1)}, f32[12]{0:T(128)}, u32[]{:S(2)}) copy-start(f32[12]{0:T(128)} %param.19) | copy-start | bytes 148
  88.5 20.6 %copy-start.17 = (s32[1,128]{1,0:T(1,128)S(1)}, s32[1,128]{1,0:T(1,128)}, u32[]{:S(2)}) copy-start(s32[1,128]{1,0:T(1,128)} %param.20) | copy-start | bytes 1540
  104.9 13.8 %all-to-all-start.2 = ((bf16[8,16,2048]{2,1,0:T(8,128)(2,1)}), bf16[8,16,2048]{2,1,0:T(8,128)(2,1)S(1)}, u32[]{:S(2)}, u32[]{:S(2)}) async-start(bf16[8,16,2048]{2,1,0:T(8,128)(2,1)} %pad_maximum_fusion.2), calls=%async_computation.2 | async-start | bytes 1048576 | tf_op jit(solution)/shard_map/all_to_all | solution.py:149
  144.2 2.8 %copy-start.15 = (f32[1024]{0:T(1024)S(1)}, f32[1024]{0:T(1024)}, u32[]{:S(2)}) copy-start(f32[1024]{0:T(1024)} %param.16) | copy-start | bytes 12292
  147.0 2.1 copy-start
  149.1 1.2 copy-start.14
  150.1 1.5 copy-start.4
  150.3 2.6 %copy-start.5 = (bf16[128,768]{0,1:T(8,128)(2,1)}, bf16[128,768]{0,1:T(8,128)(2,1)S(1)}, u32[]{:S(2)}) copy-start(bf16[128,768]{0,1:T(8,128)(2,1)S(1)} %copy.124) | copy-start | bytes 589828
  157.8 4.2 %copy-start.1 = (bf16[16,8,2048]{2,1,0:T(8,128)(2,1)S(1)}, bf16[16,8,2048]{2,1,0:T(8,128)(2,1)}, u32[]{:S(2)}) copy-start(bf16[16,8,2048]{2,1,0:T(8,128)(2,1)} %copy.162) | copy-start | bytes 1572868
  162.9 33.0 %copy-start.3 = (f32[12,128,128]{1,2,0:T(8,128)S(1)}, f32[12,128,128]{1,2,0:T(8,128)}, u32[]{:S(2)}) copy-start(f32[12,128,128]{1,2,0:T(8,128)} %copy-done.2) | copy-start | bytes 2359300
  162.9 33.0 %copy-start.11 = (bf16[128,12,64]{0,2,1:T(8,128)(2,1)S(1)}, bf16[128,12,64]{0,2,1:T(8,128)(2,1)}, u32[]{:S(2)}) copy-start(bf16[128,12,64]{0,2,1:T(8,128)(2,1)} %copy-done.10) | copy-start | bytes 589828
  195.8 0.9 copy-start.9
  196.3 5.1 %copy-start.7 = (bf16[128,12,64]{0,2,1:T(8,128)(2,1)S(1)}, bf16[128,12,64]{0,2,1:T(8,128)(2,1)}, u32[]{:S(2)}) copy-start(bf16[128,12,64]{0,2,1:T(8,128)(2,1)} %copy-done.6) | copy-start | bytes 589828
  198.0 10.9 %all-to-all-start.4 = ((bf16[8,16,1024]{2,1,0:T(8,128)(2,1)}), bf16[8,16,1024]{2,1,0:T(8,128)(2,1)S(1)}, u32[]{:S(2)}, u32[]{:S(2)}) async-start(bf16[8,16,1024]{2,1,0:T(8,128)(2,1)} %bitcast.104), calls=%async_computation.4 | async-start | bytes 524288 | tf_op jit(solution)/shard_map/all_to_all | solution.py:163
  208.9 25.6 %all-to-all-start.5 = ((bf16[16,24,768]{2,1,0:T(8,128)(2,1)}), bf16[16,24,768]{2,1,0:T(8,128)(2,1)S(1)}, u32[]{:S(2)}, u32[]{:S(2)}) async-start(bf16[16,24,768]{2,1,0:T(8,128)(2,1)} %pad_maximum_fusion.1), calls=%async_computation.5 | async-start | bytes 1179648 | tf_op jit(solution)/shard_map/all_to_all | solution.py:167
Sparse Core Ops, SparseCore 0:
  73.0 28.7 all-gather.5
  103.9 40.2 all-gather.3

commit v2 on v1

v2 whole, which is shorter than its diff:
```python
import numpy as np
import jax
import jax.numpy as jnp
from jax import lax
from jax.experimental import pallas as pl
from jax.experimental.pallas import tpu as pltpu
from jax.sharding import PartitionSpec as P

HEADS = 12
HD = 64
GRID = 32
SCALE = HD ** (-0.5)
EPSILON = 1e-05
F32 = jnp.float32
BF16 = jnp.bfloat16
VMEM = pl.BlockSpec(memory_space=pltpu.VMEM)
SMEM = pl.BlockSpec(memory_space=pltpu.SMEM)
ANY = pl.BlockSpec(memory_space=pl.ANY)


def params(mib):
    return pltpu.CompilerParams(vmem_limit_bytes=mib * 2**20)


def nn(a, b):
    return jnp.dot(a, b, preferred_element_type=F32)


def nt(a, b):
    return lax.dot_general(a, b, (((1,), (1,)), ((), ())), preferred_element_type=F32)


def tn(a, b):
    return lax.dot_general(a, b, (((0,), (0,)), ((), ())), preferred_element_type=F32)


def transposed_rows(outer, inner):
    m = np.zeros((outer * inner, outer * inner), np.float32)
    i, j = np.meshgrid(np.arange(outer), np.arange(inner), indexing="ij")
    m[(j * outer + i).ravel(), (i * inner + j).ravel()] = 1
    return m.astype(BF16)


def gathered_order(tm, sp, rows):
    size = tm * sp * rows
    m = np.zeros((size, size), np.float32)
    a, b, r = (v.ravel() for v in np.meshgrid(*map(np.arange, (tm, sp, rows)), indexing="ij"))
    m[(a * sp + b) * rows + r, (b * tm + a) * rows + r] = 1
    return m.astype(BF16)


def shard_order(tm):
    main = np.zeros((12 * tm, 16 * tm), np.float32)
    rest = np.zeros((3, 3, 4 * tm, 16 * tm), np.float32)
    third = 2 * tm
    for which in range(2):
        for n in range(6 * tm):
            a, r = divmod(n, 6)
            g = which * 6 + r
            main[which * 6 * tm + n, a * 16 + g] = 1
            rest[n // third, g // 4, which * third + n % third, a * 16 + 12 + g % 4] = 1
    return main.astype(BF16), rest.astype(BF16)


def weights_pack_kernel(fc_ref, out_ref, qkv_ref, o_ref):
    both = jnp.concatenate([fc_ref[...].astype(F32), out_ref[...].astype(F32)], axis=0)
    tail = both[:, 768:]
    tail = jnp.concatenate([tail[0:4], tail[4:8], tail[8:12]], axis=1)
    qkv = qkv_ref[...].astype(F32)
    block = jnp.concatenate(
        [both[:, :768], tail, qkv[:, :768], qkv[:, 768:1536], qkv[:, 1536:]], axis=0
    )
    o_ref[...] = jnp.broadcast_to(block[None], o_ref.shape).astype(BF16)


def weights_unpack_kernel(x_ref, main_ref, rest_ref, o_ref):
    tm = x_ref.shape[0]
    x = x_ref[...].astype(F32)
    fo = x[:, 0:16].reshape(16 * tm, 768).astype(BF16)
    n = 8 * tm
    for j in range(3):
        o_ref[pl.ds(j * n, n), :] = x[:, 16 + 8 * j : 24 + 8 * j].reshape(n, 768).astype(BF16)
    o_ref[pl.ds(3 * n, 12 * tm), :] = nn(main_ref[...], fo).astype(BF16)
    for j in range(3):
        part = nn(rest_ref[j, 0], fo[:, :256])
        part += nn(rest_ref[j, 1], fo[:, 256:512])
        part += nn(rest_ref[j, 2], fo[:, 512:])
        o_ref[pl.ds(3 * n + 12 * tm, 4 * tm), pl.ds(j * 256, 256)] = part.astype(BF16)


def pack_kernel(q_ref, k_ref, v_ref, res_ref, cot_ref, turn_ref, o_ref, rest_ref):
    steps, tubes, inner = q_ref.shape[1:]
    rows = steps * tubes
    parts = [
        nn(turn_ref[...], ref[0].reshape(rows, inner)).reshape(tubes, steps, inner)
        for ref in (q_ref, k_ref, v_ref)
    ]
    o_ref[...] = jnp.concatenate(parts, axis=1).astype(BF16)
    rest_ref[...] = jnp.concatenate([res_ref[0], cot_ref[0]], axis=-1)


def unpack_kernel(x_ref, turn_ref, *outs):
    x = x_ref[...].astype(F32)
    tubes, steps = x.shape[0], x.shape[1] // 3
    for j, o_ref in enumerate(outs):
        part = x[:, j * steps : (j + 1) * steps].reshape(tubes * steps, -1).astype(BF16)
        o_ref[0] = nn(turn_ref[...], part).astype(BF16).reshape(steps, tubes, -1)


def lane_masks(rows):
    lane = lax.broadcasted_iota(jnp.int32, (rows, 2 * HD), 1)
    return lane < HD


def stacked(block, first):
    zero = jnp.zeros_like(block)
    return jnp.concatenate([jnp.where(first, block, zero), jnp.where(first, zero, block)], axis=0)


def softmax(scores):
    exponent = jnp.exp(scores - jnp.max(scores, axis=-1, keepdims=True))
    return exponent / jnp.sum(exponent, axis=-1, keepdims=True)


def pair_probs(q, k2, bias0=None, bias1=None):
    n = q.shape[0]
    scores = nt(q, k2) * SCALE
    s0, s1 = scores[:, :n], scores[:, n:]
    if bias0 is not None:
        s0, s1 = s0 + bias0, s1 + bias1
    return softmax(s0), softmax(s1)


def pair_backward(p0, p1, q, k, v, g, first):
    n = q.shape[0]
    k2, v2, q2, g2 = (stacked(x, first) for x in (k, v, q, g))
    gp = nt(g, v2)
    g0, g1 = gp[:, :n], gp[:, n:]
    d0 = (p0 * (g0 - jnp.sum(p0 * g0, axis=-1, keepdims=True))).astype(BF16)
    d1 = (p1 * (g1 - jnp.sum(p1 * g1, axis=-1, keepdims=True))).astype(BF16)
    grad_q = nn(jnp.concatenate([d0, d1], axis=1), k2)
    grad_k = tn(jnp.concatenate([d0, d1], axis=0), q2)
    grad_v = tn(jnp.concatenate([p0.astype(BF16), p1.astype(BF16)], axis=0), g2)
    return grad_q * SCALE, grad_k * SCALE, grad_v


def qkv_of(x, steps):
    return [
        x[:, j * steps : (j + 1) * steps].reshape(x.shape[0] * steps, -1).astype(BF16)
        for j in range(3)
    ]


def forward_kernel(x_ref, o_ref, p_ref, turned):
    x = x_ref[...].astype(F32)
    q, k, v = qkv_of(x, x.shape[1] // 3)
    n = q.shape[0]
    first = lane_masks(n)
    for h in range(HEADS // 2):
        at = slice(h * 128, (h + 1) * 128)
        p0, p1 = pair_probs(q[:, at], stacked(k[:, at], first))
        p_ref[h, :, 0:n] = p0
        p_ref[h, :, n : 2 * n] = p1
        both = jnp.concatenate([p0.astype(BF16), p1.astype(BF16)], axis=1)
        turned[:, h, :] = nn(both, stacked(v[:, at], first))
    o_ref[...] = turned[...].astype(BF16)


def backward_kernel(x_ref, p_ref, g_ref, o_ref, turned):
    x = x_ref[...].astype(F32)
    steps = x.shape[1] // 3
    q, k, v = qkv_of(x, steps)
    n = q.shape[0]
    turned[...] = g_ref[...].astype(F32)
    first = lane_masks(n)
    for h in range(HEADS // 2):
        at = slice(h * 128, (h + 1) * 128)
        grads = pair_backward(
            p_ref[h, :, 0:n],
            p_ref[h, :, n : 2 * n],
            q[:, at],
            k[:, at],
            v[:, at],
            turned[:, h, :].astype(BF16),
            first,
        )
        joined = jnp.concatenate([d.reshape(n // steps, steps, 128) for d in grads], axis=1)
        o_ref[:, :, at] = joined.astype(BF16)


def middle_kernel(
    w_hbm, x_ref, rest_ref, gain_ref, slope_ref, row_ref, col_ref, turn_ref, inner_ref, width_ref,
    gr_ref, gt_ref, qkv_v, fc_v, out_v, turned, proj, joined, sem,
):
    sp = w_hbm.shape[0]
    tm = w_hbm.shape[1] // 40
    n, third = 8 * tm, 2 * tm
    copies = []

    def load(src, dst):
        copies.append(pltpu.make_async_copy(src, dst, sem.at[len(copies)]))
        copies[-1].start()

    at = 3 * n
    for dst, base, tail in (
        (fc_v, at, at + 12 * tm),
        (out_v, at + 6 * tm, at + 12 * tm + third),
    ):
        load(w_hbm.at[:, pl.ds(base, 6 * tm), :], dst.at[:, :, pl.ds(0, 768)])
        for j in range(3):
            load(
                w_hbm.at[:, pl.ds(tail, third), pl.ds(j * 256, 256)],
                dst.at[:, pl.ds(j * third, third), pl.ds(768, 256)],
            )
    for j in range(3):
        load(w_hbm.at[:, pl.ds(j * n, n), :], qkv_v.at[:, :, pl.ds(j * 768, 768)])

    tokens = x_ref.shape[0]
    width = gain_ref.shape[1]
    inner = 768
    rows, cols = row_ref[...], col_ref[...]
    distance = jnp.abs((rows >> 5) - (cols >> 5)) + jnp.abs((rows & 31) - (cols & 31))
    distance = distance.astype(F32)
    gain = gain_ref[...]
    turn = turn_ref[...]
    turned[...] = x_ref[...].astype(F32)
    mixed = jnp.concatenate([turned[:, h, :] for h in range(6)], axis=1).astype(BF16)
    mixed = nn(turn, mixed).astype(BF16)
    mixed = nn(mixed, inner_ref[...]).astype(BF16)
    cot = rest_ref[:, width:]

    for c in copies[:4]:
        c.wait()
    fc = fc_v[...].reshape(inner, width)
    hidden = rest_ref[:, :width].astype(F32) + nn(mixed, fc)
    centred = hidden - jnp.mean(hidden, axis=-1, keepdims=True)
    inv_std = lax.rsqrt(jnp.mean(centred * centred, axis=-1, keepdims=True) + EPSILON)
    normed = centred * inv_std
    normed_in = (normed * gain).astype(BF16)
    normed_in = nn(normed_in, width_ref[...]).astype(BF16)

    for c in copies[4:8]:
        c.wait()
    grad_mixed = nt(cot, out_v[...].reshape(inner, width)).astype(BF16)
    grad_mixed = nt(grad_mixed, inner_ref[...]).astype(BF16)

    for c in copies[8:]:
        c.wait()
    qkv = qkv_v[...].reshape(width, 3 * inner)
    proj[...] = nn(normed_in, qkv).astype(BF16)

    first = lane_masks(tokens)
    for h in range(HEADS // 2):
        q, k, v = (proj[:, j * inner + h * 128 : j * inner + (h + 1) * 128] for j in range(3))
        g = grad_mixed[:, h * 128 : (h + 1) * 128]
        p0, p1 = pair_probs(
            q, stacked(k, first), -slope_ref[2 * h] * distance, -slope_ref[2 * h + 1] * distance
        )
        for j, d in enumerate(pair_backward(p0, p1, q, k, v, g, first)):
            joined[:, j * inner + h * 128 : j * inner + (h + 1) * 128] = d.astype(BF16)

    grad_normed = nt(joined[...], qkv).astype(BF16)
    grad_normed = nt(grad_normed, width_ref[...])
    scaled = grad_normed * gain
    first_mean = jnp.mean(scaled, axis=-1, keepdims=True)
    second_mean = jnp.mean(scaled * normed, axis=-1, keepdims=True)
    term = inv_std * (scaled - first_mean - normed * second_mean)
    grad_resid = (cot.astype(F32) + term).astype(BF16)
    gr_ref[...] = grad_resid
    grad_time = nt(grad_resid, fc).astype(BF16)
    grad_time = nt(grad_time, inner_ref[...]).astype(BF16)
    grad_time = tn(turn, grad_time)
    for h in range(6):
        turned[:, h, :] = grad_time[:, h * 128 : (h + 1) * 128]
    gt_ref[...] = turned[...].astype(BF16)


def body(
    time_query,
    time_key,
    time_value,
    residual_in,
    fc_weight,
    norm_gain,
    qkv_weight,
    out_weight,
    bias_slope,
    visible,
    cotangent,
):
    tm, sp = lax.axis_size("tm"), lax.axis_size("space")
    steps, tubes, inner = time_query.shape[1:]
    width = residual_in.shape[-1]
    total = tm * steps
    both = ("tm", "space")
    shape = jax.ShapeDtypeStruct

    def exchange(x, axes):
        return lax.all_to_all(x, axes, split_axis=0, concat_axis=0, tiled=True)

    to_tubes = jnp.asarray(transposed_rows(steps, tubes))
    to_steps = jnp.asarray(transposed_rows(tubes, steps))
    to_order = jnp.asarray(transposed_rows(tm, sp))
    main_map, rest_map = map(jnp.asarray, shard_order(tm))
    inner_map = jnp.asarray(gathered_order(tm, sp, fc_weight.shape[0]))
    width_map = jnp.asarray(gathered_order(tm, sp, qkv_weight.shape[0]))

    shards = pl.pallas_call(
        weights_pack_kernel,
        out_shape=shape((tm, 40, inner), BF16),
        in_specs=[VMEM] * 3,
        out_specs=VMEM,
        compiler_params=params(16),
        name="weights_pack",
    )(fc_weight, out_weight, qkv_weight)
    shards = exchange(shards, "tm")

    send, rest = pl.pallas_call(
        pack_kernel,
        out_shape=(shape((tubes, 3 * steps, inner), BF16), shape((steps, tubes, 2 * width), BF16)),
        in_specs=[VMEM] * 6,
        out_specs=(VMEM, VMEM),
        compiler_params=params(16),
        name="pack",
    )(time_query, time_key, time_value, residual_in, cotangent, to_tubes)

    shards = pl.pallas_call(
        weights_unpack_kernel,
        out_shape=shape((40 * tm, inner), BF16),
        in_specs=[VMEM] * 3,
        out_specs=VMEM,
        compiler_params=params(24),
        name="weights_unpack",
    )(shards, main_map, rest_map)
    weights = lax.all_gather(shards, "space", axis=0)

    send, shards = lax.optimization_barrier((send, shards))
    got = exchange(send, "tm")
    rest, got = lax.optimization_barrier((rest, got))
    rest = exchange(rest, "space").reshape(total, 2 * width)

    mixed, probs = pl.pallas_call(
        forward_kernel,
        out_shape=(shape((total, 6, 128), BF16), shape((HEADS // 2, total, 2 * total), F32)),
        in_specs=[VMEM],
        out_specs=(VMEM, VMEM),
        scratch_shapes=[pltpu.VMEM((total, 6, 128), F32)],
        compiler_params=params(24),
        cost_estimate=pl.CostEstimate(flops=10**8, bytes_accessed=2 * 10**6, transcendentals=2 * 10**5),
        name="temporal_forward",
    )(got)
    mixed, rest = lax.optimization_barrier((mixed, rest))
    mixed = exchange(mixed, both)

    grad_resid, grad_time = pl.pallas_call(
        middle_kernel,
        out_shape=(shape((total, width), BF16), shape((total, 6, 128), BF16)),
        in_specs=[ANY, VMEM, VMEM, VMEM, SMEM, VMEM, VMEM, VMEM, VMEM, VMEM],
        out_specs=(VMEM, VMEM),
        scratch_shapes=[
            pltpu.VMEM((sp, 8 * tm, 3 * inner), BF16),
            pltpu.VMEM((sp, 6 * tm, width), BF16),
            pltpu.VMEM((sp, 6 * tm, width), BF16),
            pltpu.VMEM((total, 6, 128), F32),
            pltpu.VMEM((total, 3 * inner), BF16),
            pltpu.VMEM((total, 3 * inner), BF16),
            pltpu.SemaphoreType.DMA((11,)),
        ],
        compiler_params=params(48),
        cost_estimate=pl.CostEstimate(flops=4 * 10**9, bytes_accessed=10**7, transcendentals=2 * 10**5),
        name="middle",
    )(
        weights,
        mixed,
        rest,
        norm_gain.reshape(1, width),
        bias_slope,
        visible.reshape(total, 1),
        visible.reshape(1, total),
        to_order,
        inner_map,
        width_map,
    )
    grad_time = exchange(grad_time, both)
    grad_resid, grad_time = lax.optimization_barrier((grad_resid, grad_time))
    grad_resid = exchange(grad_resid.reshape(steps, tubes, width), "space")

    back = pl.pallas_call(
        backward_kernel,
        out_shape=shape((tm, 3 * steps, inner), BF16),
        in_specs=[VMEM] * 3,
        out_specs=VMEM,
        scratch_shapes=[pltpu.VMEM((total, 6, 128), F32)],
        compiler_params=params(24),
        cost_estimate=pl.CostEstimate(flops=3 * 10**8, bytes_accessed=2 * 10**6, transcendentals=0),
        name="temporal_backward",
    )(got, probs, grad_time)
    back, grad_resid = lax.optimization_barrier((back, grad_resid))
    back = exchange(back, "tm")
    outs = pl.pallas_call(
        unpack_kernel,
        out_shape=(shape(time_query.shape, BF16),) * 3,
        in_specs=[VMEM] * 2,
        out_specs=(VMEM,) * 3,
        compiler_params=params(16),
        name="unpack",
    )(back, to_steps)
    return (grad_resid.reshape(residual_in.shape), *outs)


def solution(mesh):
    token = P("dp", "tm", "space", None)
    row = P(("tm", "space"), None)
    in_specs = (token, token, token, token, row, P(), row, row, P(), P("dp", None), token)
    return jax.shard_map(
        body, mesh=mesh, in_specs=in_specs, out_specs=(token,) * 4, check_vma=False
    )
```

time: 245 us -> 211 us (0.86)
  local copies, waits for them, and re-layouts: 40.7 us -> 4.72 us
  Pallas kernels: 0 us -> 19.3 us
  matrix products: 17.7 us -> 0 us
  other arithmetic: 7.17 us -> 0 us
  blocking collectives: 90.5 us -> 97 us
  waiting for transfers between devices: 53.4 us -> 57.6 us
    pallas_call x0 -> x7, Pallas kernels: none -> 19.3 us  [the longest x1 11 us: body(): pl.pallas_call(middle_kernel, out_shape=(shape((total, width), BF16), sha...]
    dot_general x12 -> x0, matrix products: 13.5 us -> none  [the longest x1 4.15 us: middle(): jnp.dot(joined, qkv_full.T, preferred_element_type=f32).astype(jnp.bfloat16)]
    transpose x8 -> x0, local copies, waits for them, and re-layouts: 11.9 us -> none  [the longest x3 7.73 us: natural(): return block.transpose(1, 0, 2, 3).reshape(sp * tm * rows, -1)]
    all_to_all x4, waiting for transfers between devices: 48.8 us -> 57.6 us  [exchange(): return lax.all_to_all(x, axes, split_axis=0, concat_axis=0, tiled=True)]
    reshape x9 -> x1, local copies, waits for them, and re-layouts: 8.81 us -> 0.11 us  [body(): visible.reshape(total, 1)]
    all_to_all x2 -> x3, blocking collectives: 90.5 us -> 97 us  [exchange(): return lax.all_to_all(x, axes, split_axis=0, concat_axis=0, tiled=True)]
    all_gather x2 -> x1, waiting for transfers between devices: 4.66 us -> 0.01 us  [body(): weights = lax.all_gather(shards, 'space', axis=0)]
    sub x4 -> x0, matrix products: 4.24 us -> none  [the longest x2 2.46 us: attention_backward(): grad_scores = rounded(attend * (grad_attend - inner_sum))]
  transfers between devices with their start and end apart: 6 -> 5, of which waited for: 5 -> 4; matrix products, arithmetic and copies ran while one was open for 14% -> 0% of each run, Pallas kernels for 0% -> 3%
where the time goes in v2:
time: 211 us
  blocking collectives  97 us (46%)
  waiting for transfers between devices  57.6 us (27%)
  Pallas kernels  19.3 us (9%)
  starting transfers between devices  17.9 us (8%)
  between operations  14.3 us (7%)
  local copies, waits for them, and re-layouts  4.72 us (2%)
    all_to_all x3, blocking collectives, exchange(): return lax.all_to_all(x, axes, split_axis=0, concat_axis=0, tiled=True)  97 us
    all_to_all x4, waiting for transfers between devices, exchange(): return lax.all_to_all(x, axes, split_axis=0, concat_axis=0, tiled=True)  57.6 us
    all_to_all x4, starting transfers between devices, exchange(): return lax.all_to_all(x, axes, split_axis=0, concat_axis=0, tiled=True)  17.9 us
    pallas_call x1, Pallas kernels, body(): pl.pallas_call(middle_kernel, out_shape=(shape((total, width), BF16), sha...  11 us
    unnamed x35, local copies, waits for them, and re-layouts  4.6 us
  transfers between devices with their start and end apart: 5, of which 4 were waited for; matrix products, arithmetic and copies ran while one was open for 0% of the time, Pallas kernels for 3%

profile of v2, /device:TPU:8, one launch (start us, length us, event | category | flops | bytes accessed | tf_op | source)
XLA Modules:
  0.0 210.7 jit_solution(6739267739817513626)
XLA Ops:
  7.2 0.8 copy-done.7
  8.0 0.7 copy-done.10
  8.8 0.7 copy-done.11
  9.5 0.1 weights_pack.1
  9.6 45.9 %all_to_all.35.x_ref = bf16[16,40,768]{2,1,0:T(8,128)(2,1)S(1)} all-to-all(bf16[16,40,768]{2,1,0:T(8,128)(2,1)S(1)} %weights_pack.1), channel_id=1, replica_groups=mesh['tm'=16,'space'=8,'dp'=4] {'tm'}, dimensions={0} | all-to-all | bytes 1966080 | tf_op jit(solution)/shard_map/all_to_all | solution.py:299
  55.5 1.5 weights_unpack.1
  57.1 1.1 pack.1
  58.2 26.7 %all_to_all.36.x_ref = bf16[16,24,768]{2,1,0:T(8,128)(2,1)S(1)} all-to-all(bf16[16,24,768]{2,1,0:T(8,128)(2,1)S(1)} %get-tuple-element.24), channel_id=1, replica_groups=mesh['tm'=16,'space'=8,'dp'=4] {'tm'}, dimensions={0} | all-to-all | bytes 1179648 | tf_op jit(solution)/shard_map/all_to_all | solution.py:299
  84.9 4.3 %all-to-all-start.2 = ((bf16[8,16,2048]{2,1,0:T(8,128)(2,1)}), bf16[8,16,2048]{2,1,0:T(8,128)(2,1)S(1)}, u32[]{:S(2)}, u32[]{:S(2)}) async-start(bf16[8,16,2048]{2,1,0:T(8,128)(2,1)} %get-tuple-element.28), calls=%async_computation.2 | async-start | bytes 1048576 | tf_op jit(solution)/shard_map/all_to_all | solution.py:299
  89.2 1.8 temporal_forward.1
  91.0 14.5 %all-to-all-done.2 = bf16[8,16,2048]{2,1,0:T(8,128)(2,1)S(1)} async-done(((bf16[8,16,2048]{2,1,0:T(8,128)(2,1)}), bf16[8,16,2048]{2,1,0:T(8,128)(2,1)S(1)}, u32[]{:S(2)}, u32[]{:S(2)}) %all-to-all-start.2) | async-done | bytes 524320 | tf_op jit(solution)/shard_map/all_to_all | solution.py:299
  105.5 6.6 %all-to-all-start.3 = ((bf16[128,6,128]{2,1,0:T(8,128)(2,1)}), bf16[128,6,128]{2,1,0:T(8,128)(2,1)S(1)}, u32[]{:S(2)}, u32[]{:S(2)}) async-start(bf16[128,6,128]{2,1,0:T(8,128)(2,1)} %get-tuple-element.29), calls=%async_computation.3 | async-start | bytes 524288 | tf_op jit(solution)/shard_map/all_to_all | solution.py:299
  112.0 0.1 copy.22.row_ref
  112.1 16.5 %all-to-all-done.3.x_ref = bf16[128,6,128]{2,1,0:T(8,128)(2,1)S(1)} async-done(((bf16[128,6,128]{2,1,0:T(8,128)(2,1)}), bf16[128,6,128]{2,1,0:T(8,128)(2,1)S(1)}, u32[]{:S(2)}, u32[]{:S(2)}) %all-to-all-start.3) | async-done | bytes 196640 | tf_op jit(solution)/shard_map/all_to_all | solution.py:299
  128.7 1.6 copy-done.15
  130.2 11.0 %middle.1 = (bf16[128,1024]{1,0:T(8,128)(2,1)}, bf16[128,6,128]{2,1,0:T(8,128)(2,1)S(1)}) custom-call(bf16[8,640,768]{2,1,0:T(8,128)(2,1)} %bitcast.10, bf16[128,6,128]{2,1,0:T(8,128)(2,1)S(1)} %all-to-all-done.3.x_ref, bf16[128,2048]{1,0:T(8,128)(2,1)S(1)} %bitcast.6, f32[1,1024]{1,0:T(1,128)S(1)} %bitcast.8, f32[12]{0:T(128)S(1)} %copy-done.14, ...), custom_call_target="tpu_custom_call" | custom-call | flops 4000000000 | bytes 10000000 | tf_op jit(solution)/shard_map/middle/pallas_call | solution.py:355
  141.3 24.4 %all_to_all.37.g_ref = bf16[128,6,128]{2,1,0:T(8,128)(2,1)S(1)} all-to-all(bf16[128,6,128]{2,1,0:T(8,128)(2,1)S(1)} %get-tuple-element.32), channel_id=1, replica_groups=mesh['tm'=16,'space'=8,'dp'=4] {'tm','space'}, dimensions={0} | all-to-all | bytes 393216 | tf_op jit(solution)/shard_map/all_to_all | solution.py:299
  165.7 3.4 %all-to-all-start.5 = ((bf16[8,16,1024]{2,1,0:T(8,128)(2,1)}), bf16[8,16,1024]{2,1,0:T(8,128)(2,1)S(1)}, u32[]{:S(2)}, u32[]{:S(2)}) async-start(bf16[8,16,1024]{2,1,0:T(8,128)(2,1)} %bitcast.4), calls=%async_computation.5 | async-start | bytes 524288 | tf_op jit(solution)/shard_map/all_to_all | solution.py:299
  169.1 2.9 %temporal_backward.1 = bf16[16,24,768]{2,1,0:T(8,128)(2,1)} custom-call(bf16[16,24,768]{2,1,0:T(8,128)(2,1)S(1)} %all_to_all.36.x_ref, f32[6,128,256]{2,1,0:T(8,128)S(1)} %get-tuple-element.26.p_ref, bf16[128,6,128]{2,1,0:T(8,128)(2,1)S(1)} %all_to_all.37.g_ref), custom_call_target="tpu_custom_call" | custom-call | flops 300000000 | bytes 2000000 | tf_op jit(solution)/shard_map/temporal_backward/pallas_call | solution.py:388
  172.0 4.6 %all-to-all-done.5 = bf16[8,16,1024]{2,1,0:T(8,128)(2,1)S(1)} async-done(((bf16[8,16,1024]{2,1,0:T(8,128)(2,1)}), bf16[8,16,1024]{2,1,0:T(8,128)(2,1)S(1)}, u32[]{:S(2)}, u32[]{:S(2)}) %all-to-all-start.5) | async-done | bytes 262176 | tf_op jit(solution)/shard_map/all_to_all | solution.py:299
  176.6 3.6 %all-to-all-start.6 = ((bf16[16,24,768]{2,1,0:T(8,128)(2,1)}), bf16[16,24,768]{2,1,0:T(8,128)(2,1)S(1)}, u32[]{:S(2)}, u32[]{:S(2)}) async-start(bf16[16,24,768]{2,1,0:T(8,128)(2,1)} %temporal_backward.1), calls=%async_computation.6 | async-start | bytes 1179648 | tf_op jit(solution)/shard_map/all_to_all | solution.py:299
  180.2 22.0 %all-to-all-done.6.x_ref = bf16[16,24,768]{2,1,0:T(8,128)(2,1)S(1)} async-done(((bf16[16,24,768]{2,1,0:T(8,128)(2,1)}), bf16[16,24,768]{2,1,0:T(8,128)(2,1)S(1)}, u32[]{:S(2)}, u32[]{:S(2)}) %all-to-all-start.6) | async-done | bytes 589856 | tf_op jit(solution)/shard_map/all_to_all | solution.py:299
  202.2 1.0 unpack.1
  203.2 0.7 copy.24
  (33 shorter events, 0.1 us)
Async XLA Ops:
  7.2 48.3 %copy-start = (bf16[3,3,64,256]{3,2,1,0:T(8,128)(2,1)S(1)}, bf16[3,3,64,256]{3,2,1,0:T(8,128)(2,1)}, u32[]{:S(2)}) copy-start(bf16[3,3,64,256]{3,2,1,0:T(8,128)(2,1)} %constant.15.clone.rest_ref) | copy-start | bytes 884740
  7.2 48.3 %copy-start.6 = (bf16[192,256]{1,0:T(8,128)(2,1)S(1)}, bf16[192,256]{1,0:T(8,128)(2,1)}, u32[]{:S(2)}) copy-start(bf16[192,256]{1,0:T(8,128)(2,1)} %constant.14.clone.main_ref) | copy-start | bytes 294916
  7.2 121.4 %all-gather.3.cloned.1.call-start = ((), (), s32[]{:S(2)}) async-start(), calls=%async_computation.7 | async-start | bytes 8847360 | tf_op jit(solution)/shard_map/all_gather | solution.py:335
  7.2 0.8 copy-start.7
  8.0 0.7 copy-start.10
  8.8 0.7 copy-start.11
  55.4 1.5 copy-start.1
  55.4 1.6 copy-start.2
  55.4 1.6 copy-start.3
  55.5 1.6 copy-start.4
  55.5 1.5 copy-start.5
  55.5 1.5 copy-start.9
  57.0 55.0 %copy-start.12 = (s32[1,128]{1,0:T(1,128)S(1)}, s32[1,128]{1,0:T(1,128)}, u32[]{:S(2)}) copy-start(s32[1,128]{1,0:T(1,128)} %col_ref.1) | copy-start | bytes 1540
  57.0 71.6 %copy-start.8 = (bf16[128,128]{1,0:T(8,128)(2,1)S(1)}, bf16[128,128]{1,0:T(8,128)(2,1)}, u32[]{:S(2)}) copy-start(bf16[128,128]{1,0:T(8,128)(2,1)} %constant.13.clone.turn_ref) | copy-start | bytes 98308
  57.1 71.6 %copy-start.13 = (f32[1024]{0:T(1024)S(1)}, f32[1024]{0:T(1024)}, u32[]{:S(2)}) copy-start(f32[1024]{0:T(1024)} %param.23) | copy-start | bytes 12292
  57.1 71.6 %copy-start.14 = (f32[12]{0:T(128)S(1)}, f32[12]{0:T(128)}, u32[]{:S(2)}) copy-start(f32[12]{0:T(128)} %slope_ref.1) | copy-start | bytes 148
  57.1 71.6 %copy-start.16 = (bf16[768,768]{1,0:T(8,128)(2,1)S(1)}, bf16[768,768]{1,0:T(8,128)(2,1)}, u32[]{:S(2)}) copy-start(bf16[768,768]{1,0:T(8,128)(2,1)} %constant.16.clone.inner_ref) | copy-start | bytes 3538948
  84.9 20.6 %all-to-all-start.2 = ((bf16[8,16,2048]{2,1,0:T(8,128)(2,1)}), bf16[8,16,2048]{2,1,0:T(8,128)(2,1)S(1)}, u32[]{:S(2)}, u32[]{:S(2)}) async-start(bf16[8,16,2048]{2,1,0:T(8,128)(2,1)} %get-tuple-element.28), calls=%async_computation.2 | async-start | bytes 1048576 | tf_op jit(solution)/shard_map/all_to_all | solution.py:299
  105.5 23.2 %all-to-all-start.3 = ((bf16[128,6,128]{2,1,0:T(8,128)(2,1)}), bf16[128,6,128]{2,1,0:T(8,128)(2,1)S(1)}, u32[]{:S(2)}, u32[]{:S(2)}) async-start(bf16[128,6,128]{2,1,0:T(8,128)(2,1)} %get-tuple-element.29), calls=%async_computation.3 | async-start | bytes 524288 | tf_op jit(solution)/shard_map/all_to_all | solution.py:299
  128.6 1.6 copy-start.15
  165.7 10.9 %all-to-all-start.5 = ((bf16[8,16,1024]{2,1,0:T(8,128)(2,1)}), bf16[8,16,1024]{2,1,0:T(8,128)(2,1)S(1)}, u32[]{:S(2)}, u32[]{:S(2)}) async-start(bf16[8,16,1024]{2,1,0:T(8,128)(2,1)} %bitcast.4), calls=%async_computation.5 | async-start | bytes 524288 | tf_op jit(solution)/shard_map/all_to_all | solution.py:299
  176.6 25.6 %all-to-all-start.6 = ((bf16[16,24,768]{2,1,0:T(8,128)(2,1)}), bf16[16,24,768]{2,1,0:T(8,128)(2,1)S(1)}, u32[]{:S(2)}, u32[]{:S(2)}) async-start(bf16[16,24,768]{2,1,0:T(8,128)(2,1)} %temporal_backward.1), calls=%async_computation.6 | async-start | bytes 1179648 | tf_op jit(solution)/shard_map/all_to_all | solution.py:299
Sparse Core Ops, SparseCore 0:
  57.1 52.4 all-gather.2

commit v3 on v2

--- a/solution.py
+++ b/solution.py
@@ -15,7 +15,7 @@
 BF16 = jnp.bfloat16
 VMEM = pl.BlockSpec(memory_space=pltpu.VMEM)
 SMEM = pl.BlockSpec(memory_space=pltpu.SMEM)
-ANY = pl.BlockSpec(memory_space=pl.ANY)
+HBM = pl.BlockSpec(memory_space=pltpu.HBM)
 
 
 def params(mib):
@@ -62,7 +62,19 @@
     return main.astype(BF16), rest.astype(BF16)
 
 
-def weights_pack_kernel(fc_ref, out_ref, qkv_ref, o_ref):
+def first_kernel(fc_hbm, out_hbm, qkv_hbm, res_hbm, cot_hbm, o_ref, rest_hbm, fc_ref, out_ref, qkv_ref, sem):
+    width = res_hbm.shape[-1]
+    copies = [
+        pltpu.make_async_copy(res_hbm.at[0], rest_hbm.at[:, :, pl.ds(0, width)], sem.at[0]),
+        pltpu.make_async_copy(cot_hbm.at[0], rest_hbm.at[:, :, pl.ds(width, width)], sem.at[1]),
+        pltpu.make_async_copy(fc_hbm, fc_ref, sem.at[2]),
+        pltpu.make_async_copy(out_hbm, out_ref, sem.at[3]),
+        pltpu.make_async_copy(qkv_hbm, qkv_ref, sem.at[4]),
+    ]
+    for c in copies:
+        c.start()
+    for c in copies[2:]:
+        c.wait()
     both = jnp.concatenate([fc_ref[...].astype(F32), out_ref[...].astype(F32)], axis=0)
     tail = both[:, 768:]
     tail = jnp.concatenate([tail[0:4], tail[4:8], tail[8:12]], axis=1)
@@ -71,6 +83,8 @@
         [both[:, :768], tail, qkv[:, :768], qkv[:, 768:1536], qkv[:, 1536:]], axis=0
     )
     o_ref[...] = jnp.broadcast_to(block[None], o_ref.shape).astype(BF16)
+    for c in copies[:2]:
+        c.wait()
 
 
 def weights_unpack_kernel(x_ref, main_ref, rest_ref, o_ref):
@@ -88,7 +102,7 @@
         o_ref[pl.ds(3 * n + 12 * tm, 4 * tm), pl.ds(j * 256, 256)] = part.astype(BF16)
 
 
-def pack_kernel(q_ref, k_ref, v_ref, res_ref, cot_ref, turn_ref, o_ref, rest_ref):
+def pack_kernel(q_ref, k_ref, v_ref, turn_ref, o_ref):
     steps, tubes, inner = q_ref.shape[1:]
     rows = steps * tubes
     parts = [
@@ -96,15 +110,20 @@
         for ref in (q_ref, k_ref, v_ref)
     ]
     o_ref[...] = jnp.concatenate(parts, axis=1).astype(BF16)
-    rest_ref[...] = jnp.concatenate([res_ref[0], cot_ref[0]], axis=-1)
-
-
-def unpack_kernel(x_ref, turn_ref, *outs):
+
+
+def unpack_kernel(me_ref, x_ref, turn_ref, gr_hbm, *refs):
+    outs, gr_out, sem = refs[:3], refs[3], refs[4]
+    mine = outs[0].shape[2]
+    at = pl.multiple_of(me_ref[0] * mine, mine)
+    copy = pltpu.make_async_copy(gr_hbm.at[:, pl.ds(at, mine), :], gr_out.at[0], sem)
+    copy.start()
     x = x_ref[...].astype(F32)
     tubes, steps = x.shape[0], x.shape[1] // 3
     for j, o_ref in enumerate(outs):
         part = x[:, j * steps : (j + 1) * steps].reshape(tubes * steps, -1).astype(BF16)
         o_ref[0] = nn(turn_ref[...], part).astype(BF16).reshape(steps, tubes, -1)
+    copy.wait()
 
 
 def lane_masks(rows):
@@ -189,8 +208,8 @@
 
 
 def middle_kernel(
-    w_hbm, x_ref, rest_ref, gain_ref, slope_ref, row_ref, col_ref, turn_ref, inner_ref, width_ref,
-    gr_ref, gt_ref, qkv_v, fc_v, out_v, turned, proj, joined, sem,
+    me_ref, w_hbm, x_ref, rest_hbm, gain_ref, slope_ref, row_ref, col_ref, turn_ref, inner_hbm, width_hbm,
+    gr_ref, gt_ref, rest_v, inner_ref, width_v, qkv_v, fc_v, out_v, turned, proj, joined, sem,
 ):
     sp = w_hbm.shape[0]
     tm = w_hbm.shape[1] // 40
@@ -201,6 +220,8 @@
         copies.append(pltpu.make_async_copy(src, dst, sem.at[len(copies)]))
         copies[-1].start()
 
+    load(inner_hbm, inner_ref)
+    load(rest_hbm.at[:, me_ref[0]], rest_v)
     at = 3 * n
     for dst, base, tail in (
         (fc_v, at, at + 12 * tm),
@@ -212,6 +233,7 @@
                 w_hbm.at[:, pl.ds(tail, third), pl.ds(j * 256, 256)],
                 dst.at[:, pl.ds(j * third, third), pl.ds(768, 256)],
             )
+    load(width_hbm, width_v)
     for j in range(3):
         load(w_hbm.at[:, pl.ds(j * n, n), :], qkv_v.at[:, :, pl.ds(j * 768, 768)])
 
@@ -226,25 +248,26 @@
     turned[...] = x_ref[...].astype(F32)
     mixed = jnp.concatenate([turned[:, h, :] for h in range(6)], axis=1).astype(BF16)
     mixed = nn(turn, mixed).astype(BF16)
+
+    for c in copies[:6]:
+        c.wait()
     mixed = nn(mixed, inner_ref[...]).astype(BF16)
-    cot = rest_ref[:, width:]
-
-    for c in copies[:4]:
-        c.wait()
+    rest = rest_v[...].reshape(tokens, 2 * width)
+    cot = rest[:, width:]
     fc = fc_v[...].reshape(inner, width)
-    hidden = rest_ref[:, :width].astype(F32) + nn(mixed, fc)
+    hidden = rest[:, :width].astype(F32) + nn(mixed, fc)
     centred = hidden - jnp.mean(hidden, axis=-1, keepdims=True)
     inv_std = lax.rsqrt(jnp.mean(centred * centred, axis=-1, keepdims=True) + EPSILON)
     normed = centred * inv_std
     normed_in = (normed * gain).astype(BF16)
-    normed_in = nn(normed_in, width_ref[...]).astype(BF16)
-
-    for c in copies[4:8]:
+
+    for c in copies[6:11]:
         c.wait()
+    normed_in = nn(normed_in, width_v[...]).astype(BF16)
     grad_mixed = nt(cot, out_v[...].reshape(inner, width)).astype(BF16)
     grad_mixed = nt(grad_mixed, inner_ref[...]).astype(BF16)
 
-    for c in copies[8:]:
+    for c in copies[11:]:
         c.wait()
     qkv = qkv_v[...].reshape(width, 3 * inner)
     proj[...] = nn(normed_in, qkv).astype(BF16)
@@ -260,7 +283,7 @@
             joined[:, j * inner + h * 128 : j * inner + (h + 1) * 128] = d.astype(BF16)
 
     grad_normed = nt(joined[...], qkv).astype(BF16)
-    grad_normed = nt(grad_normed, width_ref[...])
+    grad_normed = nt(grad_normed, width_v[...])
     scaled = grad_normed * gain
     first_mean = jnp.mean(scaled, axis=-1, keepdims=True)
     second_mean = jnp.mean(scaled * normed, axis=-1, keepdims=True)
@@ -305,24 +328,33 @@
     inner_map = jnp.asarray(gathered_order(tm, sp, fc_weight.shape[0]))
     width_map = jnp.asarray(gathered_order(tm, sp, qkv_weight.shape[0]))
 
-    shards = pl.pallas_call(
-        weights_pack_kernel,
-        out_shape=shape((tm, 40, inner), BF16),
-        in_specs=[VMEM] * 3,
+    me = lax.axis_index("space").astype(jnp.int32).reshape(1)
+    shards, rest = pl.pallas_call(
+        first_kernel,
+        out_shape=(shape((tm, 40, inner), BF16), shape((steps, tubes, 2 * width), BF16)),
+        in_specs=[HBM] * 5,
+        out_specs=(VMEM, HBM),
+        scratch_shapes=[
+            pltpu.VMEM(fc_weight.shape, BF16),
+            pltpu.VMEM(out_weight.shape, BF16),
+            pltpu.VMEM(qkv_weight.shape, BF16),
+            pltpu.SemaphoreType.DMA((5,)),
+        ],
+        compiler_params=params(56),
+        name="first",
+    )(fc_weight, out_weight, qkv_weight, residual_in, cotangent)
+    rest = lax.all_gather(rest, "space", axis=0)
+    shards = exchange(shards, "tm")
+
+    send = pl.pallas_call(
+        pack_kernel,
+        out_shape=shape((tubes, 3 * steps, inner), BF16),
+        in_specs=[VMEM] * 4,
         out_specs=VMEM,
         compiler_params=params(16),
-        name="weights_pack",
-    )(fc_weight, out_weight, qkv_weight)
-    shards = exchange(shards, "tm")
-
-    send, rest = pl.pallas_call(
-        pack_kernel,
-        out_shape=(shape((tubes, 3 * steps, inner), BF16), shape((steps, tubes, 2 * width), BF16)),
-        in_specs=[VMEM] * 6,
-        out_specs=(VMEM, VMEM),
-        compiler_params=params(16),
+        cost_estimate=pl.CostEstimate(flops=10**9, bytes_accessed=4 * 10**6, transcendentals=0),
         name="pack",
-    )(time_query, time_key, time_value, residual_in, cotangent, to_tubes)
+    )(time_query, time_key, time_value, to_tubes)
 
     shards = pl.pallas_call(
         weights_unpack_kernel,
@@ -336,8 +368,6 @@
 
     send, shards = lax.optimization_barrier((send, shards))
     got = exchange(send, "tm")
-    rest, got = lax.optimization_barrier((rest, got))
-    rest = exchange(rest, "space").reshape(total, 2 * width)
 
     mixed, probs = pl.pallas_call(
         forward_kernel,
@@ -349,27 +379,30 @@
         cost_estimate=pl.CostEstimate(flops=10**8, bytes_accessed=2 * 10**6, transcendentals=2 * 10**5),
         name="temporal_forward",
     )(got)
-    mixed, rest = lax.optimization_barrier((mixed, rest))
     mixed = exchange(mixed, both)
 
     grad_resid, grad_time = pl.pallas_call(
         middle_kernel,
         out_shape=(shape((total, width), BF16), shape((total, 6, 128), BF16)),
-        in_specs=[ANY, VMEM, VMEM, VMEM, SMEM, VMEM, VMEM, VMEM, VMEM, VMEM],
+        in_specs=[SMEM, HBM, VMEM, HBM, VMEM, SMEM, VMEM, VMEM, VMEM, HBM, HBM],
         out_specs=(VMEM, VMEM),
         scratch_shapes=[
+            pltpu.VMEM((sp, tubes, 2 * width), BF16),
+            pltpu.VMEM((inner, inner), BF16),
+            pltpu.VMEM((width, width), BF16),
             pltpu.VMEM((sp, 8 * tm, 3 * inner), BF16),
             pltpu.VMEM((sp, 6 * tm, width), BF16),
             pltpu.VMEM((sp, 6 * tm, width), BF16),
             pltpu.VMEM((total, 6, 128), F32),
             pltpu.VMEM((total, 3 * inner), BF16),
             pltpu.VMEM((total, 3 * inner), BF16),
-            pltpu.SemaphoreType.DMA((11,)),
+            pltpu.SemaphoreType.DMA((14,)),
         ],
         compiler_params=params(48),
         cost_estimate=pl.CostEstimate(flops=4 * 10**9, bytes_accessed=10**7, transcendentals=2 * 10**5),
         name="middle",
     )(
+        me,
         weights,
         mixed,
         rest,
@@ -381,9 +414,8 @@
         inner_map,
         width_map,
     )
+    grad_resid = lax.all_gather(grad_resid, "space", axis=0)
     grad_time = exchange(grad_time, both)
-    grad_resid, grad_time = lax.optimization_barrier((grad_resid, grad_time))
-    grad_resid = exchange(grad_resid.reshape(steps, tubes, width), "space")
 
     back = pl.pallas_call(
         backward_kernel,
@@ -395,17 +427,17 @@
         cost_estimate=pl.CostEstimate(flops=3 * 10**8, bytes_accessed=2 * 10**6, transcendentals=0),
         name="temporal_backward",
     )(got, probs, grad_time)
-    back, grad_resid = lax.optimization_barrier((back, grad_resid))
     back = exchange(back, "tm")
     outs = pl.pallas_call(
         unpack_kernel,
-        out_shape=(shape(time_query.shape, BF16),) * 3,
-        in_specs=[VMEM] * 2,
-        out_specs=(VMEM,) * 3,
-        compiler_params=params(16),
+        out_shape=(shape(time_query.shape, BF16),) * 3 + (shape(residual_in.shape, BF16),),
+        in_specs=[SMEM, VMEM, VMEM, HBM],
+        out_specs=(VMEM, VMEM, VMEM, HBM),
+        scratch_shapes=[pltpu.SemaphoreType.DMA],
+        compiler_params=params(56),
         name="unpack",
-    )(back, to_steps)
-    return (grad_resid.reshape(residual_in.shape), *outs)
+    )(me, back, to_steps, grad_resid)
+    return (outs[3], *outs[:3])
 
 
 def solution(mesh):

time: 211 us -> 221 us (1.047)
  waiting for transfers between devices: 57.6 us -> 16.5 us
  blocking collectives: 97 us -> 132 us
  Pallas kernels: 19.3 us -> 46.2 us
  starting transfers between devices: 17.9 us -> 8.44 us
    all_to_all x4 -> x1, waiting for transfers between devices: 57.6 us -> 16.4 us  [exchange(): return lax.all_to_all(x, axes, split_axis=0, concat_axis=0, tiled=True)]
    all_to_all x3 -> x4, blocking collectives: 97 us -> 132 us  [exchange(): return lax.all_to_all(x, axes, split_axis=0, concat_axis=0, tiled=True)]
    pallas_call x2, Pallas kernels: 1.13 us -> 18.3 us  [the longest x1 18 us: body(): pl.pallas_call(first_kernel, out_shape=(shape((tm, 40, inner), BF16), sha...]
    pallas_call x1, Pallas kernels: 1.02 us -> 10.9 us  [body(): pl.pallas_call(unpack_kernel, out_shape=(shape(time_query.shape, BF16),)...]
    all_to_all x4 -> x1, starting transfers between devices: 17.9 us -> 8.32 us  [exchange(): return lax.all_to_all(x, axes, split_axis=0, concat_axis=0, tiled=True)]
    unnamed x35 -> x28, local copies, waits for them, and re-layouts: 4.6 us -> 3.35 us
  transfers between devices with their start and end apart: 5 -> 4, of which waited for: 4 -> 1; matrix products, arithmetic and copies ran while one was open for 0% -> 0% of each run, Pallas kernels for 3% -> 3%
where the time goes in v3:
time: 221 us; the launch traced here: 220 us
  blocking collectives  132 us (60%)
  Pallas kernels  46.2 us (21%)
  waiting for transfers between devices  16.5 us (7%)
  between operations  14 us (6%)
  starting transfers between devices  8.44 us (4%)
  local copies, waits for them, and re-layouts  3.47 us (2%)
    all_to_all x4, blocking collectives, exchange(): return lax.all_to_all(x, axes, split_axis=0, concat_axis=0, tiled=True)  132 us
    pallas_call x1, Pallas kernels, body(): pl.pallas_call(first_kernel, out_shape=(shape((tm, 40, inner), BF16), sha...  18 us
    all_to_all x1, waiting for transfers between devices, exchange(): return lax.all_to_all(x, axes, split_axis=0, concat_axis=0, tiled=True)  16.4 us
    pallas_call x1, Pallas kernels, body(): pl.pallas_call(middle_kernel, out_shape=(shape((total, width), BF16), sha...  11.7 us
    pallas_call x1, Pallas kernels, body(): pl.pallas_call(unpack_kernel, out_shape=(shape(time_query.shape, BF16),)...  10.9 us
    all_to_all x1, starting transfers between devices, exchange(): return lax.all_to_all(x, axes, split_axis=0, concat_axis=0, tiled=True)  8.32 us
  transfers between devices with their start and end apart: 4, of which 1 were waited for; matrix products, arithmetic and copies ran while one was open for 0% of the time, Pallas kernels for 3%

profile of v3, /device:TPU:8, one launch (start us, length us, event | category | flops | bytes accessed | tf_op | source)
XLA Modules:
  0.0 220.0 jit_solution(12863453984368142043)
XLA Ops:
  7.2 0.0 copy-start.4
  7.2 0.0 all-gather.9.cloned.1.call-start
  7.2 18.0 %first.1 = (bf16[16,40,768]{2,1,0:T(8,128)(2,1)}, bf16[8,16,2048]{2,1,0:T(8,128)(2,1)}) custom-call(bf16[6,1024]{1,0:T(8,128)(2,1)} %fc_hbm.1, bf16[6,1024]{1,0:T(8,128)(2,1)} %out_hbm.1, bf16[8,2304]{1,0:T(8,128)(2,1)} %qkv_hbm.1, bf16[1,8,16,1024]{3,2,1,0:T(8,128)(2,1)} %res_hbm.1, bf16[1,8,16,1024]{3,2,1,0:T(8,128)(2,1)} %cot_hbm.1), custom_call_target="tpu_custom_call" | custom-call | tf_op jit(solution)/shard_map/first/pallas_call | solution.py:332
  25.2 0.0 all-gather.9.cloned.1.call-update
  25.3 0.0 all-gather.7.cloned.1.call-start
  25.3 46.1 %all_to_all.25.x_ref = bf16[16,40,768]{2,1,0:T(8,128)(2,1)S(1)} all-to-all(bf16[16,40,768]{2,1,0:T(8,128)(2,1)} %get-tuple-element.15), channel_id=1, replica_groups=mesh['tm'=16,'space'=8,'dp'=4] {'tm'}, dimensions={0} | all-to-all | bytes 1966080 | tf_op jit(solution)/shard_map/all_to_all | solution.py:322
  71.5 1.4 weights_unpack.1
  72.9 0.0 all-gather.7.cloned.1.call-update
  73.0 0.3 pack.1
  73.3 26.9 %all_to_all.26.x_ref = bf16[16,24,768]{2,1,0:T(8,128)(2,1)S(1)} all-to-all(bf16[16,24,768]{2,1,0:T(8,128)(2,1)S(1)} %pack.1), channel_id=1, replica_groups=mesh['tm'=16,'space'=8,'dp'=4] {'tm'}, dimensions={0} | all-to-all | bytes 1179648 | tf_op jit(solution)/shard_map/all_to_all | solution.py:322
  100.3 1.8 temporal_forward.1
  102.1 0.9 copy-done.2
  103.0 8.3 %all-to-all-start.2 = ((bf16[128,6,128]{2,1,0:T(8,128)(2,1)}), bf16[128,6,128]{2,1,0:T(8,128)(2,1)S(1)}, u32[]{:S(2)}, u32[]{:S(2)}) async-start(bf16[128,6,128]{2,1,0:T(8,128)(2,1)} %get-tuple-element.18), calls=%async_computation.2 | async-start | bytes 524288 | tf_op jit(solution)/shard_map/all_to_all | solution.py:322
  111.3 0.0 all-gather.11.cloned.1.call-start
  111.4 0.1 copy.23.row_ref
  111.5 16.4 %all-to-all-done.2.x_ref = bf16[128,6,128]{2,1,0:T(8,128)(2,1)S(1)} async-done(((bf16[128,6,128]{2,1,0:T(8,128)(2,1)}), bf16[128,6,128]{2,1,0:T(8,128)(2,1)S(1)}, u32[]{:S(2)}, u32[]{:S(2)}) %all-to-all-start.2) | async-done | bytes 196640 | tf_op jit(solution)/shard_map/all_to_all | solution.py:322
  128.0 1.3 copy-done.1
  129.2 11.7 %middle.1 = (bf16[128,1024]{1,0:T(8,128)(2,1)}, bf16[128,6,128]{2,1,0:T(8,128)(2,1)S(1)}) custom-call(s32[1]{0:T(128)} %bitcast.me_ref, bf16[8,640,768]{2,1,0:T(8,128)(2,1)} %bitcast.8, bf16[128,6,128]{2,1,0:T(8,128)(2,1)S(1)} %all-to-all-done.2.x_ref, bf16[8,8,16,2048]{3,2,1,0:T(8,128)(2,1)} %bitcast.9, f32[1,1024]{1,0:T(1,128)S(1)} %bitcast.6, ...), custom_call_target="tpu_custom_call" | custom-call | flops 4000000000 | bytes 10000000 | tf_op jit(solution)/shard_map/middle/pallas_call | solution.py:384
  140.9 0.0 all-gather.11.cloned.1.call-update
  140.9 30.5 %all_to_all.27.g_ref = bf16[128,6,128]{2,1,0:T(8,128)(2,1)S(1)} all-to-all(bf16[128,6,128]{2,1,0:T(8,128)(2,1)S(1)} %get-tuple-element.20), channel_id=1, replica_groups=mesh['tm'=16,'space'=8,'dp'=4] {'tm','space'}, dimensions={0} | all-to-all | bytes 393216 | tf_op jit(solution)/shard_map/all_to_all | solution.py:322
  171.4 1.1 copy-done.3
  172.5 2.0 temporal_backward.1
  174.5 28.0 %all_to_all.28.x_ref = bf16[16,24,768]{2,1,0:T(8,128)(2,1)} all-to-all(bf16[16,24,768]{2,1,0:T(8,128)(2,1)S(1)} %temporal_backward.1), channel_id=1, replica_groups=mesh['tm'=16,'space'=8,'dp'=4] {'tm'}, dimensions={0} | all-to-all | bytes 1179648 | tf_op jit(solution)/shard_map/all_to_all | solution.py:322
  202.6 10.9 %unpack.1 = (bf16[1,8,16,768]{3,2,1,0:T(8,128)(2,1)}, bf16[1,8,16,768]{3,2,1,0:T(8,128)(2,1)}, bf16[1,8,16,768]{3,2,1,0:T(8,128)(2,1)}, bf16[1,8,16,1024]{3,2,1,0:T(8,128)(2,1)}) custom-call(s32[1]{0:T(128)} %bitcast.me_ref, bf16[16,24,768]{2,1,0:T(8,128)(2,1)} %all_to_all.28.x_ref, bf16[128,128]{1,0:T(8,128)(2,1)} %constant.19.clone.turn_ref, ...), custom_call_target="tpu_custom_call" | custom-call | tf_op jit(solution)/shard_map/unpack/pallas_call | solution.py:431
  (27 shorter events, 0.1 us)
Async XLA Ops:
  7.2 64.2 %copy-start.4 = (bf16[3,3,64,256]{3,2,1,0:T(8,128)(2,1)S(1)}, bf16[3,3,64,256]{3,2,1,0:T(8,128)(2,1)}, u32[]{:S(2)}) copy-start(bf16[3,3,64,256]{3,2,1,0:T(8,128)(2,1)} %constant.21.clone.rest_ref) | copy-start | bytes 884740
  7.2 64.2 %copy-start.6 = (bf16[192,256]{1,0:T(8,128)(2,1)S(1)}, bf16[192,256]{1,0:T(8,128)(2,1)}, u32[]{:S(2)}) copy-start(bf16[192,256]{1,0:T(8,128)(2,1)} %constant.20.clone.main_ref) | copy-start | bytes 294916
  7.2 120.7 %all-gather.9.cloned.1.call-start = ((), (), s32[]{:S(2)}) async-start(), calls=%async_computation.6 | async-start | bytes 4718592 | tf_op jit(solution)/shard_map/all_gather | solution.py:346
  25.3 102.6 %all-gather.7.cloned.1.call-start = ((), (), s32[]{:S(2)}) async-start(), calls=%async_computation.5 | async-start | bytes 8847360 | tf_op jit(solution)/shard_map/all_gather | solution.py:367
  71.4 1.5 copy-start.10
  71.4 1.5 copy-start.11
  71.4 1.5 copy-start.12
  71.4 1.5 copy-start.13
  73.0 38.4 %copy-start.8 = (s32[1,128]{1,0:T(1,128)S(1)}, s32[1,128]{1,0:T(1,128)}, u32[]{:S(2)}) copy-start(s32[1,128]{1,0:T(1,128)} %col_ref.1) | copy-start | bytes 1540
  73.3 54.6 %copy-start = (bf16[1024,1024]{1,0:T(8,128)(2,1)S(1)}, bf16[1024,1024]{1,0:T(8,128)(2,1)}, u32[]{:S(2)}) copy-start(bf16[1024,1024]{1,0:T(8,128)(2,1)} %constant.23.clone.width_hbm) | copy-start | bytes 6291460
  73.3 54.6 %copy-start.5 = (bf16[128,128]{1,0:T(8,128)(2,1)S(1)}, bf16[128,128]{1,0:T(8,128)(2,1)}, u32[]{:S(2)}) copy-start(bf16[128,128]{1,0:T(8,128)(2,1)} %constant.19.clone.turn_ref) | copy-start | bytes 98308
  73.3 54.6 %copy-start.7 = (f32[1024]{0:T(1024)S(1)}, f32[1024]{0:T(1024)}, u32[]{:S(2)}) copy-start(f32[1024]{0:T(1024)} %param.23) | copy-start | bytes 12292
  73.3 54.6 %copy-start.9 = (f32[12]{0:T(128)S(1)}, f32[12]{0:T(128)}, u32[]{:S(2)}) copy-start(f32[12]{0:T(128)} %slope_ref.1) | copy-start | bytes 148
  102.1 0.9 copy-start.2
  103.0 24.9 %all-to-all-start.2 = ((bf16[128,6,128]{2,1,0:T(8,128)(2,1)}), bf16[128,6,128]{2,1,0:T(8,128)(2,1)S(1)}, u32[]{:S(2)}, u32[]{:S(2)}) async-start(bf16[128,6,128]{2,1,0:T(8,128)(2,1)} %get-tuple-element.18), calls=%async_computation.2 | async-start | bytes 524288 | tf_op jit(solution)/shard_map/all_to_all | solution.py:322
  111.3 91.3 %all-gather.11.cloned.1.call-start = ((), (), s32[]{:S(2)}) async-start(), calls=%async_computation.7 | async-start | bytes 2359296 | tf_op jit(solution)/shard_map/all_gather | solution.py:417
  127.9 1.3 copy-start.1
  171.4 1.1 copy-start.3
Sparse Core Ops, SparseCore 0:
  25.4 41.9 all-gather.8
  73.0 50.9 all-gather.6
  141.0 29.2 all-gather.10

commit v4 on v3

--- a/solution.py
+++ b/solution.py
@@ -62,11 +62,11 @@
     return main.astype(BF16), rest.astype(BF16)
 
 
-def first_kernel(fc_hbm, out_hbm, qkv_hbm, res_hbm, cot_hbm, o_ref, rest_hbm, fc_ref, out_ref, qkv_ref, sem):
+def first_kernel(fc_hbm, out_hbm, qkv_hbm, res_hbm, cot_hbm, o_ref, rest_ref, fc_ref, out_ref, qkv_ref, sem):
     width = res_hbm.shape[-1]
     copies = [
-        pltpu.make_async_copy(res_hbm.at[0], rest_hbm.at[:, :, pl.ds(0, width)], sem.at[0]),
-        pltpu.make_async_copy(cot_hbm.at[0], rest_hbm.at[:, :, pl.ds(width, width)], sem.at[1]),
+        pltpu.make_async_copy(res_hbm.at[0], rest_ref.at[:, :, pl.ds(0, width)], sem.at[0]),
+        pltpu.make_async_copy(cot_hbm.at[0], rest_ref.at[:, :, pl.ds(width, width)], sem.at[1]),
         pltpu.make_async_copy(fc_hbm, fc_ref, sem.at[2]),
         pltpu.make_async_copy(out_hbm, out_ref, sem.at[3]),
         pltpu.make_async_copy(qkv_hbm, qkv_ref, sem.at[4]),
@@ -333,7 +333,7 @@
         first_kernel,
         out_shape=(shape((tm, 40, inner), BF16), shape((steps, tubes, 2 * width), BF16)),
         in_specs=[HBM] * 5,
-        out_specs=(VMEM, HBM),
+        out_specs=(VMEM, VMEM),
         scratch_shapes=[
             pltpu.VMEM(fc_weight.shape, BF16),
             pltpu.VMEM(out_weight.shape, BF16),
@@ -375,7 +375,7 @@
         in_specs=[VMEM],
         out_specs=(VMEM, VMEM),
         scratch_shapes=[pltpu.VMEM((total, 6, 128), F32)],
-        compiler_params=params(24),
+        compiler_params=params(56),
         cost_estimate=pl.CostEstimate(flops=10**8, bytes_accessed=2 * 10**6, transcendentals=2 * 10**5),
         name="temporal_forward",
     )(got)
@@ -398,7 +398,7 @@
             pltpu.VMEM((total, 3 * inner), BF16),
             pltpu.SemaphoreType.DMA((14,)),
         ],
-        compiler_params=params(48),
+        compiler_params=params(56),
         cost_estimate=pl.CostEstimate(flops=4 * 10**9, bytes_accessed=10**7, transcendentals=2 * 10**5),
         name="middle",
     )(
@@ -423,7 +423,7 @@
         in_specs=[VMEM] * 3,
         out_specs=VMEM,
         scratch_shapes=[pltpu.VMEM((total, 6, 128), F32)],
-        compiler_params=params(24),
+        compiler_params=params(56),
         cost_estimate=pl.CostEstimate(flops=3 * 10**8, bytes_accessed=2 * 10**6, transcendentals=0),
         name="temporal_backward",
     )(got, probs, grad_time)
@@ -432,7 +432,7 @@
         unpack_kernel,
         out_shape=(shape(time_query.shape, BF16),) * 3 + (shape(residual_in.shape, BF16),),
         in_specs=[SMEM, VMEM, VMEM, HBM],
-        out_specs=(VMEM, VMEM, VMEM, HBM),
+        out_specs=(VMEM, VMEM, VMEM, VMEM),
         scratch_shapes=[pltpu.SemaphoreType.DMA],
         compiler_params=params(56),
         name="unpack",

time: 221 us -> 200 us (0.905)
  Pallas kernels: 46.2 us -> 27.4 us
    pallas_call x1, Pallas kernels: 18 us -> 2.24 us  [body(): pl.pallas_call(first_kernel, out_shape=(shape((tm, 40, inner), BF16), sha...]
    pallas_call x1, Pallas kernels: 10.9 us -> 2.93 us  [body(): pl.pallas_call(unpack_kernel, out_shape=(shape(time_query.shape, BF16),)...]
    unnamed x28 -> x16, local copies, waits for them, and re-layouts: 3.35 us -> 0.74 us
  transfers between devices with their start and end apart: 4 -> 4, of which waited for: 1 -> 1; matrix products, arithmetic and copies ran while one was open for 0% -> 0% of each run, Pallas kernels for 3% -> 4%
where the time goes in v4:
time: 200 us
  blocking collectives  132 us (66%)
  Pallas kernels  27.4 us (14%)
  waiting for transfers between devices  15.9 us (8%)
  between operations  13.9 us (7%)
  starting transfers between devices  8.45 us (4%)
    all_to_all x4, blocking collectives, exchange(): return lax.all_to_all(x, axes, split_axis=0, concat_axis=0, tiled=True)  132 us
    all_to_all x1, waiting for transfers between devices, exchange(): return lax.all_to_all(x, axes, split_axis=0, concat_axis=0, tiled=True)  15.8 us
    pallas_call x1, Pallas kernels, body(): pl.pallas_call(middle_kernel, out_shape=(shape((total, width), BF16), sha...  13.3 us
    all_to_all x1, starting transfers between devices, exchange(): return lax.all_to_all(x, axes, split_axis=0, concat_axis=0, tiled=True)  8.33 us
    pallas_call x1, Pallas kernels, body(): pl.pallas_call(backward_kernel, out_shape=shape((tm, 3 * steps, inner), B...  4.23 us
  transfers between devices with their start and end apart: 4, of which 1 were waited for; matrix products, arithmetic and copies ran while one was open for 0% of the time, Pallas kernels for 4%

profile of v4, /device:TPU:8, one launch (start us, length us, event | category | flops | bytes accessed | tf_op | source)
XLA Modules:
  0.0 199.6 jit_solution(11649993177537163620)
XLA Ops:
  7.2 0.0 copy-start
  7.2 0.0 copy-start.1
  7.2 0.0 all-gather.9.cloned.1.call-start
  7.2 2.2 %first.1 = (bf16[16,40,768]{2,1,0:T(8,128)(2,1)}, bf16[8,16,2048]{2,1,0:T(8,128)(2,1)}) custom-call(bf16[6,1024]{1,0:T(8,128)(2,1)} %fc_hbm.1, bf16[6,1024]{1,0:T(8,128)(2,1)} %out_hbm.1, bf16[8,2304]{1,0:T(8,128)(2,1)} %qkv_hbm.1, bf16[1,8,16,1024]{3,2,1,0:T(8,128)(2,1)} %res_hbm.1, bf16[1,8,16,1024]{3,2,1,0:T(8,128)(2,1)} %cot_hbm.1), custom_call_target="tpu_custom_call" | custom-call | tf_op jit(solution)/shard_map/first/pallas_call | solution.py:332
  9.5 0.0 all-gather.9.cloned.1.call-update
  9.5 0.0 all-gather.7.cloned.1.call-start
  9.6 46.1 %all_to_all.25.x_ref = bf16[16,40,768]{2,1,0:T(8,128)(2,1)S(1)} all-to-all(bf16[16,40,768]{2,1,0:T(8,128)(2,1)} %get-tuple-element.15), channel_id=1, replica_groups=mesh['tm'=16,'space'=8,'dp'=4] {'tm'}, dimensions={0} | all-to-all | bytes 1966080 | tf_op jit(solution)/shard_map/all_to_all | solution.py:322
  55.7 0.0 copy-start.5
  55.7 1.4 weights_unpack.1
  57.1 0.0 all-gather.7.cloned.1.call-update
  57.2 0.3 pack.1
  57.5 26.9 %all_to_all.26.x_ref = bf16[16,24,768]{2,1,0:T(8,128)(2,1)} all-to-all(bf16[16,24,768]{2,1,0:T(8,128)(2,1)S(1)} %pack.1), channel_id=1, replica_groups=mesh['tm'=16,'space'=8,'dp'=4] {'tm'}, dimensions={0} | all-to-all | bytes 1179648 | tf_op jit(solution)/shard_map/all_to_all | solution.py:322
  84.4 2.9 %temporal_forward.1 = (bf16[128,6,128]{2,1,0:T(8,128)(2,1)}, f32[6,128,256]{2,1,0:T(8,128)}) custom-call(bf16[16,24,768]{2,1,0:T(8,128)(2,1)} %all_to_all.26.x_ref), custom_call_target="tpu_custom_call" | custom-call | flops 100000000 | bytes 2000000 | tf_op jit(solution)/shard_map/temporal_forward/pallas_call | solution.py:372
  87.4 8.3 %all-to-all-start.2 = ((bf16[128,6,128]{2,1,0:T(8,128)(2,1)}), bf16[128,6,128]{2,1,0:T(8,128)(2,1)S(1)}, u32[]{:S(2)}, u32[]{:S(2)}) async-start(bf16[128,6,128]{2,1,0:T(8,128)(2,1)} %get-tuple-element.18), calls=%async_computation.2 | async-start | bytes 524288 | tf_op jit(solution)/shard_map/all_to_all | solution.py:322
  95.7 0.0 all-gather.11.cloned.1.call-start
  95.8 0.7 copy.23.row_ref
  96.5 15.8 %all-to-all-done.2.x_ref = bf16[128,6,128]{2,1,0:T(8,128)(2,1)S(1)} async-done(((bf16[128,6,128]{2,1,0:T(8,128)(2,1)}), bf16[128,6,128]{2,1,0:T(8,128)(2,1)S(1)}, u32[]{:S(2)}, u32[]{:S(2)}) %all-to-all-start.2) | async-done | bytes 196640 | tf_op jit(solution)/shard_map/all_to_all | solution.py:322
  112.3 0.7 copy-done.6
  113.0 13.3 %middle.1 = (bf16[128,1024]{1,0:T(8,128)(2,1)}, bf16[128,6,128]{2,1,0:T(8,128)(2,1)}) custom-call(s32[1]{0:T(128)} %bitcast.me_ref, bf16[8,640,768]{2,1,0:T(8,128)(2,1)} %bitcast.6, bf16[128,6,128]{2,1,0:T(8,128)(2,1)} %copy-done.6, bf16[8,8,16,2048]{3,2,1,0:T(8,128)(2,1)} %bitcast.7, f32[1,1024]{1,0:T(1,128)} %bitcast.9, f32[12]{0:T(128)} %slope_ref.1, ...), custom_call_target="tpu_custom_call" | custom-call | flops 4000000000 | bytes 10000000 | tf_op jit(solution)/shard_map/middle/pallas_call | solution.py:384
  126.3 0.0 all-gather.11.cloned.1.call-update
  126.4 30.5 %all_to_all.27.g_ref = bf16[128,6,128]{2,1,0:T(8,128)(2,1)} all-to-all(bf16[128,6,128]{2,1,0:T(8,128)(2,1)} %get-tuple-element.20), channel_id=1, replica_groups=mesh['tm'=16,'space'=8,'dp'=4] {'tm','space'}, dimensions={0} | all-to-all | bytes 393216 | tf_op jit(solution)/shard_map/all_to_all | solution.py:322
  156.8 4.2 %temporal_backward.1 = bf16[16,24,768]{2,1,0:T(8,128)(2,1)} custom-call(bf16[16,24,768]{2,1,0:T(8,128)(2,1)} %all_to_all.26.x_ref, f32[6,128,256]{2,1,0:T(8,128)} %get-tuple-element.17.p_ref, bf16[128,6,128]{2,1,0:T(8,128)(2,1)} %all_to_all.27.g_ref), custom_call_target="tpu_custom_call" | custom-call | flops 300000000 | bytes 2000000 | tf_op jit(solution)/shard_map/temporal_backward/pallas_call | solution.py:420
  161.1 29.0 %all_to_all.28.x_ref = bf16[16,24,768]{2,1,0:T(8,128)(2,1)} all-to-all(bf16[16,24,768]{2,1,0:T(8,128)(2,1)} %temporal_backward.1), channel_id=1, replica_groups=mesh['tm'=16,'space'=8,'dp'=4] {'tm'}, dimensions={0} | all-to-all | bytes 1179648 | tf_op jit(solution)/shard_map/all_to_all | solution.py:322
  190.1 2.9 %unpack.1 = (bf16[1,8,16,768]{3,2,1,0:T(8,128)(2,1)}, bf16[1,8,16,768]{3,2,1,0:T(8,128)(2,1)}, bf16[1,8,16,768]{3,2,1,0:T(8,128)(2,1)}, bf16[1,8,16,1024]{3,2,1,0:T(8,128)(2,1)}) custom-call(s32[1]{0:T(128)} %bitcast.me_ref, bf16[16,24,768]{2,1,0:T(8,128)(2,1)} %all_to_all.28.x_ref, bf16[128,128]{1,0:T(8,128)(2,1)} %constant.19.clone.turn_ref, ...), custom_call_target="tpu_custom_call" | custom-call | tf_op jit(solution)/shard_map/unpack/pallas_call | solution.py:431
  (15 shorter events, 0.0 us)
Async XLA Ops:
  7.2 48.5 %copy-start = (bf16[3,3,64,256]{3,2,1,0:T(8,128)(2,1)S(1)}, bf16[3,3,64,256]{3,2,1,0:T(8,128)(2,1)}, u32[]{:S(2)}) copy-start(bf16[3,3,64,256]{3,2,1,0:T(8,128)(2,1)} %constant.21.clone.rest_ref) | copy-start | bytes 884740
  7.2 48.5 %copy-start.1 = (bf16[192,256]{1,0:T(8,128)(2,1)S(1)}, bf16[192,256]{1,0:T(8,128)(2,1)}, u32[]{:S(2)}) copy-start(bf16[192,256]{1,0:T(8,128)(2,1)} %constant.20.clone.main_ref) | copy-start | bytes 294916
  7.2 105.1 %all-gather.9.cloned.1.call-start = ((), (), s32[]{:S(2)}) async-start(), calls=%async_computation.6 | async-start | bytes 4718592 | tf_op jit(solution)/shard_map/all_gather | solution.py:346
  9.5 102.8 %all-gather.7.cloned.1.call-start = ((), (), s32[]{:S(2)}) async-start(), calls=%async_computation.5 | async-start | bytes 8847360 | tf_op jit(solution)/shard_map/all_gather | solution.py:367
  55.7 1.5 copy-start.2
  55.7 1.5 copy-start.3
  55.7 1.5 copy-start.4
  55.7 1.5 copy-start.5
  57.2 38.6 %copy-start.7 = (s32[1,128]{1,0:T(1,128)S(1)}, s32[1,128]{1,0:T(1,128)}, u32[]{:S(2)}) copy-start(s32[1,128]{1,0:T(1,128)} %col_ref.1) | copy-start | bytes 1540
  87.4 24.9 %all-to-all-start.2 = ((bf16[128,6,128]{2,1,0:T(8,128)(2,1)}), bf16[128,6,128]{2,1,0:T(8,128)(2,1)S(1)}, u32[]{:S(2)}, u32[]{:S(2)}) async-start(bf16[128,6,128]{2,1,0:T(8,128)(2,1)} %get-tuple-element.18), calls=%async_computation.2 | async-start | bytes 524288 | tf_op jit(solution)/shard_map/all_to_all | solution.py:322
  95.7 94.4 %all-gather.11.cloned.1.call-start = ((), (), s32[]{:S(2)}) async-start(), calls=%async_computation.7 | async-start | bytes 2359296 | tf_op jit(solution)/shard_map/all_gather | solution.py:417
  112.3 0.7 copy-start.6
Sparse Core Ops, SparseCore 0:
  10.2 41.9 all-gather.8
  57.3 51.5 all-gather.6
  126.5 29.1 all-gather.10

commit v5 on v4

--- a/solution.py
+++ b/solution.py
@@ -43,23 +43,38 @@
 
 def gathered_order(tm, sp, rows):
     size = tm * sp * rows
-    m = np.zeros((size, size), np.float32)
-    a, b, r = (v.ravel() for v in np.meshgrid(*map(np.arange, (tm, sp, rows)), indexing="ij"))
-    m[(a * sp + b) * rows + r, (b * tm + a) * rows + r] = 1
-    return m.astype(BF16)
-
-
-def shard_order(tm):
-    main = np.zeros((12 * tm, 16 * tm), np.float32)
-    rest = np.zeros((3, 3, 4 * tm, 16 * tm), np.float32)
+    at = lax.broadcasted_iota(jnp.int32, (size, 1), 0)
+    block = (at * (65536 // rows + 1)) >> 16
+    a = (block * (65536 // sp + 1)) >> 16
+    to = ((block - a * sp) * tm + a) * rows + at - block * rows
+    column = lax.broadcasted_iota(jnp.int32, (size, size), 1)
+    return jnp.where(column == to, 1.0, 0.0).astype(BF16)
+
+
+def sixth(n):
+    return (n * 10923) >> 16
+
+
+def main_order(tm):
+    at = lax.broadcasted_iota(jnp.int32, (12 * tm, 1), 0)
+    which = jnp.where(at >= 6 * tm, 1, 0)
+    n = at - which * 6 * tm
+    a = sixth(n)
+    source = a * 16 + which * 6 + n - a * 6
+    column = lax.broadcasted_iota(jnp.int32, (12 * tm, 16 * tm), 1)
+    return jnp.where(column == source, 1.0, 0.0).astype(BF16)
+
+
+def rest_order(tm, to, src):
     third = 2 * tm
-    for which in range(2):
-        for n in range(6 * tm):
-            a, r = divmod(n, 6)
-            g = which * 6 + r
-            main[which * 6 * tm + n, a * 16 + g] = 1
-            rest[n // third, g // 4, which * third + n % third, a * 16 + 12 + g % 4] = 1
-    return main.astype(BF16), rest.astype(BF16)
+    at = lax.broadcasted_iota(jnp.int32, (2 * third, 1), 0)
+    which = jnp.where(at >= third, 1, 0)
+    n = at - which * third + to * third
+    a = sixth(n)
+    g = which * 6 + n - a * 6
+    source = jnp.where((g >> 2) == src, a * 16 + 12 + (g & 3), -1)
+    column = lax.broadcasted_iota(jnp.int32, (2 * third, 16 * tm), 1)
+    return jnp.where(column == source, 1.0, 0.0).astype(BF16)
 
 
 def first_kernel(fc_hbm, out_hbm, qkv_hbm, res_hbm, cot_hbm, o_ref, rest_ref, fc_ref, out_ref, qkv_ref, sem):
@@ -87,18 +102,18 @@
         c.wait()
 
 
-def weights_unpack_kernel(x_ref, main_ref, rest_ref, o_ref):
+def weights_unpack_kernel(x_ref, o_ref):
     tm = x_ref.shape[0]
     x = x_ref[...].astype(F32)
     fo = x[:, 0:16].reshape(16 * tm, 768).astype(BF16)
     n = 8 * tm
     for j in range(3):
         o_ref[pl.ds(j * n, n), :] = x[:, 16 + 8 * j : 24 + 8 * j].reshape(n, 768).astype(BF16)
-    o_ref[pl.ds(3 * n, 12 * tm), :] = nn(main_ref[...], fo).astype(BF16)
+    o_ref[pl.ds(3 * n, 12 * tm), :] = nn(main_order(tm), fo).astype(BF16)
     for j in range(3):
-        part = nn(rest_ref[j, 0], fo[:, :256])
-        part += nn(rest_ref[j, 1], fo[:, 256:512])
-        part += nn(rest_ref[j, 2], fo[:, 512:])
+        part = nn(rest_order(tm, j, 0), fo[:, :256])
+        part += nn(rest_order(tm, j, 1), fo[:, 256:512])
+        part += nn(rest_order(tm, j, 2), fo[:, 512:])
         o_ref[pl.ds(3 * n + 12 * tm, 4 * tm), pl.ds(j * 256, 256)] = part.astype(BF16)
 
 
@@ -112,18 +127,20 @@
     o_ref[...] = jnp.concatenate(parts, axis=1).astype(BF16)
 
 
-def unpack_kernel(me_ref, x_ref, turn_ref, gr_hbm, *refs):
-    outs, gr_out, sem = refs[:3], refs[3], refs[4]
-    mine = outs[0].shape[2]
+def slice_kernel(me_ref, gr_hbm, o_ref, sem):
+    mine = o_ref.shape[2]
     at = pl.multiple_of(me_ref[0] * mine, mine)
-    copy = pltpu.make_async_copy(gr_hbm.at[:, pl.ds(at, mine), :], gr_out.at[0], sem)
+    copy = pltpu.make_async_copy(gr_hbm.at[:, pl.ds(at, mine), :], o_ref.at[0], sem)
     copy.start()
+    copy.wait()
+
+
+def unpack_kernel(x_ref, turn_ref, *outs):
     x = x_ref[...].astype(F32)
     tubes, steps = x.shape[0], x.shape[1] // 3
     for j, o_ref in enumerate(outs):
         part = x[:, j * steps : (j + 1) * steps].reshape(tubes * steps, -1).astype(BF16)
         o_ref[0] = nn(turn_ref[...], part).astype(BF16).reshape(steps, tubes, -1)
-    copy.wait()
 
 
 def lane_masks(rows):
@@ -170,7 +187,7 @@
     ]
 
 
-def forward_kernel(x_ref, o_ref, p_ref, turned):
+def forward_kernel(x_ref, o_ref, turned):
     x = x_ref[...].astype(F32)
     q, k, v = qkv_of(x, x.shape[1] // 3)
     n = q.shape[0]
@@ -178,14 +195,12 @@
     for h in range(HEADS // 2):
         at = slice(h * 128, (h + 1) * 128)
         p0, p1 = pair_probs(q[:, at], stacked(k[:, at], first))
-        p_ref[h, :, 0:n] = p0
-        p_ref[h, :, n : 2 * n] = p1
         both = jnp.concatenate([p0.astype(BF16), p1.astype(BF16)], axis=1)
         turned[:, h, :] = nn(both, stacked(v[:, at], first))
     o_ref[...] = turned[...].astype(BF16)
 
 
-def backward_kernel(x_ref, p_ref, g_ref, o_ref, turned):
+def backward_kernel(x_ref, g_ref, o_ref, turned):
     x = x_ref[...].astype(F32)
     steps = x.shape[1] // 3
     q, k, v = qkv_of(x, steps)
@@ -194,9 +209,10 @@
     first = lane_masks(n)
     for h in range(HEADS // 2):
         at = slice(h * 128, (h + 1) * 128)
+        p0, p1 = pair_probs(q[:, at], stacked(k[:, at], first))
         grads = pair_backward(
-            p_ref[h, :, 0:n],
-            p_ref[h, :, n : 2 * n],
+            p0,
+            p1,
             q[:, at],
             k[:, at],
             v[:, at],
@@ -208,7 +224,7 @@
 
 
 def middle_kernel(
-    me_ref, w_hbm, x_ref, rest_hbm, gain_ref, slope_ref, row_ref, col_ref, turn_ref, inner_hbm, width_hbm,
+    me_ref, w_hbm, x_ref, rest_hbm, gain_ref, slope_ref, row_ref, col_ref, turn_ref,
     gr_ref, gt_ref, rest_v, inner_ref, width_v, qkv_v, fc_v, out_v, turned, proj, joined, sem,
 ):
     sp = w_hbm.shape[0]
@@ -220,7 +236,6 @@
         copies.append(pltpu.make_async_copy(src, dst, sem.at[len(copies)]))
         copies[-1].start()
 
-    load(inner_hbm, inner_ref)
     load(rest_hbm.at[:, me_ref[0]], rest_v)
     at = 3 * n
     for dst, base, tail in (
@@ -233,7 +248,6 @@
                 w_hbm.at[:, pl.ds(tail, third), pl.ds(j * 256, 256)],
                 dst.at[:, pl.ds(j * third, third), pl.ds(768, 256)],
             )
-    load(width_hbm, width_v)
     for j in range(3):
         load(w_hbm.at[:, pl.ds(j * n, n), :], qkv_v.at[:, :, pl.ds(j * 768, 768)])
 
@@ -249,9 +263,11 @@
     mixed = jnp.concatenate([turned[:, h, :] for h in range(6)], axis=1).astype(BF16)
     mixed = nn(turn, mixed).astype(BF16)
 
-    for c in copies[:6]:
+    inner_ref[...] = gathered_order(tm, sp, 6)
+    width_v[...] = gathered_order(tm, sp, 8)
+    mixed = nn(mixed, inner_ref[...]).astype(BF16)
+    for c in copies[:5]:
         c.wait()
-    mixed = nn(mixed, inner_ref[...]).astype(BF16)
     rest = rest_v[...].reshape(tokens, 2 * width)
     cot = rest[:, width:]
     fc = fc_v[...].reshape(inner, width)
@@ -261,13 +277,13 @@
     normed = centred * inv_std
     normed_in = (normed * gain).astype(BF16)
 
-    for c in copies[6:11]:
+    for c in copies[5:9]:
         c.wait()
     normed_in = nn(normed_in, width_v[...]).astype(BF16)
     grad_mixed = nt(cot, out_v[...].reshape(inner, width)).astype(BF16)
     grad_mixed = nt(grad_mixed, inner_ref[...]).astype(BF16)
 
-    for c in copies[11:]:
+    for c in copies[9:]:
         c.wait()
     qkv = qkv_v[...].reshape(width, 3 * inner)
     proj[...] = nn(normed_in, qkv).astype(BF16)
@@ -324,10 +340,6 @@
     to_tubes = jnp.asarray(transposed_rows(steps, tubes))
     to_steps = jnp.asarray(transposed_rows(tubes, steps))
     to_order = jnp.asarray(transposed_rows(tm, sp))
-    main_map, rest_map = map(jnp.asarray, shard_order(tm))
-    inner_map = jnp.asarray(gathered_order(tm, sp, fc_weight.shape[0]))
-    width_map = jnp.asarray(gathered_order(tm, sp, qkv_weight.shape[0]))
-
     me = lax.axis_index("space").astype(jnp.int32).reshape(1)
     shards, rest = pl.pallas_call(
         first_kernel,
@@ -359,23 +371,23 @@
     shards = pl.pallas_call(
         weights_unpack_kernel,
         out_shape=shape((40 * tm, inner), BF16),
-        in_specs=[VMEM] * 3,
+        in_specs=[VMEM],
         out_specs=VMEM,
         compiler_params=params(24),
         name="weights_unpack",
-    )(shards, main_map, rest_map)
+    )(shards)
     weights = lax.all_gather(shards, "space", axis=0)
 
     send, shards = lax.optimization_barrier((send, shards))
     got = exchange(send, "tm")
 
-    mixed, probs = pl.pallas_call(
+    mixed = pl.pallas_call(
         forward_kernel,
-        out_shape=(shape((total, 6, 128), BF16), shape((HEADS // 2, total, 2 * total), F32)),
+        out_shape=shape((total, 6, 128), BF16),
         in_specs=[VMEM],
-        out_specs=(VMEM, VMEM),
+        out_specs=VMEM,
         scratch_shapes=[pltpu.VMEM((total, 6, 128), F32)],
-        compiler_params=params(56),
+        compiler_params=params(24),
         cost_estimate=pl.CostEstimate(flops=10**8, bytes_accessed=2 * 10**6, transcendentals=2 * 10**5),
         name="temporal_forward",
     )(got)
@@ -384,7 +396,7 @@
     grad_resid, grad_time = pl.pallas_call(
         middle_kernel,
         out_shape=(shape((total, width), BF16), shape((total, 6, 128), BF16)),
-        in_specs=[SMEM, HBM, VMEM, HBM, VMEM, SMEM, VMEM, VMEM, VMEM, HBM, HBM],
+        in_specs=[SMEM, HBM, VMEM, HBM, VMEM, SMEM, VMEM, VMEM, VMEM],
         out_specs=(VMEM, VMEM),
         scratch_shapes=[
             pltpu.VMEM((sp, tubes, 2 * width), BF16),
@@ -396,7 +408,7 @@
             pltpu.VMEM((total, 6, 128), F32),
             pltpu.VMEM((total, 3 * inner), BF16),
             pltpu.VMEM((total, 3 * inner), BF16),
-            pltpu.SemaphoreType.DMA((14,)),
+            pltpu.SemaphoreType.DMA((12,)),
         ],
         compiler_params=params(56),
         cost_estimate=pl.CostEstimate(flops=4 * 10**9, bytes_accessed=10**7, transcendentals=2 * 10**5),
@@ -411,8 +423,6 @@
         visible.reshape(total, 1),
         visible.reshape(1, total),
         to_order,
-        inner_map,
-        width_map,
     )
     grad_resid = lax.all_gather(grad_resid, "space", axis=0)
     grad_time = exchange(grad_time, both)
@@ -420,24 +430,34 @@
     back = pl.pallas_call(
         backward_kernel,
         out_shape=shape((tm, 3 * steps, inner), BF16),
-        in_specs=[VMEM] * 3,
+        in_specs=[VMEM] * 2,
         out_specs=VMEM,
         scratch_shapes=[pltpu.VMEM((total, 6, 128), F32)],
-        compiler_params=params(56),
+        compiler_params=params(24),
         cost_estimate=pl.CostEstimate(flops=3 * 10**8, bytes_accessed=2 * 10**6, transcendentals=0),
         name="temporal_backward",
-    )(got, probs, grad_time)
+    )(got, grad_time)
+    back, grad_resid = lax.optimization_barrier((back, grad_resid))
     back = exchange(back, "tm")
     outs = pl.pallas_call(
         unpack_kernel,
-        out_shape=(shape(time_query.shape, BF16),) * 3 + (shape(residual_in.shape, BF16),),
-        in_specs=[SMEM, VMEM, VMEM, HBM],
-        out_specs=(VMEM, VMEM, VMEM, VMEM),
+        out_shape=(shape(time_query.shape, BF16),) * 3,
+        in_specs=[VMEM, VMEM],
+        out_specs=(VMEM,) * 3,
+        compiler_params=params(24),
+        name="unpack",
+    )(back, to_steps)
+    grad_resid = pl.pallas_call(
+        slice_kernel,
+        out_shape=shape(residual_in.shape, BF16),
+        in_specs=[SMEM, HBM],
+        out_specs=VMEM,
         scratch_shapes=[pltpu.SemaphoreType.DMA],
         compiler_params=params(56),
-        name="unpack",
-    )(me, back, to_steps, grad_resid)
-    return (outs[3], *outs[:3])
+        cost_estimate=pl.CostEstimate(flops=10**9, bytes_accessed=4 * 10**6, transcendentals=0),
+        name="slice",
+    )(me, grad_resid)
+    return (grad_resid, *outs)
 
 
 def solution(mesh):

time: 200 us -> 198 us (0.990)
  blocking collectives: 132 us -> 105 us
  waiting for transfers between devices: 15.9 us -> 37.1 us
  starting transfers between devices: 8.45 us -> 15.3 us
  Pallas kernels: 27.4 us -> 25 us
    all_to_all x4 -> x3, blocking collectives: 132 us -> 105 us  [exchange(): return lax.all_to_all(x, axes, split_axis=0, concat_axis=0, tiled=True)]
    all_to_all x1 -> x2, waiting for transfers between devices: 15.8 us -> 37.1 us  [exchange(): return lax.all_to_all(x, axes, split_axis=0, concat_axis=0, tiled=True)]
    all_to_all x1 -> x2, starting transfers between devices: 8.33 us -> 15.2 us  [exchange(): return lax.all_to_all(x, axes, split_axis=0, concat_axis=0, tiled=True)]
  transfers between devices with their start and end apart: 4 -> 5, of which waited for: 1 -> 2; matrix products, arithmetic and copies ran while one was open for 0% -> 0% of each run, Pallas kernels for 4% -> 5%
where the time goes in v5:
time: 198 us; the launch traced here: 197 us
  blocking collectives  105 us (53%)
  waiting for transfers between devices  37.1 us (19%)
  Pallas kernels  25 us (13%)
  starting transfers between devices  15.3 us (8%)
  between operations  13.9 us (7%)
    all_to_all x3, blocking collectives, exchange(): return lax.all_to_all(x, axes, split_axis=0, concat_axis=0, tiled=True)  105 us
    all_to_all x2, waiting for transfers between devices, exchange(): return lax.all_to_all(x, axes, split_axis=0, concat_axis=0, tiled=True)  37.1 us
    all_to_all x2, starting transfers between devices, exchange(): return lax.all_to_all(x, axes, split_axis=0, concat_axis=0, tiled=True)  15.2 us
    pallas_call x1, Pallas kernels, body(): pl.pallas_call(middle_kernel, out_shape=(shape((total, width), BF16), sha...  12.5 us
  transfers between devices with their start and end apart: 5, of which 2 were waited for; matrix products, arithmetic and copies ran while one was open for 0% of the time, Pallas kernels for 5%

profile of v5, /device:TPU:8, one launch (start us, length us, event | category | flops | bytes accessed | tf_op | source)
XLA Modules:
  0.0 197.3 jit_solution(7693883283812507144)
XLA Ops:
  7.2 0.0 copy-start.4
  7.2 0.0 all-gather.9.cloned.1.call-start
  7.3 2.4 %first.1 = (bf16[16,40,768]{2,1,0:T(8,128)(2,1)}, bf16[8,16,2048]{2,1,0:T(8,128)(2,1)}) custom-call(bf16[6,1024]{1,0:T(8,128)(2,1)} %fc_hbm.1, bf16[6,1024]{1,0:T(8,128)(2,1)} %out_hbm.1, bf16[8,2304]{1,0:T(8,128)(2,1)} %qkv_hbm.1, bf16[1,8,16,1024]{3,2,1,0:T(8,128)(2,1)} %res_hbm.1, bf16[1,8,16,1024]{3,2,1,0:T(8,128)(2,1)} %cot_hbm.1), custom_call_target="tpu_custom_call" | custom-call | tf_op jit(solution)/shard_map/first/pallas_call | solution.py:344
  9.6 0.0 all-gather.9.cloned.1.call-update
  9.7 0.0 all-gather.7.cloned.1.call-start
  9.7 46.1 %all_to_all.25.x_ref = bf16[16,40,768]{2,1,0:T(8,128)(2,1)S(1)} all-to-all(bf16[16,40,768]{2,1,0:T(8,128)(2,1)} %get-tuple-element.14), channel_id=1, replica_groups=mesh['tm'=16,'space'=8,'dp'=4] {'tm'}, dimensions={0} | all-to-all | bytes 1966080 | tf_op jit(solution)/shard_map/all_to_all | solution.py:338
  55.8 1.4 weights_unpack.1
  57.3 0.0 all-gather.7.cloned.1.call-update
  57.3 0.3 pack.1
  57.6 26.8 %all_to_all.26.x_ref = bf16[16,24,768]{2,1,0:T(8,128)(2,1)S(1)} all-to-all(bf16[16,24,768]{2,1,0:T(8,128)(2,1)S(1)} %pack.1), channel_id=1, replica_groups=mesh['tm'=16,'space'=8,'dp'=4] {'tm'}, dimensions={0} | all-to-all | bytes 1179648 | tf_op jit(solution)/shard_map/all_to_all | solution.py:338
  84.4 1.8 temporal_forward.1
  86.3 8.3 %all-to-all-start.2 = ((bf16[128,6,128]{2,1,0:T(8,128)(2,1)}), bf16[128,6,128]{2,1,0:T(8,128)(2,1)S(1)}, u32[]{:S(2)}, u32[]{:S(2)}) async-start(bf16[128,6,128]{2,1,0:T(8,128)(2,1)} %temporal_forward.1), calls=%async_computation.2 | async-start | bytes 524288 | tf_op jit(solution)/shard_map/all_to_all | solution.py:338
  94.6 0.0 all-gather.11.cloned.1.call-start
  94.6 0.7 copy.19.row_ref
  95.4 15.8 %all-to-all-done.2.x_ref = bf16[128,6,128]{2,1,0:T(8,128)(2,1)S(1)} async-done(((bf16[128,6,128]{2,1,0:T(8,128)(2,1)}), bf16[128,6,128]{2,1,0:T(8,128)(2,1)S(1)}, u32[]{:S(2)}, u32[]{:S(2)}) %all-to-all-start.2) | async-done | bytes 196640 | tf_op jit(solution)/shard_map/all_to_all | solution.py:338
  111.2 0.7 copy-done.5
  111.9 12.5 %middle.1 = (bf16[128,1024]{1,0:T(8,128)(2,1)}, bf16[128,6,128]{2,1,0:T(8,128)(2,1)}) custom-call(s32[1]{0:T(128)} %bitcast.me_ref, bf16[8,640,768]{2,1,0:T(8,128)(2,1)} %bitcast.7, bf16[128,6,128]{2,1,0:T(8,128)(2,1)} %copy-done.5, bf16[8,8,16,2048]{3,2,1,0:T(8,128)(2,1)} %bitcast.8, f32[1,1024]{1,0:T(1,128)} %bitcast.10, f32[12]{0:T(128)} %slope_ref.1, ...), custom_call_target="tpu_custom_call" | custom-call | flops 4000000000 | bytes 10000000 | tf_op jit(solution)/shard_map/middle/pallas_call | solution.py:396
  124.4 0.0 all-gather.11.cloned.1.call-update
  124.4 31.7 %all_to_all.27.g_ref = bf16[128,6,128]{2,1,0:T(8,128)(2,1)S(1)} all-to-all(bf16[128,6,128]{2,1,0:T(8,128)(2,1)} %get-tuple-element.17), channel_id=1, replica_groups=mesh['tm'=16,'space'=8,'dp'=4] {'tm','space'}, dimensions={0} | all-to-all | bytes 393216 | tf_op jit(solution)/shard_map/all_to_all | solution.py:338
  156.1 3.8 %temporal_backward.1 = bf16[16,24,768]{2,1,0:T(8,128)(2,1)} custom-call(bf16[16,24,768]{2,1,0:T(8,128)(2,1)S(1)} %all_to_all.26.x_ref, bf16[128,6,128]{2,1,0:T(8,128)(2,1)S(1)} %all_to_all.27.g_ref), custom_call_target="tpu_custom_call" | custom-call | flops 300000000 | bytes 2000000 | tf_op jit(solution)/shard_map/temporal_backward/pallas_call | solution.py:430
  160.0 6.8 %all-to-all-start.4 = ((bf16[16,24,768]{2,1,0:T(8,128)(2,1)}), bf16[16,24,768]{2,1,0:T(8,128)(2,1)S(1)}, u32[]{:S(2)}, u32[]{:S(2)}) async-start(bf16[16,24,768]{2,1,0:T(8,128)(2,1)} %temporal_backward.1), calls=%async_computation.4 | async-start | bytes 1179648 | tf_op jit(solution)/shard_map/all_to_all | solution.py:338
  166.8 1.7 slice.1
  168.5 21.3 %all-to-all-done.4.x_ref = bf16[16,24,768]{2,1,0:T(8,128)(2,1)S(1)} async-done(((bf16[16,24,768]{2,1,0:T(8,128)(2,1)}), bf16[16,24,768]{2,1,0:T(8,128)(2,1)S(1)}, u32[]{:S(2)}, u32[]{:S(2)}) %all-to-all-start.4) | async-done | bytes 589856 | tf_op jit(solution)/shard_map/all_to_all | solution.py:338
  189.8 1.0 unpack.1
  (15 shorter events, 0.0 us)
Async XLA Ops:
  7.2 50.1 %copy-start.4 = (bf16[128,128]{1,0:T(8,128)(2,1)S(1)}, bf16[128,128]{1,0:T(8,128)(2,1)}, u32[]{:S(2)}) copy-start(bf16[128,128]{1,0:T(8,128)(2,1)} %constant.10.clone.turn_ref) | copy-start | bytes 98308
  7.2 50.1 %copy-start.1 = (bf16[1,8,16,768]{3,2,1,0:T(8,128)(2,1)S(1)}, bf16[1,8,16,768]{3,2,1,0:T(8,128)(2,1)}, u32[]{:S(2)}) copy-start(bf16[1,8,16,768]{3,2,1,0:T(8,128)(2,1)} %q_ref.1) | copy-start | bytes 589828
  7.2 50.1 %copy-start.2 = (bf16[1,8,16,768]{3,2,1,0:T(8,128)(2,1)S(1)}, bf16[1,8,16,768]{3,2,1,0:T(8,128)(2,1)}, u32[]{:S(2)}) copy-start(bf16[1,8,16,768]{3,2,1,0:T(8,128)(2,1)} %k_ref.1) | copy-start | bytes 589828
  7.2 50.1 %copy-start.3 = (bf16[1,8,16,768]{3,2,1,0:T(8,128)(2,1)S(1)}, bf16[1,8,16,768]{3,2,1,0:T(8,128)(2,1)}, u32[]{:S(2)}) copy-start(bf16[1,8,16,768]{3,2,1,0:T(8,128)(2,1)} %v_ref.1) | copy-start | bytes 589828
  7.2 104.0 %all-gather.9.cloned.1.call-start = ((), (), s32[]{:S(2)}) async-start(), calls=%async_computation.6 | async-start | bytes 4718592 | tf_op jit(solution)/shard_map/all_gather | solution.py:358
  9.7 101.5 %all-gather.7.cloned.1.call-start = ((), (), s32[]{:S(2)}) async-start(), calls=%async_computation.5 | async-start | bytes 8847360 | tf_op jit(solution)/shard_map/all_gather | solution.py:379
  55.8 38.8 %copy-start.6 = (s32[1,128]{1,0:T(1,128)S(1)}, s32[1,128]{1,0:T(1,128)}, u32[]{:S(2)}) copy-start(s32[1,128]{1,0:T(1,128)} %col_ref.1) | copy-start | bytes 1540
  86.3 24.9 %all-to-all-start.2 = ((bf16[128,6,128]{2,1,0:T(8,128)(2,1)}), bf16[128,6,128]{2,1,0:T(8,128)(2,1)S(1)}, u32[]{:S(2)}, u32[]{:S(2)}) async-start(bf16[128,6,128]{2,1,0:T(8,128)(2,1)} %temporal_forward.1), calls=%async_computation.2 | async-start | bytes 524288 | tf_op jit(solution)/shard_map/all_to_all | solution.py:338
  94.6 65.4 %all-gather.11.cloned.1.call-start = ((), (), s32[]{:S(2)}) async-start(), calls=%async_computation.7 | async-start | bytes 2359296 | tf_op jit(solution)/shard_map/all_gather | solution.py:427
  111.2 0.7 copy-start.5
  124.4 65.4 %copy-start = (bf16[128,128]{1,0:T(8,128)(2,1)S(1)}, bf16[128,128]{1,0:T(8,128)(2,1)}, u32[]{:S(2)}) copy-start(bf16[128,128]{1,0:T(8,128)(2,1)} %constant.11.clone.turn_ref) | copy-start | bytes 98308
  160.0 29.8 %all-to-all-start.4 = ((bf16[16,24,768]{2,1,0:T(8,128)(2,1)}), bf16[16,24,768]{2,1,0:T(8,128)(2,1)S(1)}, u32[]{:S(2)}, u32[]{:S(2)}) async-start(bf16[16,24,768]{2,1,0:T(8,128)(2,1)} %temporal_backward.1), calls=%async_computation.4 | async-start | bytes 1179648 | tf_op jit(solution)/shard_map/all_to_all | solution.py:338
Sparse Core Ops, SparseCore 0:
  10.2 41.9 all-gather.8
  57.4 51.7 all-gather.6
  124.6 30.1 all-gather.10

commit v6 on v5

--- a/solution.py
+++ b/solution.py
@@ -77,18 +77,26 @@
     return jnp.where(column == source, 1.0, 0.0).astype(BF16)
 
 
-def first_kernel(fc_hbm, out_hbm, qkv_hbm, res_hbm, cot_hbm, o_ref, rest_ref, fc_ref, out_ref, qkv_ref, sem):
+def first_kernel(me_ref, fc_hbm, out_hbm, qkv_hbm, res_hbm, cot_hbm, o_ref, *refs):
+    pieces, (fc_ref, out_ref, qkv_ref, sem) = refs[:-4], refs[-4:]
     width = res_hbm.shape[-1]
+    n = len(pieces)
     copies = [
-        pltpu.make_async_copy(res_hbm.at[0], rest_ref.at[:, :, pl.ds(0, width)], sem.at[0]),
-        pltpu.make_async_copy(cot_hbm.at[0], rest_ref.at[:, :, pl.ds(width, width)], sem.at[1]),
-        pltpu.make_async_copy(fc_hbm, fc_ref, sem.at[2]),
-        pltpu.make_async_copy(out_hbm, out_ref, sem.at[3]),
-        pltpu.make_async_copy(qkv_hbm, qkv_ref, sem.at[4]),
+        pltpu.make_async_copy(fc_hbm, fc_ref, sem.at[0]),
+        pltpu.make_async_copy(out_hbm, out_ref, sem.at[1]),
+        pltpu.make_async_copy(qkv_hbm, qkv_ref, sem.at[2]),
     ]
+    for k, ref in enumerate(pieces):
+        to = lax.rem(me_ref[0] + k, n)
+        for j, src in enumerate((res_hbm, cot_hbm)):
+            copies.append(
+                pltpu.make_async_copy(
+                    src.at[0, to], ref.at[:, pl.ds(j * width, width)], sem.at[3 + 2 * k + j]
+                )
+            )
     for c in copies:
         c.start()
-    for c in copies[2:]:
+    for c in copies[:3]:
         c.wait()
     both = jnp.concatenate([fc_ref[...].astype(F32), out_ref[...].astype(F32)], axis=0)
     tail = both[:, 768:]
@@ -98,7 +106,7 @@
         [both[:, :768], tail, qkv[:, :768], qkv[:, 768:1536], qkv[:, 1536:]], axis=0
     )
     o_ref[...] = jnp.broadcast_to(block[None], o_ref.shape).astype(BF16)
-    for c in copies[:2]:
+    for c in copies[3:]:
         c.wait()
 
 
@@ -127,12 +135,11 @@
     o_ref[...] = jnp.concatenate(parts, axis=1).astype(BF16)
 
 
-def slice_kernel(me_ref, gr_hbm, o_ref, sem):
-    mine = o_ref.shape[2]
-    at = pl.multiple_of(me_ref[0] * mine, mine)
-    copy = pltpu.make_async_copy(gr_hbm.at[:, pl.ds(at, mine), :], o_ref.at[0], sem)
-    copy.start()
-    copy.wait()
+def assemble_kernel(me_ref, *refs):
+    pieces, o_ref = refs[:-1], refs[-1]
+    n = len(pieces)
+    for k, ref in enumerate(pieces):
+        o_ref[0, lax.rem(me_ref[0] + n - k, n)] = ref[...]
 
 
 def unpack_kernel(x_ref, turn_ref, *outs):
@@ -224,9 +231,11 @@
 
 
 def middle_kernel(
-    me_ref, w_hbm, x_ref, rest_hbm, gain_ref, slope_ref, row_ref, col_ref, turn_ref,
-    gr_ref, gt_ref, rest_v, inner_ref, width_v, qkv_v, fc_v, out_v, turned, proj, joined, sem,
+    me_ref, w_hbm, x_ref, gain_ref, slope_ref, row_ref, col_ref, turn_ref, *refs,
 ):
+    pieces, refs = refs[: w_hbm.shape[0]], refs[w_hbm.shape[0] :]
+    grs, refs = refs[: w_hbm.shape[0]], refs[w_hbm.shape[0] :]
+    (gt_ref, gr_v, rest_v, inner_ref, width_v, qkv_v, fc_v, out_v, turned, proj, joined, sem) = refs
     sp = w_hbm.shape[0]
     tm = w_hbm.shape[1] // 40
     n, third = 8 * tm, 2 * tm
@@ -236,7 +245,8 @@
         copies.append(pltpu.make_async_copy(src, dst, sem.at[len(copies)]))
         copies[-1].start()
 
-    load(rest_hbm.at[:, me_ref[0]], rest_v)
+    for k, p in enumerate(pieces):
+        load(p, rest_v.at[lax.rem(me_ref[0] + sp - k, sp)])
     at = 3 * n
     for dst, base, tail in (
         (fc_v, at, at + 12 * tm),
@@ -266,7 +276,7 @@
     inner_ref[...] = gathered_order(tm, sp, 6)
     width_v[...] = gathered_order(tm, sp, 8)
     mixed = nn(mixed, inner_ref[...]).astype(BF16)
-    for c in copies[:5]:
+    for c in copies[: sp + 4]:
         c.wait()
     rest = rest_v[...].reshape(tokens, 2 * width)
     cot = rest[:, width:]
@@ -277,13 +287,13 @@
     normed = centred * inv_std
     normed_in = (normed * gain).astype(BF16)
 
-    for c in copies[5:9]:
+    for c in copies[sp + 4 : sp + 8]:
         c.wait()
     normed_in = nn(normed_in, width_v[...]).astype(BF16)
     grad_mixed = nt(cot, out_v[...].reshape(inner, width)).astype(BF16)
     grad_mixed = nt(grad_mixed, inner_ref[...]).astype(BF16)
 
-    for c in copies[9:]:
+    for c in copies[sp + 8 :]:
         c.wait()
     qkv = qkv_v[...].reshape(width, 3 * inner)
     proj[...] = nn(normed_in, qkv).astype(BF16)
@@ -305,7 +315,9 @@
     second_mean = jnp.mean(scaled * normed, axis=-1, keepdims=True)
     term = inv_std * (scaled - first_mean - normed * second_mean)
     grad_resid = (cot.astype(F32) + term).astype(BF16)
-    gr_ref[...] = grad_resid
+    gr_v[...] = grad_resid.reshape(gr_v.shape)
+    for k, ref in enumerate(grs):
+        ref[...] = gr_v[lax.rem(me_ref[0] + k, sp)]
     grad_time = nt(grad_resid, fc).astype(BF16)
     grad_time = nt(grad_time, inner_ref[...]).astype(BF16)
     grad_time = tn(turn, grad_time)
@@ -334,6 +346,12 @@
     both = ("tm", "space")
     shape = jax.ShapeDtypeStruct
 
+    def turned_round(parts):
+        return [
+            lax.ppermute(p, "space", [(i, (i + k) % sp) for i in range(sp)]) if k else p
+            for k, p in enumerate(parts)
+        ]
+
     def exchange(x, axes):
         return lax.all_to_all(x, axes, split_axis=0, concat_axis=0, tiled=True)
 
@@ -341,21 +359,21 @@
     to_steps = jnp.asarray(transposed_rows(tubes, steps))
     to_order = jnp.asarray(transposed_rows(tm, sp))
     me = lax.axis_index("space").astype(jnp.int32).reshape(1)
-    shards, rest = pl.pallas_call(
+    shards, *pieces = pl.pallas_call(
         first_kernel,
-        out_shape=(shape((tm, 40, inner), BF16), shape((steps, tubes, 2 * width), BF16)),
-        in_specs=[HBM] * 5,
-        out_specs=(VMEM, VMEM),
+        out_shape=(shape((tm, 40, inner), BF16),) + (shape((tubes, 2 * width), BF16),) * sp,
+        in_specs=[SMEM] + [HBM] * 5,
+        out_specs=(VMEM,) * (sp + 1),
         scratch_shapes=[
             pltpu.VMEM(fc_weight.shape, BF16),
             pltpu.VMEM(out_weight.shape, BF16),
             pltpu.VMEM(qkv_weight.shape, BF16),
-            pltpu.SemaphoreType.DMA((5,)),
+            pltpu.SemaphoreType.DMA((3 + 2 * sp,)),
         ],
         compiler_params=params(56),
         name="first",
-    )(fc_weight, out_weight, qkv_weight, residual_in, cotangent)
-    rest = lax.all_gather(rest, "space", axis=0)
+    )(me, fc_weight, out_weight, qkv_weight, residual_in, cotangent)
+    pieces = turned_round(pieces)
     shards = exchange(shards, "tm")
 
     send = pl.pallas_call(
@@ -393,12 +411,13 @@
     )(got)
     mixed = exchange(mixed, both)
 
-    grad_resid, grad_time = pl.pallas_call(
+    *grs, grad_time = pl.pallas_call(
         middle_kernel,
-        out_shape=(shape((total, width), BF16), shape((total, 6, 128), BF16)),
-        in_specs=[SMEM, HBM, VMEM, HBM, VMEM, SMEM, VMEM, VMEM, VMEM],
-        out_specs=(VMEM, VMEM),
+        out_shape=(shape((tubes, width), BF16),) * sp + (shape((total, 6, 128), BF16),),
+        in_specs=[SMEM, HBM, VMEM, VMEM, SMEM, VMEM, VMEM, VMEM] + [HBM] * sp,
+        out_specs=(VMEM,) * (sp + 1),
         scratch_shapes=[
+            pltpu.VMEM((sp, tubes, width), BF16),
             pltpu.VMEM((sp, tubes, 2 * width), BF16),
             pltpu.VMEM((inner, inner), BF16),
             pltpu.VMEM((width, width), BF16),
@@ -408,7 +427,7 @@
             pltpu.VMEM((total, 6, 128), F32),
             pltpu.VMEM((total, 3 * inner), BF16),
             pltpu.VMEM((total, 3 * inner), BF16),
-            pltpu.SemaphoreType.DMA((12,)),
+            pltpu.SemaphoreType.DMA((11 + sp,)),
         ],
         compiler_params=params(56),
         cost_estimate=pl.CostEstimate(flops=4 * 10**9, bytes_accessed=10**7, transcendentals=2 * 10**5),
@@ -417,14 +436,14 @@
         me,
         weights,
         mixed,
-        rest,
         norm_gain.reshape(1, width),
         bias_slope,
         visible.reshape(total, 1),
         visible.reshape(1, total),
         to_order,
+        *pieces,
     )
-    grad_resid = lax.all_gather(grad_resid, "space", axis=0)
+    grs = turned_round(grs)
     grad_time = exchange(grad_time, both)
 
     back = pl.pallas_call(
@@ -437,7 +456,7 @@
         cost_estimate=pl.CostEstimate(flops=3 * 10**8, bytes_accessed=2 * 10**6, transcendentals=0),
         name="temporal_backward",
     )(got, grad_time)
-    back, grad_resid = lax.optimization_barrier((back, grad_resid))
+    back, grs = lax.optimization_barrier((back, grs))
     back = exchange(back, "tm")
     outs = pl.pallas_call(
         unpack_kernel,
@@ -448,15 +467,14 @@
         name="unpack",
     )(back, to_steps)
     grad_resid = pl.pallas_call(
-        slice_kernel,
+        assemble_kernel,
         out_shape=shape(residual_in.shape, BF16),
-        in_specs=[SMEM, HBM],
+        in_specs=[SMEM] + [VMEM] * sp,
         out_specs=VMEM,
-        scratch_shapes=[pltpu.SemaphoreType.DMA],
-        compiler_params=params(56),
+        compiler_params=params(24),
         cost_estimate=pl.CostEstimate(flops=10**9, bytes_accessed=4 * 10**6, transcendentals=0),
-        name="slice",
-    )(me, grad_resid)
+        name="assemble",
+    )(me, *grs)
     return (grad_resid, *outs)
 
 

time: 198 us -> 213 us (1.076)
  starting transfers between devices: 15.3 us -> 73.1 us
  blocking collectives: 105 us -> 72.9 us
  waiting for transfers between devices: 37.1 us -> 21.9 us
  local copies, waits for them, and re-layouts: 1.47 us -> 5.74 us
    ppermute x0 -> x14, starting transfers between devices: none -> 36 us  [turned_round(): lax.ppermute(p, 'space', [(i, (i + k) % sp) for i in range(sp)])]
    all_to_all x3 -> x2, blocking collectives: 105 us -> 72.9 us  [exchange(): return lax.all_to_all(x, axes, split_axis=0, concat_axis=0, tiled=True)]
    all_to_all x2 -> x3, starting transfers between devices: 15.2 us -> 37 us  [exchange(): return lax.all_to_all(x, axes, split_axis=0, concat_axis=0, tiled=True)]
    all_to_all x2 -> x3, waiting for transfers between devices: 37.1 us -> 20.1 us  [exchange(): return lax.all_to_all(x, axes, split_axis=0, concat_axis=0, tiled=True)]
    unnamed x14 -> x44, local copies, waits for them, and re-layouts: 0.73 us -> 5 us
  transfers between devices with their start and end apart: 5 -> 18, of which waited for: 2 -> 2; matrix products, arithmetic and copies ran while one was open for 0% -> 0% of each run, Pallas kernels for 5% -> 3%
where the time goes in v6:
time: 213 us; the launch traced here: 212 us
  starting transfers between devices  73.1 us (34%)
  blocking collectives  72.9 us (34%)
  Pallas kernels  24.1 us (11%)
  waiting for transfers between devices  21.9 us (10%)
  between operations  14.5 us (7%)
  local copies, waits for them, and re-layouts  5.74 us (3%)
    all_to_all x2, blocking collectives, exchange(): return lax.all_to_all(x, axes, split_axis=0, concat_axis=0, tiled=True)  72.9 us
    all_to_all x3, starting transfers between devices, exchange(): return lax.all_to_all(x, axes, split_axis=0, concat_axis=0, tiled=True)  37 us
    ppermute x14, starting transfers between devices, turned_round(): lax.ppermute(p, 'space', [(i, (i + k) % sp) for i in range(sp)])  36 us
    all_to_all x3, waiting for transfers between devices, exchange(): return lax.all_to_all(x, axes, split_axis=0, concat_axis=0, tiled=True)  20.1 us
    pallas_call x1, Pallas kernels, body(): pl.pallas_call(middle_kernel, out_shape=(shape((tubes, width), BF16),) *...  12.6 us
    unnamed x44, local copies, waits for them, and re-layouts  5 us
  transfers between devices with their start and end apart: 18, of which 2 were waited for; matrix products, arithmetic and copies ran while one was open for 0% of the time, Pallas kernels for 3%

profile of v6, /device:TPU:8, one launch (start us, length us, event | category | flops | bytes accessed | tf_op | source)
XLA Modules:
  0.0 212.3 jit_solution(15531115785782658946)
XLA Ops:
  7.2 2.3 %first.1 = (bf16[16,40,768]{2,1,0:T(8,128)(2,1)}, bf16[16,2048]{1,0:T(8,128)(2,1)}, bf16[16,2048]{1,0:T(8,128)(2,1)}, bf16[16,2048]{1,0:T(8,128)(2,1)}, bf16[16,...) custom-call(s32[1]{0:T(128)} %bitcast.me_ref, ...), custom_call_target="tpu_custom_call" | custom-call | tf_op jit(solution)/shard_map/first/pallas_call | solution.py:362
  9.6 46.2 %all_to_all.25.x_ref = bf16[16,40,768]{2,1,0:T(8,128)(2,1)S(1)} all-to-all(bf16[16,40,768]{2,1,0:T(8,128)(2,1)} %get-tuple-element.35), channel_id=1, replica_groups=mesh['tm'=16,'space'=8,'dp'=4] {'tm'}, dimensions={0} | all-to-all | bytes 1966080 | tf_op jit(solution)/shard_map/all_to_all | solution.py:356
  55.8 1.5 weights_unpack.1
  58.3 0.9 copy-done.2
  61.2 26.7 %all_to_all.26.x_ref = bf16[16,24,768]{2,1,0:T(8,128)(2,1)S(1)} all-to-all(bf16[16,24,768]{2,1,0:T(8,128)(2,1)S(1)} %pack.1), channel_id=1, replica_groups=mesh['tm'=16,'space'=8,'dp'=4] {'tm'}, dimensions={0} | all-to-all | bytes 1179648 | tf_op jit(solution)/shard_map/all_to_all | solution.py:356
  87.9 1.8 temporal_forward.1
  89.7 8.4 %all-to-all-start.2 = ((bf16[128,6,128]{2,1,0:T(8,128)(2,1)}), bf16[128,6,128]{2,1,0:T(8,128)(2,1)S(1)}, u32[]{:S(2)}, u32[]{:S(2)}) async-start(bf16[128,6,128]{2,1,0:T(8,128)(2,1)} %temporal_forward.1), calls=%async_computation.2 | async-start | bytes 524288 | tf_op jit(solution)/shard_map/all_to_all | solution.py:356
  98.2 3.2 %collective-permute-start.1 = (bf16[16,2048]{1,0:T(8,128)(2,1)S(1)}, bf16[16,2048]{1,0:T(8,128)(2,1)S(1)}, u32[]{:S(2)}, u32[]{:S(2)}) collective-permute-start(bf16[16,2048]{1,0:T(8,128)(2,1)S(1)} %copy-done.18), channel_id=1, source_target_pairs={{0,8},{4,12},{8,16},{12,20},{16,24},{20,28},{24,0},{28,4},{1,9},{5... | collective-permute-start | bytes 196616 | tf_op jit(solution)/shard_map/ppermute | solution.py:351
  101.3 3.8 %collective-permute-start.2 = (bf16[16,2048]{1,0:T(8,128)(2,1)S(1)}, bf16[16,2048]{1,0:T(8,128)(2,1)S(1)}, u32[]{:S(2)}, u32[]{:S(2)}) collective-permute-start(bf16[16,2048]{1,0:T(8,128)(2,1)S(1)} %copy-done.16), channel_id=1, source_target_pairs={{0,12},{4,16},{8,20},{12,24},{16,28},{20,0},{24,4},{28,8},{1,13},{... | collective-permute-start | bytes 196616 | tf_op jit(solution)/shard_map/ppermute | solution.py:351
  105.2 4.0 %collective-permute-start.3 = (bf16[16,2048]{1,0:T(8,128)(2,1)S(1)}, bf16[16,2048]{1,0:T(8,128)(2,1)S(1)}, u32[]{:S(2)}, u32[]{:S(2)}) collective-permute-start(bf16[16,2048]{1,0:T(8,128)(2,1)S(1)} %copy-done.14), channel_id=1, source_target_pairs={{0,16},{4,20},{8,24},{12,28},{16,0},{20,4},{24,8},{28,12},{1,17},{... | collective-permute-start | bytes 196616 | tf_op jit(solution)/shard_map/ppermute | solution.py:351
  109.2 3.6 %collective-permute-start.4 = (bf16[16,2048]{1,0:T(8,128)(2,1)S(1)}, bf16[16,2048]{1,0:T(8,128)(2,1)S(1)}, u32[]{:S(2)}, u32[]{:S(2)}) collective-permute-start(bf16[16,2048]{1,0:T(8,128)(2,1)S(1)} %copy-done.12), channel_id=1, source_target_pairs={{0,20},{4,24},{8,28},{12,0},{16,4},{20,8},{24,12},{28,16},{1,21},{... | collective-permute-start | bytes 196616 | tf_op jit(solution)/shard_map/ppermute | solution.py:351
  112.8 3.5 %collective-permute-start.5 = (bf16[16,2048]{1,0:T(8,128)(2,1)S(1)}, bf16[16,2048]{1,0:T(8,128)(2,1)S(1)}, u32[]{:S(2)}, u32[]{:S(2)}) collective-permute-start(bf16[16,2048]{1,0:T(8,128)(2,1)S(1)} %copy-done.10), channel_id=1, source_target_pairs={{0,24},{4,28},{8,0},{12,4},{16,8},{20,12},{24,16},{28,20},{1,25},{... | collective-permute-start | bytes 196616 | tf_op jit(solution)/shard_map/ppermute | solution.py:351
  117.2 1.8 collective-permute-done.5.refs_6_
  119.7 12.6 %middle.1 = (bf16[16,1024]{1,0:T(8,128)(2,1)}, bf16[16,1024]{1,0:T(8,128)(2,1)}, bf16[16,1024]{1,0:T(8,128)(2,1)}, bf16[16,1024]{1,0:T(8,128)(2,1)}, bf16[16,102...) custom-call(s32[1]{0:T(128)} %bitcast.me_ref, ...), custom_call_target="tpu_custom_call" | custom-call | flops 4000000000 | bytes 10000000 | tf_op jit(solution)/shard_map/middle/pallas_call | solution.py:414
  132.3 16.5 %all-to-all-start.3 = ((bf16[128,6,128]{2,1,0:T(8,128)(2,1)}), bf16[128,6,128]{2,1,0:T(8,128)(2,1)S(1)}, u32[]{:S(2)}, u32[]{:S(2)}) async-start(bf16[128,6,128]{2,1,0:T(8,128)(2,1)} %get-tuple-element.45), calls=%async_computation.3 | async-start | bytes 524288 | tf_op jit(solution)/shard_map/all_to_all | solution.py:356
  148.8 3.2 %collective-permute-start.8 = (bf16[16,1024]{1,0:T(8,128)(2,1)}, bf16[16,1024]{1,0:T(8,128)(2,1)S(1)}, u32[]{:S(2)}, u32[]{:S(2)}) collective-permute-start(bf16[16,1024]{1,0:T(8,128)(2,1)} %get-tuple-element.48), channel_id=1, source_target_pairs={{0,8},{4,12},{8,16},{12,20},{16,24},{20,28},{24,0},{28,4},{1,9},{5... | collective-permute-start | bytes 98312 | tf_op jit(solution)/shard_map/ppermute | solution.py:351
  152.0 3.8 %collective-permute-start.9 = (bf16[16,1024]{1,0:T(8,128)(2,1)}, bf16[16,1024]{1,0:T(8,128)(2,1)S(1)}, u32[]{:S(2)}, u32[]{:S(2)}) collective-permute-start(bf16[16,1024]{1,0:T(8,128)(2,1)} %get-tuple-element.49), channel_id=1, source_target_pairs={{0,12},{4,16},{8,20},{12,24},{16,28},{20,0},{24,4},{28,8},{1,13},{... | collective-permute-start | bytes 98312 | tf_op jit(solution)/shard_map/ppermute | solution.py:351
  155.8 4.0 %collective-permute-start.10 = (bf16[16,1024]{1,0:T(8,128)(2,1)}, bf16[16,1024]{1,0:T(8,128)(2,1)S(1)}, u32[]{:S(2)}, u32[]{:S(2)}) collective-permute-start(bf16[16,1024]{1,0:T(8,128)(2,1)} %get-tuple-element.50), channel_id=1, source_target_pairs={{0,16},{4,20},{8,24},{12,28},{16,0},{20,4},{24,8},{28,12},{1,17},{... | collective-permute-start | bytes 98312 | tf_op jit(solution)/shard_map/ppermute | solution.py:351
  159.8 3.6 %collective-permute-start.11 = (bf16[16,1024]{1,0:T(8,128)(2,1)}, bf16[16,1024]{1,0:T(8,128)(2,1)S(1)}, u32[]{:S(2)}, u32[]{:S(2)}) collective-permute-start(bf16[16,1024]{1,0:T(8,128)(2,1)} %get-tuple-element.51), channel_id=1, source_target_pairs={{0,20},{4,24},{8,28},{12,0},{16,4},{20,8},{24,12},{28,16},{1,21},{... | collective-permute-start | bytes 98312 | tf_op jit(solution)/shard_map/ppermute | solution.py:351
  163.4 3.4 %collective-permute-start.12 = (bf16[16,1024]{1,0:T(8,128)(2,1)}, bf16[16,1024]{1,0:T(8,128)(2,1)S(1)}, u32[]{:S(2)}, u32[]{:S(2)}) collective-permute-start(bf16[16,1024]{1,0:T(8,128)(2,1)} %get-tuple-element.52), channel_id=1, source_target_pairs={{0,24},{4,28},{8,0},{12,4},{16,8},{20,12},{24,16},{28,20},{1,25},{... | collective-permute-start | bytes 98312 | tf_op jit(solution)/shard_map/ppermute | solution.py:351
  166.8 3.8 %temporal_backward.1 = bf16[16,24,768]{2,1,0:T(8,128)(2,1)} custom-call(bf16[16,24,768]{2,1,0:T(8,128)(2,1)S(1)} %all_to_all.26.x_ref, bf16[128,6,128]{2,1,0:T(8,128)(2,1)S(1)} %all-to-all-done.3.g_ref), custom_call_target="tpu_custom_call" | custom-call | flops 300000000 | bytes 2000000 | tf_op jit(solution)/shard_map/temporal_backward/pallas_call | solution.py:449
  170.7 12.1 %all-to-all-start.4 = ((bf16[16,24,768]{2,1,0:T(8,128)(2,1)}), bf16[16,24,768]{2,1,0:T(8,128)(2,1)S(1)}, u32[]{:S(2)}, u32[]{:S(2)}) async-start(bf16[16,24,768]{2,1,0:T(8,128)(2,1)} %temporal_backward.1), calls=%async_computation.4 | async-start | bytes 1179648 | tf_op jit(solution)/shard_map/all_to_all | solution.py:356
  184.3 20.1 %all-to-all-done.4.x_ref = bf16[16,24,768]{2,1,0:T(8,128)(2,1)S(1)} async-done(((bf16[16,24,768]{2,1,0:T(8,128)(2,1)}), bf16[16,24,768]{2,1,0:T(8,128)(2,1)S(1)}, u32[]{:S(2)}, u32[]{:S(2)}) %all-to-all-start.4) | async-done | bytes 589856 | tf_op jit(solution)/shard_map/all_to_all | solution.py:356
  204.4 1.0 unpack.1
  (68 shorter events, 6.0 us)
Async XLA Ops:
  7.2 109.2 %copy-start.7 = (s32[1,128]{1,0:T(1,128)S(1)}, s32[1,128]{1,0:T(1,128)}, u32[]{:S(2)}) copy-start(s32[1,128]{1,0:T(1,128)} %col_ref.1) | copy-start | bytes 1540
  7.2 111.8 %all-gather.3.cloned.1.call-start = ((), (), s32[]{:S(2)}) async-start(), calls=%async_computation.5 | async-start | bytes 8847360 | tf_op jit(solution)/shard_map/all_gather | solution.py:397
  9.6 91.8 %copy-start.16 = (bf16[16,2048]{1,0:T(8,128)(2,1)S(1)}, bf16[16,2048]{1,0:T(8,128)(2,1)}, u32[]{:S(2)}) copy-start(bf16[16,2048]{1,0:T(8,128)(2,1)} %get-tuple-element.40) | copy-start | bytes 196612
  9.6 95.6 %copy-start.14 = (bf16[16,2048]{1,0:T(8,128)(2,1)S(1)}, bf16[16,2048]{1,0:T(8,128)(2,1)}, u32[]{:S(2)}) copy-start(bf16[16,2048]{1,0:T(8,128)(2,1)} %get-tuple-element.41) | copy-start | bytes 196612
  9.6 99.6 %copy-start.12 = (bf16[16,2048]{1,0:T(8,128)(2,1)S(1)}, bf16[16,2048]{1,0:T(8,128)(2,1)}, u32[]{:S(2)}) copy-start(bf16[16,2048]{1,0:T(8,128)(2,1)} %get-tuple-element.42) | copy-start | bytes 196612
  9.6 103.2 %copy-start.10 = (bf16[16,2048]{1,0:T(8,128)(2,1)S(1)}, bf16[16,2048]{1,0:T(8,128)(2,1)}, u32[]{:S(2)}) copy-start(bf16[16,2048]{1,0:T(8,128)(2,1)} %get-tuple-element.43) | copy-start | bytes 196612
  9.6 106.8 %copy-start.8 = (bf16[16,2048]{1,0:T(8,128)(2,1)S(1)}, bf16[16,2048]{1,0:T(8,128)(2,1)}, u32[]{:S(2)}) copy-start(bf16[16,2048]{1,0:T(8,128)(2,1)} %get-tuple-element.44) | copy-start | bytes 196612
  89.7 29.3 %all-to-all-start.2 = ((bf16[128,6,128]{2,1,0:T(8,128)(2,1)}), bf16[128,6,128]{2,1,0:T(8,128)(2,1)S(1)}, u32[]{:S(2)}, u32[]{:S(2)}) async-start(bf16[128,6,128]{2,1,0:T(8,128)(2,1)} %temporal_forward.1), calls=%async_computation.2 | async-start | bytes 524288 | tf_op jit(solution)/shard_map/all_to_all | solution.py:356
  98.1 14.6 %collective-permute-start = (bf16[16,2048]{1,0:T(8,128)(2,1)S(1)}, bf16[16,2048]{1,0:T(8,128)(2,1)S(1)}, u32[]{:S(2)}, u32[]{:S(2)}) collective-permute-start(bf16[16,2048]{1,0:T(8,128)(2,1)S(1)} %copy-done.20), channel_id=1, source_target_pairs={{0,4},{4,8},{8,12},{12,16},{16,20},{20,24},{24,28},{28,0},{1,5},{5... | collective-permute-start | bytes 196616 | tf_op jit(solution)/shard_map/ppermute | solution.py:351
  98.2 18.2 %collective-permute-start.1 = (bf16[16,2048]{1,0:T(8,128)(2,1)S(1)}, bf16[16,2048]{1,0:T(8,128)(2,1)S(1)}, u32[]{:S(2)}, u32[]{:S(2)}) collective-permute-start(bf16[16,2048]{1,0:T(8,128)(2,1)S(1)} %copy-done.18), channel_id=1, source_target_pairs={{0,8},{4,12},{8,16},{12,20},{16,24},{20,28},{24,0},{28,4},{1,9},{5... | collective-permute-start | bytes 196616 | tf_op jit(solution)/shard_map/ppermute | solution.py:351
  101.3 15.8 %collective-permute-start.2 = (bf16[16,2048]{1,0:T(8,128)(2,1)S(1)}, bf16[16,2048]{1,0:T(8,128)(2,1)S(1)}, u32[]{:S(2)}, u32[]{:S(2)}) collective-permute-start(bf16[16,2048]{1,0:T(8,128)(2,1)S(1)} %copy-done.16), channel_id=1, source_target_pairs={{0,12},{4,16},{8,20},{12,24},{16,28},{20,0},{24,4},{28,8},{1,13},{... | collective-permute-start | bytes 196616 | tf_op jit(solution)/shard_map/ppermute | solution.py:351
  105.2 12.0 %collective-permute-start.3 = (bf16[16,2048]{1,0:T(8,128)(2,1)S(1)}, bf16[16,2048]{1,0:T(8,128)(2,1)S(1)}, u32[]{:S(2)}, u32[]{:S(2)}) collective-permute-start(bf16[16,2048]{1,0:T(8,128)(2,1)S(1)} %copy-done.14), channel_id=1, source_target_pairs={{0,16},{4,20},{8,24},{12,28},{16,0},{20,4},{24,8},{28,12},{1,17},{... | collective-permute-start | bytes 196616 | tf_op jit(solution)/shard_map/ppermute | solution.py:351
  109.2 8.0 %collective-permute-start.4 = (bf16[16,2048]{1,0:T(8,128)(2,1)S(1)}, bf16[16,2048]{1,0:T(8,128)(2,1)S(1)}, u32[]{:S(2)}, u32[]{:S(2)}) collective-permute-start(bf16[16,2048]{1,0:T(8,128)(2,1)S(1)} %copy-done.12), channel_id=1, source_target_pairs={{0,20},{4,24},{8,28},{12,0},{16,4},{20,8},{24,12},{28,16},{1,21},{... | collective-permute-start | bytes 196616 | tf_op jit(solution)/shard_map/ppermute | solution.py:351
  112.8 6.2 %collective-permute-start.5 = (bf16[16,2048]{1,0:T(8,128)(2,1)S(1)}, bf16[16,2048]{1,0:T(8,128)(2,1)S(1)}, u32[]{:S(2)}, u32[]{:S(2)}) collective-permute-start(bf16[16,2048]{1,0:T(8,128)(2,1)S(1)} %copy-done.10), channel_id=1, source_target_pairs={{0,24},{4,28},{8,0},{12,4},{16,8},{20,12},{24,16},{28,20},{1,25},{... | collective-permute-start | bytes 196616 | tf_op jit(solution)/shard_map/ppermute | solution.py:351
  116.4 2.6 %collective-permute-start.6 = (bf16[16,2048]{1,0:T(8,128)(2,1)S(1)}, bf16[16,2048]{1,0:T(8,128)(2,1)S(1)}, u32[]{:S(2)}, u32[]{:S(2)}) collective-permute-start(bf16[16,2048]{1,0:T(8,128)(2,1)S(1)} %copy-done.8), channel_id=1, source_target_pairs={{0,28},{4,0},{8,4},{12,8},{16,12},{20,16},{24,20},{28,24},{1,29},{... | collective-permute-start | bytes 196616 | tf_op jit(solution)/shard_map/ppermute | solution.py:351
  132.3 34.5 %all-to-all-start.3 = ((bf16[128,6,128]{2,1,0:T(8,128)(2,1)}), bf16[128,6,128]{2,1,0:T(8,128)(2,1)S(1)}, u32[]{:S(2)}, u32[]{:S(2)}) async-start(bf16[128,6,128]{2,1,0:T(8,128)(2,1)} %get-tuple-element.45), calls=%async_computation.3 | async-start | bytes 524288 | tf_op jit(solution)/shard_map/all_to_all | solution.py:356
  148.8 14.6 %collective-permute-start.7 = (bf16[16,1024]{1,0:T(8,128)(2,1)}, bf16[16,1024]{1,0:T(8,128)(2,1)S(1)}, u32[]{:S(2)}, u32[]{:S(2)}) collective-permute-start(bf16[16,1024]{1,0:T(8,128)(2,1)} %get-tuple-element.47), channel_id=1, source_target_pairs={{0,4},{4,8},{8,12},{12,16},{16,20},{20,24},{24,28},{28,0},{1,5},{5... | collective-permute-start | bytes 98312 | tf_op jit(solution)/shard_map/ppermute | solution.py:351
  148.8 18.0 %collective-permute-start.8 = (bf16[16,1024]{1,0:T(8,128)(2,1)}, bf16[16,1024]{1,0:T(8,128)(2,1)S(1)}, u32[]{:S(2)}, u32[]{:S(2)}) collective-permute-start(bf16[16,1024]{1,0:T(8,128)(2,1)} %get-tuple-element.48), channel_id=1, source_target_pairs={{0,8},{4,12},{8,16},{12,20},{16,24},{20,28},{24,0},{28,4},{1,9},{5... | collective-permute-start | bytes 98312 | tf_op jit(solution)/shard_map/ppermute | solution.py:351
  152.0 18.7 %collective-permute-start.9 = (bf16[16,1024]{1,0:T(8,128)(2,1)}, bf16[16,1024]{1,0:T(8,128)(2,1)S(1)}, u32[]{:S(2)}, u32[]{:S(2)}) collective-permute-start(bf16[16,1024]{1,0:T(8,128)(2,1)} %get-tuple-element.49), channel_id=1, source_target_pairs={{0,12},{4,16},{8,20},{12,24},{16,28},{20,0},{24,4},{28,8},{1,13},{... | collective-permute-start | bytes 98312 | tf_op jit(solution)/shard_map/ppermute | solution.py:351
  155.8 14.8 %collective-permute-start.10 = (bf16[16,1024]{1,0:T(8,128)(2,1)}, bf16[16,1024]{1,0:T(8,128)(2,1)S(1)}, u32[]{:S(2)}, u32[]{:S(2)}) collective-permute-start(bf16[16,1024]{1,0:T(8,128)(2,1)} %get-tuple-element.50), channel_id=1, source_target_pairs={{0,16},{4,20},{8,24},{12,28},{16,0},{20,4},{24,8},{28,12},{1,17},{... | collective-permute-start | bytes 98312 | tf_op jit(solution)/shard_map/ppermute | solution.py:351
  159.8 10.9 %collective-permute-start.11 = (bf16[16,1024]{1,0:T(8,128)(2,1)}, bf16[16,1024]{1,0:T(8,128)(2,1)S(1)}, u32[]{:S(2)}, u32[]{:S(2)}) collective-permute-start(bf16[16,1024]{1,0:T(8,128)(2,1)} %get-tuple-element.51), channel_id=1, source_target_pairs={{0,20},{4,24},{8,28},{12,0},{16,4},{20,8},{24,12},{28,16},{1,21},{... | collective-permute-start | bytes 98312 | tf_op jit(solution)/shard_map/ppermute | solution.py:351
  163.4 7.3 %collective-permute-start.12 = (bf16[16,1024]{1,0:T(8,128)(2,1)}, bf16[16,1024]{1,0:T(8,128)(2,1)S(1)}, u32[]{:S(2)}, u32[]{:S(2)}) collective-permute-start(bf16[16,1024]{1,0:T(8,128)(2,1)} %get-tuple-element.52), channel_id=1, source_target_pairs={{0,24},{4,28},{8,0},{12,4},{16,8},{20,12},{24,16},{28,20},{1,25},{... | collective-permute-start | bytes 98312 | tf_op jit(solution)/shard_map/ppermute | solution.py:351
  166.8 3.9 %collective-permute-start.13 = (bf16[16,1024]{1,0:T(8,128)(2,1)}, bf16[16,1024]{1,0:T(8,128)(2,1)S(1)}, u32[]{:S(2)}, u32[]{:S(2)}) collective-permute-start(bf16[16,1024]{1,0:T(8,128)(2,1)} %get-tuple-element.53), channel_id=1, source_target_pairs={{0,28},{4,0},{8,4},{12,8},{16,12},{20,16},{24,20},{28,24},{1,29},{... | collective-permute-start | bytes 98312 | tf_op jit(solution)/shard_map/ppermute | solution.py:351
  170.7 33.7 %all-to-all-start.4 = ((bf16[16,24,768]{2,1,0:T(8,128)(2,1)}), bf16[16,24,768]{2,1,0:T(8,128)(2,1)S(1)}, u32[]{:S(2)}, u32[]{:S(2)}) async-start(bf16[16,24,768]{2,1,0:T(8,128)(2,1)} %temporal_backward.1), calls=%async_computation.4 | async-start | bytes 1179648 | tf_op jit(solution)/shard_map/all_to_all | solution.py:356
  (16 other events, 282.7 us)
Sparse Core Ops, SparseCore 0:
  57.5 47.4 all-gather.2

commit v7 on v5

--- a/solution.py
+++ b/solution.py
@@ -155,7 +155,7 @@
 
 def softmax(scores):
     exponent = jnp.exp(scores - jnp.max(scores, axis=-1, keepdims=True))
-    return exponent / jnp.sum(exponent, axis=-1, keepdims=True)
+    return exponent * (1.0 / jnp.sum(exponent, axis=-1, keepdims=True))
 
 
 def pair_probs(q, k2, bias0=None, bias1=None):
@@ -200,7 +200,19 @@
     o_ref[...] = turned[...].astype(BF16)
 
 
-def backward_kernel(x_ref, g_ref, o_ref, turned):
+def probs_kernel(x_ref, p_ref):
+    x = x_ref[...].astype(F32)
+    q, k, _ = qkv_of(x, x.shape[1] // 3)
+    n = q.shape[0]
+    first = lane_masks(n)
+    for h in range(HEADS // 2):
+        at = slice(h * 128, (h + 1) * 128)
+        p0, p1 = pair_probs(q[:, at], stacked(k[:, at], first))
+        p_ref[h, :, 0:n] = p0
+        p_ref[h, :, n : 2 * n] = p1
+
+
+def backward_kernel(x_ref, p_ref, g_ref, o_ref, turned):
     x = x_ref[...].astype(F32)
     steps = x.shape[1] // 3
     q, k, v = qkv_of(x, steps)
@@ -209,10 +221,9 @@
     first = lane_masks(n)
     for h in range(HEADS // 2):
         at = slice(h * 128, (h + 1) * 128)
-        p0, p1 = pair_probs(q[:, at], stacked(k[:, at], first))
         grads = pair_backward(
-            p0,
-            p1,
+            p_ref[h, :, 0:n],
+            p_ref[h, :, n : 2 * n],
             q[:, at],
             k[:, at],
             v[:, at],
@@ -425,18 +436,28 @@
         to_order,
     )
     grad_resid = lax.all_gather(grad_resid, "space", axis=0)
+    got, grad_time = lax.optimization_barrier((got, grad_time))
     grad_time = exchange(grad_time, both)
+    probs = pl.pallas_call(
+        probs_kernel,
+        out_shape=shape((HEADS // 2, total, 2 * total), F32),
+        in_specs=[VMEM],
+        out_specs=VMEM,
+        compiler_params=params(24),
+        cost_estimate=pl.CostEstimate(flops=10**9, bytes_accessed=4 * 10**6, transcendentals=2 * 10**5),
+        name="temporal_probs",
+    )(got)
 
     back = pl.pallas_call(
         backward_kernel,
         out_shape=shape((tm, 3 * steps, inner), BF16),
-        in_specs=[VMEM] * 2,
+        in_specs=[VMEM] * 3,
         out_specs=VMEM,
         scratch_shapes=[pltpu.VMEM((total, 6, 128), F32)],
         compiler_params=params(24),
         cost_estimate=pl.CostEstimate(flops=3 * 10**8, bytes_accessed=2 * 10**6, transcendentals=0),
         name="temporal_backward",
-    )(got, grad_time)
+    )(got, probs, grad_time)
     back, grad_resid = lax.optimization_barrier((back, grad_resid))
     back = exchange(back, "tm")
     outs = pl.pallas_call(

time: 198 us -> 198 us (level)
  blocking collectives: 105 us -> 72.9 us
  waiting for transfers between devices: 37.1 us -> 54.8 us
  starting transfers between devices: 15.3 us -> 29.5 us
    all_to_all x3 -> x2, blocking collectives: 105 us -> 72.9 us  [exchange(): return lax.all_to_all(x, axes, split_axis=0, concat_axis=0, tiled=True)]
    all_to_all x2 -> x3, waiting for transfers between devices: 37.1 us -> 54.7 us  [exchange(): return lax.all_to_all(x, axes, split_axis=0, concat_axis=0, tiled=True)]
    all_to_all x2 -> x3, starting transfers between devices: 15.2 us -> 29.4 us  [exchange(): return lax.all_to_all(x, axes, split_axis=0, concat_axis=0, tiled=True)]
  transfers between devices with their start and end apart: 5 -> 6, of which waited for: 2 -> 3; matrix products, arithmetic and copies ran while one was open for 0% -> 0% of each run, Pallas kernels for 5% -> 4%
where the time goes in v7:
time: 198 us; the launch traced here: 197 us
  blocking collectives  72.9 us (37%)
  waiting for transfers between devices  54.8 us (28%)
  starting transfers between devices  29.5 us (15%)
  Pallas kernels  24.7 us (12%)
  between operations  13.9 us (7%)
    all_to_all x2, blocking collectives, exchange(): return lax.all_to_all(x, axes, split_axis=0, concat_axis=0, tiled=True)  72.9 us
    all_to_all x3, waiting for transfers between devices, exchange(): return lax.all_to_all(x, axes, split_axis=0, concat_axis=0, tiled=True)  54.7 us
    all_to_all x3, starting transfers between devices, exchange(): return lax.all_to_all(x, axes, split_axis=0, concat_axis=0, tiled=True)  29.4 us
    pallas_call x1, Pallas kernels, body(): pl.pallas_call(middle_kernel, out_shape=(shape((total, width), BF16), sha...  12.5 us
  transfers between devices with their start and end apart: 6, of which 3 were waited for; matrix products, arithmetic and copies ran while one was open for 0% of the time, Pallas kernels for 4%

profile of v7, /device:TPU:8, one launch (start us, length us, event | category | flops | bytes accessed | tf_op | source)
XLA Modules:
  0.0 197.2 jit_solution(11328814571538857924)
XLA Ops:
  7.2 0.0 all-gather.9.cloned.1.call-start
  7.3 2.4 %first.1 = (bf16[16,40,768]{2,1,0:T(8,128)(2,1)}, bf16[8,16,2048]{2,1,0:T(8,128)(2,1)}) custom-call(bf16[6,1024]{1,0:T(8,128)(2,1)} %fc_hbm.1, bf16[6,1024]{1,0:T(8,128)(2,1)} %out_hbm.1, bf16[8,2304]{1,0:T(8,128)(2,1)} %qkv_hbm.1, bf16[1,8,16,1024]{3,2,1,0:T(8,128)(2,1)} %res_hbm.1, bf16[1,8,16,1024]{3,2,1,0:T(8,128)(2,1)} %cot_hbm.1), custom_call_target="tpu_custom_call" | custom-call | tf_op jit(solution)/shard_map/first/pallas_call | solution.py:355
  9.6 0.0 all-gather.9.cloned.1.call-update
  9.7 0.0 all-gather.7.cloned.1.call-start
  9.7 46.1 %all_to_all.25.x_ref = bf16[16,40,768]{2,1,0:T(8,128)(2,1)S(1)} all-to-all(bf16[16,40,768]{2,1,0:T(8,128)(2,1)} %get-tuple-element.16), channel_id=1, replica_groups=mesh['tm'=16,'space'=8,'dp'=4] {'tm'}, dimensions={0} | all-to-all | bytes 1966080 | tf_op jit(solution)/shard_map/all_to_all | solution.py:349
  55.8 1.4 weights_unpack.1
  57.3 0.3 pack.1
  57.6 26.8 %all_to_all.26.x_ref = bf16[16,24,768]{2,1,0:T(8,128)(2,1)S(1)} all-to-all(bf16[16,24,768]{2,1,0:T(8,128)(2,1)S(1)} %pack.1), channel_id=1, replica_groups=mesh['tm'=16,'space'=8,'dp'=4] {'tm'}, dimensions={0} | all-to-all | bytes 1179648 | tf_op jit(solution)/shard_map/all_to_all | solution.py:349
  84.4 1.8 temporal_forward.1
  86.2 8.3 %all-to-all-start.2 = ((bf16[128,6,128]{2,1,0:T(8,128)(2,1)}), bf16[128,6,128]{2,1,0:T(8,128)(2,1)S(1)}, u32[]{:S(2)}, u32[]{:S(2)}) async-start(bf16[128,6,128]{2,1,0:T(8,128)(2,1)} %temporal_forward.1), calls=%async_computation.2 | async-start | bytes 524288 | tf_op jit(solution)/shard_map/all_to_all | solution.py:349
  94.6 0.0 all-gather.11.cloned.1.call-start
  94.6 0.7 copy.19.row_ref
  95.4 15.8 %all-to-all-done.2.x_ref = bf16[128,6,128]{2,1,0:T(8,128)(2,1)S(1)} async-done(((bf16[128,6,128]{2,1,0:T(8,128)(2,1)}), bf16[128,6,128]{2,1,0:T(8,128)(2,1)S(1)}, u32[]{:S(2)}, u32[]{:S(2)}) %all-to-all-start.2) | async-done | bytes 196640 | tf_op jit(solution)/shard_map/all_to_all | solution.py:349
  111.2 0.7 copy-done.5
  111.9 12.5 %middle.1 = (bf16[128,1024]{1,0:T(8,128)(2,1)}, bf16[128,6,128]{2,1,0:T(8,128)(2,1)}) custom-call(s32[1]{0:T(128)} %bitcast.me_ref, bf16[8,640,768]{2,1,0:T(8,128)(2,1)} %bitcast.7, bf16[128,6,128]{2,1,0:T(8,128)(2,1)} %copy-done.5, bf16[8,8,16,2048]{3,2,1,0:T(8,128)(2,1)} %bitcast.8, f32[1,1024]{1,0:T(1,128)} %bitcast.10, f32[12]{0:T(128)} %slope_ref.1, ...), custom_call_target="tpu_custom_call" | custom-call | flops 4000000000 | bytes 10000000 | tf_op jit(solution)/shard_map/middle/pallas_call | solution.py:407
  124.4 0.0 all-gather.11.cloned.1.call-update
  124.4 13.3 %all-to-all-start.3 = ((bf16[128,6,128]{2,1,0:T(8,128)(2,1)}), bf16[128,6,128]{2,1,0:T(8,128)(2,1)S(1)}, u32[]{:S(2)}, u32[]{:S(2)}) async-start(bf16[128,6,128]{2,1,0:T(8,128)(2,1)} %get-tuple-element.21), calls=%async_computation.3 | async-start | bytes 524288 | tf_op jit(solution)/shard_map/all_to_all | solution.py:349
  137.7 0.7 temporal_probs.1.p_ref
  138.4 17.7 %all-to-all-done.3.g_ref = bf16[128,6,128]{2,1,0:T(8,128)(2,1)S(1)} async-done(((bf16[128,6,128]{2,1,0:T(8,128)(2,1)}), bf16[128,6,128]{2,1,0:T(8,128)(2,1)S(1)}, u32[]{:S(2)}, u32[]{:S(2)}) %all-to-all-start.3) | async-done | bytes 196640 | tf_op jit(solution)/shard_map/all_to_all | solution.py:349
  156.1 2.9 %temporal_backward.1 = bf16[16,24,768]{2,1,0:T(8,128)(2,1)} custom-call(bf16[16,24,768]{2,1,0:T(8,128)(2,1)S(1)} %all_to_all.26.x_ref, f32[6,128,256]{2,1,0:T(8,128)S(1)} %temporal_probs.1.p_ref, bf16[128,6,128]{2,1,0:T(8,128)(2,1)S(1)} %all-to-all-done.3.g_ref), custom_call_target="tpu_custom_call" | custom-call | flops 300000000 | bytes 2000000 | tf_op jit(solution)/shard_map/temporal_backward/pallas_call | solution.py:451
  159.0 7.8 %all-to-all-start.4 = ((bf16[16,24,768]{2,1,0:T(8,128)(2,1)}), bf16[16,24,768]{2,1,0:T(8,128)(2,1)S(1)}, u32[]{:S(2)}, u32[]{:S(2)}) async-start(bf16[16,24,768]{2,1,0:T(8,128)(2,1)} %temporal_backward.1), calls=%async_computation.4 | async-start | bytes 1179648 | tf_op jit(solution)/shard_map/all_to_all | solution.py:349
  166.8 1.7 slice.1
  168.5 21.2 %all-to-all-done.4.x_ref = bf16[16,24,768]{2,1,0:T(8,128)(2,1)S(1)} async-done(((bf16[16,24,768]{2,1,0:T(8,128)(2,1)}), bf16[16,24,768]{2,1,0:T(8,128)(2,1)S(1)}, u32[]{:S(2)}, u32[]{:S(2)}) %all-to-all-start.4) | async-done | bytes 589856 | tf_op jit(solution)/shard_map/all_to_all | solution.py:349
  189.7 1.0 unpack.1
  (17 shorter events, 0.1 us)
Async XLA Ops:
  7.2 50.1 %copy-start.4 = (bf16[128,128]{1,0:T(8,128)(2,1)S(1)}, bf16[128,128]{1,0:T(8,128)(2,1)}, u32[]{:S(2)}) copy-start(bf16[128,128]{1,0:T(8,128)(2,1)} %constant.10.clone.turn_ref) | copy-start | bytes 98308
  7.2 50.1 %copy-start.1 = (bf16[1,8,16,768]{3,2,1,0:T(8,128)(2,1)S(1)}, bf16[1,8,16,768]{3,2,1,0:T(8,128)(2,1)}, u32[]{:S(2)}) copy-start(bf16[1,8,16,768]{3,2,1,0:T(8,128)(2,1)} %q_ref.1) | copy-start | bytes 589828
  7.2 50.1 %copy-start.2 = (bf16[1,8,16,768]{3,2,1,0:T(8,128)(2,1)S(1)}, bf16[1,8,16,768]{3,2,1,0:T(8,128)(2,1)}, u32[]{:S(2)}) copy-start(bf16[1,8,16,768]{3,2,1,0:T(8,128)(2,1)} %k_ref.1) | copy-start | bytes 589828
  7.2 50.1 %copy-start.3 = (bf16[1,8,16,768]{3,2,1,0:T(8,128)(2,1)S(1)}, bf16[1,8,16,768]{3,2,1,0:T(8,128)(2,1)}, u32[]{:S(2)}) copy-start(bf16[1,8,16,768]{3,2,1,0:T(8,128)(2,1)} %v_ref.1) | copy-start | bytes 589828
  7.2 104.0 %all-gather.9.cloned.1.call-start = ((), (), s32[]{:S(2)}) async-start(), calls=%async_computation.6 | async-start | bytes 4718592 | tf_op jit(solution)/shard_map/all_gather | solution.py:369
  9.7 101.5 %all-gather.7.cloned.1.call-start = ((), (), s32[]{:S(2)}) async-start(), calls=%async_computation.5 | async-start | bytes 8847360 | tf_op jit(solution)/shard_map/all_gather | solution.py:390
  55.8 38.8 %copy-start.6 = (s32[1,128]{1,0:T(1,128)S(1)}, s32[1,128]{1,0:T(1,128)}, u32[]{:S(2)}) copy-start(s32[1,128]{1,0:T(1,128)} %col_ref.1) | copy-start | bytes 1540
  86.2 25.0 %all-to-all-start.2 = ((bf16[128,6,128]{2,1,0:T(8,128)(2,1)}), bf16[128,6,128]{2,1,0:T(8,128)(2,1)S(1)}, u32[]{:S(2)}, u32[]{:S(2)}) async-start(bf16[128,6,128]{2,1,0:T(8,128)(2,1)} %temporal_forward.1), calls=%async_computation.2 | async-start | bytes 524288 | tf_op jit(solution)/shard_map/all_to_all | solution.py:349
  94.6 64.4 %all-gather.11.cloned.1.call-start = ((), (), s32[]{:S(2)}) async-start(), calls=%async_computation.7 | async-start | bytes 2359296 | tf_op jit(solution)/shard_map/all_gather | solution.py:438
  111.2 0.7 copy-start.5
  124.4 31.7 %all-to-all-start.3 = ((bf16[128,6,128]{2,1,0:T(8,128)(2,1)}), bf16[128,6,128]{2,1,0:T(8,128)(2,1)S(1)}, u32[]{:S(2)}, u32[]{:S(2)}) async-start(bf16[128,6,128]{2,1,0:T(8,128)(2,1)} %get-tuple-element.21), calls=%async_computation.3 | async-start | bytes 524288 | tf_op jit(solution)/shard_map/all_to_all | solution.py:349
  138.4 51.3 %copy-start = (bf16[128,128]{1,0:T(8,128)(2,1)S(1)}, bf16[128,128]{1,0:T(8,128)(2,1)}, u32[]{:S(2)}) copy-start(bf16[128,128]{1,0:T(8,128)(2,1)} %constant.11.clone.turn_ref) | copy-start | bytes 98308
  159.0 30.7 %all-to-all-start.4 = ((bf16[16,24,768]{2,1,0:T(8,128)(2,1)}), bf16[16,24,768]{2,1,0:T(8,128)(2,1)S(1)}, u32[]{:S(2)}, u32[]{:S(2)}) async-start(bf16[16,24,768]{2,1,0:T(8,128)(2,1)} %temporal_backward.1), calls=%async_computation.4 | async-start | bytes 1179648 | tf_op jit(solution)/shard_map/all_to_all | solution.py:349
Sparse Core Ops, SparseCore 0:
  10.2 41.9 all-gather.8
  57.4 51.7 all-gather.6
  124.6 30.1 all-gather.10

commit v8 on v7

--- a/solution.py
+++ b/solution.py
@@ -127,15 +127,8 @@
     o_ref[...] = jnp.concatenate(parts, axis=1).astype(BF16)
 
 
-def slice_kernel(me_ref, gr_hbm, o_ref, sem):
-    mine = o_ref.shape[2]
-    at = pl.multiple_of(me_ref[0] * mine, mine)
-    copy = pltpu.make_async_copy(gr_hbm.at[:, pl.ds(at, mine), :], o_ref.at[0], sem)
-    copy.start()
-    copy.wait()
-
-
-def unpack_kernel(x_ref, turn_ref, *outs):
+def unpack_kernel(x_ref, turn_ref, gr_ref, gr_out, *outs):
+    gr_out[0] = gr_ref[...]
     x = x_ref[...].astype(F32)
     tubes, steps = x.shape[0], x.shape[1] // 3
     for j, o_ref in enumerate(outs):
@@ -435,7 +428,6 @@
         visible.reshape(1, total),
         to_order,
     )
-    grad_resid = lax.all_gather(grad_resid, "space", axis=0)
     got, grad_time = lax.optimization_barrier((got, grad_time))
     grad_time = exchange(grad_time, both)
     probs = pl.pallas_call(
@@ -448,6 +440,8 @@
         name="temporal_probs",
     )(got)
 
+    grad_resid, grad_time = lax.optimization_barrier((grad_resid, grad_time))
+    grad_resid = exchange(grad_resid.reshape(steps, tubes, width), "space")
     back = pl.pallas_call(
         backward_kernel,
         out_shape=shape((tm, 3 * steps, inner), BF16),
@@ -462,23 +456,13 @@
     back = exchange(back, "tm")
     outs = pl.pallas_call(
         unpack_kernel,
-        out_shape=(shape(time_query.shape, BF16),) * 3,
-        in_specs=[VMEM, VMEM],
-        out_specs=(VMEM,) * 3,
+        out_shape=(shape(residual_in.shape, BF16),) + (shape(time_query.shape, BF16),) * 3,
+        in_specs=[VMEM] * 3,
+        out_specs=(VMEM,) * 4,
         compiler_params=params(24),
         name="unpack",
-    )(back, to_steps)
-    grad_resid = pl.pallas_call(
-        slice_kernel,
-        out_shape=shape(residual_in.shape, BF16),
-        in_specs=[SMEM, HBM],
-        out_specs=VMEM,
-        scratch_shapes=[pltpu.SemaphoreType.DMA],
-        compiler_params=params(56),
-        cost_estimate=pl.CostEstimate(flops=10**9, bytes_accessed=4 * 10**6, transcendentals=0),
-        name="slice",
-    )(me, grad_resid)
-    return (grad_resid, *outs)
+    )(back, to_steps, grad_resid)
+    return tuple(outs)
 
 
 def solution(mesh):

time: 198 us -> 202 us (1.020)
  blocking collectives: 72.9 us -> 128 us
  waiting for transfers between devices: 54.8 us -> 20.6 us
  starting transfers between devices: 29.5 us -> 11.9 us
  local copies, waits for them, and re-layouts: 1.47 us -> 4.98 us
  Pallas kernels: 24.7 us -> 22.1 us
    all_to_all x2 -> x4, blocking collectives: 72.9 us -> 128 us  [exchange(): return lax.all_to_all(x, axes, split_axis=0, concat_axis=0, tiled=True)]
    all_to_all x3 -> x2, waiting for transfers between devices: 54.7 us -> 20.6 us  [exchange(): return lax.all_to_all(x, axes, split_axis=0, concat_axis=0, tiled=True)]
    all_to_all x3 -> x2, starting transfers between devices: 29.4 us -> 11.8 us  [exchange(): return lax.all_to_all(x, axes, split_axis=0, concat_axis=0, tiled=True)]
    unnamed x14, local copies, waits for them, and re-layouts: 0.73 us -> 4.24 us
  transfers between devices with their start and end apart: 6 -> 4, of which waited for: 3 -> 2; matrix products, arithmetic and copies ran while one was open for 0% -> 0% of each run, Pallas kernels for 4% -> 3%
where the time goes in v8:
time: 202 us
  blocking collectives  128 us (63%)
  Pallas kernels  22.1 us (11%)
  waiting for transfers between devices  20.6 us (10%)
  between operations  14.1 us (7%)
  starting transfers between devices  11.9 us (6%)
  local copies, waits for them, and re-layouts  4.98 us (2%)
    all_to_all x4, blocking collectives, exchange(): return lax.all_to_all(x, axes, split_axis=0, concat_axis=0, tiled=True)  128 us
    all_to_all x2, waiting for transfers between devices, exchange(): return lax.all_to_all(x, axes, split_axis=0, concat_axis=0, tiled=True)  20.6 us
    pallas_call x1, Pallas kernels, body(): pl.pallas_call(middle_kernel, out_shape=(shape((total, width), BF16), sha...  12.5 us
    all_to_all x2, starting transfers between devices, exchange(): return lax.all_to_all(x, axes, split_axis=0, concat_axis=0, tiled=True)  11.8 us
    unnamed x14, local copies, waits for them, and re-layouts  4.24 us
  transfers between devices with their start and end apart: 4, of which 2 were waited for; matrix products, arithmetic and copies ran while one was open for 0% of the time, Pallas kernels for 3%

profile of v8, /device:TPU:8, one launch (start us, length us, event | category | flops | bytes accessed | tf_op | source)
XLA Modules:
  0.0 201.6 jit_solution(12112513192212287360)
XLA Ops:
  7.2 0.0 all-gather.7.cloned.1.call-start
  7.2 2.3 %first.1 = (bf16[16,40,768]{2,1,0:T(8,128)(2,1)}, bf16[8,16,2048]{2,1,0:T(8,128)(2,1)}) custom-call(bf16[6,1024]{1,0:T(8,128)(2,1)} %fc_hbm.1, bf16[6,1024]{1,0:T(8,128)(2,1)} %out_hbm.1, bf16[8,2304]{1,0:T(8,128)(2,1)} %qkv_hbm.1, bf16[1,8,16,1024]{3,2,1,0:T(8,128)(2,1)} %res_hbm.1, bf16[1,8,16,1024]{3,2,1,0:T(8,128)(2,1)} %cot_hbm.1), custom_call_target="tpu_custom_call" | custom-call | tf_op jit(solution)/shard_map/first/pallas_call | solution.py:348
  9.5 0.0 all-gather.5.cloned.1.call-start
  9.6 46.1 %all_to_all.30.x_ref = bf16[16,40,768]{2,1,0:T(8,128)(2,1)S(1)} all-to-all(bf16[16,40,768]{2,1,0:T(8,128)(2,1)} %get-tuple-element.15), channel_id=1, replica_groups=mesh['tm'=16,'space'=8,'dp'=4] {'tm'}, dimensions={0} | all-to-all | bytes 1966080 | tf_op jit(solution)/shard_map/all_to_all | solution.py:342
  55.7 1.4 weights_unpack.1
  57.1 0.9 copy-done.1
  58.0 0.9 copy-done.2
  59.0 0.9 copy-done.3
  59.9 0.8 copy-done.4
  60.7 0.3 pack.1
  61.0 26.8 %all_to_all.31.x_ref = bf16[16,24,768]{2,1,0:T(8,128)(2,1)S(1)} all-to-all(bf16[16,24,768]{2,1,0:T(8,128)(2,1)S(1)} %pack.1), channel_id=1, replica_groups=mesh['tm'=16,'space'=8,'dp'=4] {'tm'}, dimensions={0} | all-to-all | bytes 1179648 | tf_op jit(solution)/shard_map/all_to_all | solution.py:342
  87.8 1.8 temporal_forward.1
  89.6 8.4 %all-to-all-start.2 = ((bf16[128,6,128]{2,1,0:T(8,128)(2,1)}), bf16[128,6,128]{2,1,0:T(8,128)(2,1)S(1)}, u32[]{:S(2)}, u32[]{:S(2)}) async-start(bf16[128,6,128]{2,1,0:T(8,128)(2,1)} %temporal_forward.1), calls=%async_computation.2 | async-start | bytes 524288 | tf_op jit(solution)/shard_map/all_to_all | solution.py:342
  98.0 0.7 copy.19.row_ref
  98.7 15.9 %all-to-all-done.2.x_ref = bf16[128,6,128]{2,1,0:T(8,128)(2,1)S(1)} async-done(((bf16[128,6,128]{2,1,0:T(8,128)(2,1)}), bf16[128,6,128]{2,1,0:T(8,128)(2,1)S(1)}, u32[]{:S(2)}, u32[]{:S(2)}) %all-to-all-start.2) | async-done | bytes 196640 | tf_op jit(solution)/shard_map/all_to_all | solution.py:342
  114.6 0.7 copy-done.5
  115.3 12.5 %middle.1 = (bf16[128,1024]{1,0:T(8,128)(2,1)}, bf16[128,6,128]{2,1,0:T(8,128)(2,1)}) custom-call(s32[1]{0:T(128)} %bitcast.me_ref, bf16[8,640,768]{2,1,0:T(8,128)(2,1)} %bitcast.8, bf16[128,6,128]{2,1,0:T(8,128)(2,1)} %copy-done.5, bf16[8,8,16,2048]{3,2,1,0:T(8,128)(2,1)} %bitcast.9, f32[1,1024]{1,0:T(1,128)} %bitcast.10, f32[12]{0:T(128)} %slope_ref.1, ...), custom_call_target="tpu_custom_call" | custom-call | flops 4000000000 | bytes 10000000 | tf_op jit(solution)/shard_map/middle/pallas_call | solution.py:400
  127.8 28.3 %all_to_all.32.g_ref = bf16[128,6,128]{2,1,0:T(8,128)(2,1)S(1)} all-to-all(bf16[128,6,128]{2,1,0:T(8,128)(2,1)} %get-tuple-element.21), channel_id=1, replica_groups=mesh['tm'=16,'space'=8,'dp'=4] {'tm','space'}, dimensions={0} | all-to-all | bytes 393216 | tf_op jit(solution)/shard_map/all_to_all | solution.py:342
  156.1 3.4 %all-to-all-start.4 = ((bf16[8,16,1024]{2,1,0:T(8,128)(2,1)}), bf16[8,16,1024]{2,1,0:T(8,128)(2,1)S(1)}, u32[]{:S(2)}, u32[]{:S(2)}) async-start(bf16[8,16,1024]{2,1,0:T(8,128)(2,1)} %bitcast.6), calls=%async_computation.4 | async-start | bytes 524288 | tf_op jit(solution)/shard_map/all_to_all | solution.py:342
  159.5 0.7 temporal_probs.1.p_ref
  160.2 2.0 %temporal_backward.1 = bf16[16,24,768]{2,1,0:T(8,128)(2,1)S(1)} custom-call(bf16[16,24,768]{2,1,0:T(8,128)(2,1)S(1)} %all_to_all.31.x_ref, f32[6,128,256]{2,1,0:T(8,128)S(1)} %temporal_probs.1.p_ref, bf16[128,6,128]{2,1,0:T(8,128)(2,1)S(1)} %all_to_all.32.g_ref), custom_call_target="tpu_custom_call" | custom-call | flops 300000000 | bytes 2000000 | tf_op jit(solution)/shard_map/temporal_backward/pallas_call | solution.py:445
  162.3 4.7 %all-to-all-done.4.gr_ref = bf16[8,16,1024]{2,1,0:T(8,128)(2,1)S(1)} async-done(((bf16[8,16,1024]{2,1,0:T(8,128)(2,1)}), bf16[8,16,1024]{2,1,0:T(8,128)(2,1)S(1)}, u32[]{:S(2)}, u32[]{:S(2)}) %all-to-all-start.4) | async-done | bytes 262176 | tf_op jit(solution)/shard_map/all_to_all | solution.py:342
  167.0 26.8 %all_to_all.33.x_ref = bf16[16,24,768]{2,1,0:T(8,128)(2,1)S(1)} all-to-all(bf16[16,24,768]{2,1,0:T(8,128)(2,1)S(1)} %temporal_backward.1), channel_id=1, replica_groups=mesh['tm'=16,'space'=8,'dp'=4] {'tm'}, dimensions={0} | all-to-all | bytes 1179648 | tf_op jit(solution)/shard_map/all_to_all | solution.py:342
  193.7 1.1 unpack.1
  (13 shorter events, 0.1 us)
Async XLA Ops:
  7.2 90.8 %copy-start.6 = (s32[1,128]{1,0:T(1,128)S(1)}, s32[1,128]{1,0:T(1,128)}, u32[]{:S(2)}) copy-start(s32[1,128]{1,0:T(1,128)} %col_ref.1) | copy-start | bytes 1540
  7.2 107.4 %all-gather.7.cloned.1.call-start = ((), (), s32[]{:S(2)}) async-start(), calls=%async_computation.7 | async-start | bytes 4718592 | tf_op jit(solution)/shard_map/all_gather | solution.py:362
  9.5 105.1 %all-gather.5.cloned.1.call-start = ((), (), s32[]{:S(2)}) async-start(), calls=%async_computation.6 | async-start | bytes 8847360 | tf_op jit(solution)/shard_map/all_gather | solution.py:383
  57.1 0.9 copy-start.1
  58.0 0.9 copy-start.2
  59.0 0.9 copy-start.3
  59.9 0.8 copy-start.4
  89.6 25.0 %all-to-all-start.2 = ((bf16[128,6,128]{2,1,0:T(8,128)(2,1)}), bf16[128,6,128]{2,1,0:T(8,128)(2,1)S(1)}, u32[]{:S(2)}, u32[]{:S(2)}) async-start(bf16[128,6,128]{2,1,0:T(8,128)(2,1)} %temporal_forward.1), calls=%async_computation.2 | async-start | bytes 524288 | tf_op jit(solution)/shard_map/all_to_all | solution.py:342
  114.6 0.7 copy-start.5
  115.3 78.4 %copy-start = (bf16[128,128]{1,0:T(8,128)(2,1)S(1)}, bf16[128,128]{1,0:T(8,128)(2,1)}, u32[]{:S(2)}) copy-start(bf16[128,128]{1,0:T(8,128)(2,1)} %constant.11.clone.turn_ref) | copy-start | bytes 98308
  156.1 10.9 %all-to-all-start.4 = ((bf16[8,16,1024]{2,1,0:T(8,128)(2,1)}), bf16[8,16,1024]{2,1,0:T(8,128)(2,1)S(1)}, u32[]{:S(2)}, u32[]{:S(2)}) async-start(bf16[8,16,1024]{2,1,0:T(8,128)(2,1)} %bitcast.6), calls=%async_computation.4 | async-start | bytes 524288 | tf_op jit(solution)/shard_map/all_to_all | solution.py:342
Sparse Core Ops, SparseCore 0:
  10.2 41.9 all-gather.6
  57.2 51.1 all-gather.4

commit v9 on v8

--- a/solution.py
+++ b/solution.py
@@ -77,7 +77,10 @@
     return jnp.where(column == source, 1.0, 0.0).astype(BF16)
 
 
-def first_kernel(fc_hbm, out_hbm, qkv_hbm, res_hbm, cot_hbm, o_ref, rest_ref, fc_ref, out_ref, qkv_ref, sem):
+def first_kernel(
+    fc_hbm, out_hbm, qkv_hbm, res_hbm, cot_hbm, q_hbm, k_hbm, v_hbm, turn_ref,
+    o_ref, rest_ref, send_ref, fc_ref, out_ref, qkv_ref, time_ref, sem,
+):
     width = res_hbm.shape[-1]
     copies = [
         pltpu.make_async_copy(res_hbm.at[0], rest_ref.at[:, :, pl.ds(0, width)], sem.at[0]),
@@ -86,9 +89,11 @@
         pltpu.make_async_copy(out_hbm, out_ref, sem.at[3]),
         pltpu.make_async_copy(qkv_hbm, qkv_ref, sem.at[4]),
     ]
-    for c in copies:
+    for j, src in enumerate((q_hbm, k_hbm, v_hbm)):
+        copies.append(pltpu.make_async_copy(src.at[0], time_ref.at[j], sem.at[5 + j]))
+    for c in copies[2:] + copies[:2]:
         c.start()
-    for c in copies[2:]:
+    for c in copies[2:5]:
         c.wait()
     both = jnp.concatenate([fc_ref[...].astype(F32), out_ref[...].astype(F32)], axis=0)
     tail = both[:, 768:]
@@ -98,6 +103,13 @@
         [both[:, :768], tail, qkv[:, :768], qkv[:, 768:1536], qkv[:, 1536:]], axis=0
     )
     o_ref[...] = jnp.broadcast_to(block[None], o_ref.shape).astype(BF16)
+    steps, tubes, inner = time_ref.shape[1:]
+    parts = []
+    for j in range(3):
+        copies[5 + j].wait()
+        turned = nn(turn_ref[...], time_ref[j].reshape(steps * tubes, inner))
+        parts.append(turned.reshape(tubes, steps, inner))
+    send_ref[...] = jnp.concatenate(parts, axis=1).astype(BF16)
     for c in copies[:2]:
         c.wait()
 
@@ -115,16 +127,6 @@
         part += nn(rest_order(tm, j, 1), fo[:, 256:512])
         part += nn(rest_order(tm, j, 2), fo[:, 512:])
         o_ref[pl.ds(3 * n + 12 * tm, 4 * tm), pl.ds(j * 256, 256)] = part.astype(BF16)
-
-
-def pack_kernel(q_ref, k_ref, v_ref, turn_ref, o_ref):
-    steps, tubes, inner = q_ref.shape[1:]
-    rows = steps * tubes
-    parts = [
-        nn(turn_ref[...], ref[0].reshape(rows, inner)).reshape(tubes, steps, inner)
-        for ref in (q_ref, k_ref, v_ref)
-    ]
-    o_ref[...] = jnp.concatenate(parts, axis=1).astype(BF16)
 
 
 def unpack_kernel(x_ref, turn_ref, gr_ref, gr_out, *outs):
@@ -345,32 +347,37 @@
     to_steps = jnp.asarray(transposed_rows(tubes, steps))
     to_order = jnp.asarray(transposed_rows(tm, sp))
     me = lax.axis_index("space").astype(jnp.int32).reshape(1)
-    shards, rest = pl.pallas_call(
+    shards, rest, send = pl.pallas_call(
         first_kernel,
-        out_shape=(shape((tm, 40, inner), BF16), shape((steps, tubes, 2 * width), BF16)),
-        in_specs=[HBM] * 5,
-        out_specs=(VMEM, VMEM),
+        out_shape=(
+            shape((tm, 40, inner), BF16),
+            shape((steps, tubes, 2 * width), BF16),
+            shape((tubes, 3 * steps, inner), BF16),
+        ),
+        in_specs=[HBM] * 8 + [VMEM],
+        out_specs=(VMEM,) * 3,
         scratch_shapes=[
             pltpu.VMEM(fc_weight.shape, BF16),
             pltpu.VMEM(out_weight.shape, BF16),
             pltpu.VMEM(qkv_weight.shape, BF16),
-            pltpu.SemaphoreType.DMA((5,)),
+            pltpu.VMEM((3, steps, tubes, inner), BF16),
+            pltpu.SemaphoreType.DMA((8,)),
         ],
         compiler_params=params(56),
         name="first",
-    )(fc_weight, out_weight, qkv_weight, residual_in, cotangent)
+    )(
+        fc_weight,
+        out_weight,
+        qkv_weight,
+        residual_in,
+        cotangent,
+        time_query,
+        time_key,
+        time_value,
+        to_tubes,
+    )
     rest = lax.all_gather(rest, "space", axis=0)
     shards = exchange(shards, "tm")
-
-    send = pl.pallas_call(
-        pack_kernel,
-        out_shape=shape((tubes, 3 * steps, inner), BF16),
-        in_specs=[VMEM] * 4,
-        out_specs=VMEM,
-        compiler_params=params(16),
-        cost_estimate=pl.CostEstimate(flops=10**9, bytes_accessed=4 * 10**6, transcendentals=0),
-        name="pack",
-    )(time_query, time_key, time_value, to_tubes)
 
     shards = pl.pallas_call(
         weights_unpack_kernel,
@@ -414,7 +421,7 @@
             pltpu.VMEM((total, 3 * inner), BF16),
             pltpu.SemaphoreType.DMA((12,)),
         ],
-        compiler_params=params(56),
+        compiler_params=params(52),
         cost_estimate=pl.CostEstimate(flops=4 * 10**9, bytes_accessed=10**7, transcendentals=2 * 10**5),
         name="middle",
     )(

time: 202 us -> 202 us (level)
  local copies, waits for them, and re-layouts: 4.98 us -> 0.13 us
  blocking collectives: 128 us -> 132 us
    unnamed x14 -> x8, local copies, waits for them, and re-layouts: 4.24 us -> 0.02 us
    all_to_all x4, blocking collectives: 128 us -> 132 us  [exchange(): return lax.all_to_all(x, axes, split_axis=0, concat_axis=0, tiled=True)]
where the time goes in v9:
time: 202 us; the launch traced here: 201 us
  blocking collectives  132 us (65%)
  Pallas kernels  22.2 us (11%)
  waiting for transfers between devices  21.2 us (10%)
  between operations  14.1 us (7%)
  starting transfers between devices  11.8 us (6%)
    all_to_all x4, blocking collectives, exchange(): return lax.all_to_all(x, axes, split_axis=0, concat_axis=0, tiled=True)  132 us
    all_to_all x2, waiting for transfers between devices, exchange(): return lax.all_to_all(x, axes, split_axis=0, concat_axis=0, tiled=True)  21.2 us
    all_to_all x2, starting transfers between devices, exchange(): return lax.all_to_all(x, axes, split_axis=0, concat_axis=0, tiled=True)  11.7 us
    pallas_call x1, Pallas kernels, body(): pl.pallas_call(middle_kernel, out_shape=(shape((total, width), BF16), sha...  11.3 us
  transfers between devices with their start and end apart: 4, of which 2 were waited for; matrix products, arithmetic and copies ran while one was open for 0% of the time, Pallas kernels for 3%

profile of v9, /device:TPU:8, one launch (start us, length us, event | category | flops | bytes accessed | tf_op | source)
XLA Modules:
  0.0 201.2 jit_solution(17927066999665654312)
XLA Ops:
  7.2 0.0 copy-start
  7.2 0.0 copy-start.1
  7.2 0.0 copy-start.2
  7.2 0.0 copy-start.3
  7.2 0.0 all-gather.7.cloned.1.call-start
  7.3 3.8 %first.1 = (bf16[16,40,768]{2,1,0:T(8,128)(2,1)}, bf16[8,16,2048]{2,1,0:T(8,128)(2,1)}, bf16[16,24,768]{2,1,0:T(8,128)(2,1)}) custom-call(bf16[6,1024]{1,0:T(8,128)(2,1)} %fc_hbm.1, bf16[6,1024]{1,0:T(8,128)(2,1)} %out_hbm.1, bf16[8,2304]{1,0:T(8,128)(2,1)} %qkv_hbm.1, bf16[1,8,16,1024]{3,2,1,0:T(8,128)(2,1)} %res_hbm.1, bf16[1,8,16,1024]{3,2,1,0:T(8,128)(2,1)} %cot_hbm.1, ...), custom_call_target="tpu_custom_call" | custom-call | tf_op jit(solution)/shard_map/first/pallas_call | solution.py:350
  11.1 0.0 all-gather.7.cloned.1.call-update
  11.1 0.0 all-gather.5.cloned.1.call-start
  11.1 46.1 %all_to_all.30.x_ref = bf16[16,40,768]{2,1,0:T(8,128)(2,1)S(1)} all-to-all(bf16[16,40,768]{2,1,0:T(8,128)(2,1)} %get-tuple-element.17), channel_id=1, replica_groups=mesh['tm'=16,'space'=8,'dp'=4] {'tm'}, dimensions={0} | all-to-all | bytes 1966080 | tf_op jit(solution)/shard_map/all_to_all | solution.py:344
  57.2 1.4 weights_unpack.1
  58.7 0.0 all-gather.5.cloned.1.call-update
  58.7 27.0 %all_to_all.31.x_ref = bf16[16,24,768]{2,1,0:T(8,128)(2,1)S(1)} all-to-all(bf16[16,24,768]{2,1,0:T(8,128)(2,1)} %get-tuple-element.18), channel_id=1, replica_groups=mesh['tm'=16,'space'=8,'dp'=4] {'tm'}, dimensions={0} | all-to-all | bytes 1179648 | tf_op jit(solution)/shard_map/all_to_all | solution.py:344
  85.7 1.8 temporal_forward.1
  87.5 8.3 %all-to-all-start.2 = ((bf16[128,6,128]{2,1,0:T(8,128)(2,1)}), bf16[128,6,128]{2,1,0:T(8,128)(2,1)S(1)}, u32[]{:S(2)}, u32[]{:S(2)}) async-start(bf16[128,6,128]{2,1,0:T(8,128)(2,1)} %temporal_forward.1), calls=%async_computation.2 | async-start | bytes 524288 | tf_op jit(solution)/shard_map/all_to_all | solution.py:344
  95.9 0.1 copy.19.row_ref
  96.0 16.5 %all-to-all-done.2.x_ref = bf16[128,6,128]{2,1,0:T(8,128)(2,1)S(1)} async-done(((bf16[128,6,128]{2,1,0:T(8,128)(2,1)}), bf16[128,6,128]{2,1,0:T(8,128)(2,1)S(1)}, u32[]{:S(2)}, u32[]{:S(2)}) %all-to-all-start.2) | async-done | bytes 196640 | tf_op jit(solution)/shard_map/all_to_all | solution.py:344
  112.5 11.3 %middle.1 = (bf16[128,1024]{1,0:T(8,128)(2,1)}, bf16[128,6,128]{2,1,0:T(8,128)(2,1)S(1)}) custom-call(s32[1]{0:T(128)} %bitcast.me_ref, bf16[8,640,768]{2,1,0:T(8,128)(2,1)} %bitcast.8, bf16[128,6,128]{2,1,0:T(8,128)(2,1)S(1)} %all-to-all-done.2.x_ref, bf16[8,8,16,2048]{3,2,1,0:T(8,128)(2,1)} %bitcast.9, f32[1,1024]{1,0:T(1,128)S(1)} %bitcast.7, ...), custom_call_target="tpu_custom_call" | custom-call | flops 4000000000 | bytes 10000000 | tf_op jit(solution)/shard_map/middle/pallas_call | solution.py:407
  123.8 31.9 %all_to_all.32.g_ref = bf16[128,6,128]{2,1,0:T(8,128)(2,1)S(1)} all-to-all(bf16[128,6,128]{2,1,0:T(8,128)(2,1)S(1)} %get-tuple-element.23), channel_id=1, replica_groups=mesh['tm'=16,'space'=8,'dp'=4] {'tm','space'}, dimensions={0} | all-to-all | bytes 393216 | tf_op jit(solution)/shard_map/all_to_all | solution.py:344
  155.7 3.4 %all-to-all-start.4 = ((bf16[8,16,1024]{2,1,0:T(8,128)(2,1)}), bf16[8,16,1024]{2,1,0:T(8,128)(2,1)S(1)}, u32[]{:S(2)}, u32[]{:S(2)}) async-start(bf16[8,16,1024]{2,1,0:T(8,128)(2,1)} %bitcast.5), calls=%async_computation.4 | async-start | bytes 524288 | tf_op jit(solution)/shard_map/all_to_all | solution.py:344
  159.2 0.7 temporal_probs.1.p_ref
  159.9 2.0 %temporal_backward.1 = bf16[16,24,768]{2,1,0:T(8,128)(2,1)S(1)} custom-call(bf16[16,24,768]{2,1,0:T(8,128)(2,1)S(1)} %all_to_all.31.x_ref, f32[6,128,256]{2,1,0:T(8,128)S(1)} %temporal_probs.1.p_ref, bf16[128,6,128]{2,1,0:T(8,128)(2,1)S(1)} %all_to_all.32.g_ref), custom_call_target="tpu_custom_call" | custom-call | flops 300000000 | bytes 2000000 | tf_op jit(solution)/shard_map/temporal_backward/pallas_call | solution.py:452
  161.9 4.7 %all-to-all-done.4.gr_ref = bf16[8,16,1024]{2,1,0:T(8,128)(2,1)S(1)} async-done(((bf16[8,16,1024]{2,1,0:T(8,128)(2,1)}), bf16[8,16,1024]{2,1,0:T(8,128)(2,1)S(1)}, u32[]{:S(2)}, u32[]{:S(2)}) %all-to-all-start.4) | async-done | bytes 262176 | tf_op jit(solution)/shard_map/all_to_all | solution.py:344
  166.6 26.7 %all_to_all.33.x_ref = bf16[16,24,768]{2,1,0:T(8,128)(2,1)S(1)} all-to-all(bf16[16,24,768]{2,1,0:T(8,128)(2,1)S(1)} %temporal_backward.1), channel_id=1, replica_groups=mesh['tm'=16,'space'=8,'dp'=4] {'tm'}, dimensions={0} | all-to-all | bytes 1179648 | tf_op jit(solution)/shard_map/all_to_all | solution.py:344
  193.3 1.1 unpack.1
  (6 shorter events, 0.0 us)
Async XLA Ops:
  7.2 105.3 %copy-start = (bf16[128,128]{1,0:T(8,128)(2,1)S(1)}, bf16[128,128]{1,0:T(8,128)(2,1)}, u32[]{:S(2)}) copy-start(bf16[128,128]{1,0:T(8,128)(2,1)} %constant.11.clone.turn_ref) | copy-start | bytes 98308
  7.2 88.7 %copy-start.1 = (s32[1,128]{1,0:T(1,128)S(1)}, s32[1,128]{1,0:T(1,128)}, u32[]{:S(2)}) copy-start(s32[1,128]{1,0:T(1,128)} %col_ref.1) | copy-start | bytes 1540
  7.2 105.3 %copy-start.2 = (f32[1024]{0:T(1024)S(1)}, f32[1024]{0:T(1024)}, u32[]{:S(2)}) copy-start(f32[1024]{0:T(1024)} %param.19) | copy-start | bytes 12292
  7.2 105.3 %copy-start.3 = (f32[12]{0:T(128)S(1)}, f32[12]{0:T(128)}, u32[]{:S(2)}) copy-start(f32[12]{0:T(128)} %slope_ref.1) | copy-start | bytes 148
  7.2 105.2 %all-gather.7.cloned.1.call-start = ((), (), s32[]{:S(2)}) async-start(), calls=%async_computation.7 | async-start | bytes 4718592 | tf_op jit(solution)/shard_map/all_gather | solution.py:379
  11.1 101.4 %all-gather.5.cloned.1.call-start = ((), (), s32[]{:S(2)}) async-start(), calls=%async_computation.6 | async-start | bytes 8847360 | tf_op jit(solution)/shard_map/all_gather | solution.py:390
  87.5 24.9 %all-to-all-start.2 = ((bf16[128,6,128]{2,1,0:T(8,128)(2,1)}), bf16[128,6,128]{2,1,0:T(8,128)(2,1)S(1)}, u32[]{:S(2)}, u32[]{:S(2)}) async-start(bf16[128,6,128]{2,1,0:T(8,128)(2,1)} %temporal_forward.1), calls=%async_computation.2 | async-start | bytes 524288 | tf_op jit(solution)/shard_map/all_to_all | solution.py:344
  155.7 10.9 %all-to-all-start.4 = ((bf16[8,16,1024]{2,1,0:T(8,128)(2,1)}), bf16[8,16,1024]{2,1,0:T(8,128)(2,1)S(1)}, u32[]{:S(2)}, u32[]{:S(2)}) async-start(bf16[8,16,1024]{2,1,0:T(8,128)(2,1)} %bitcast.5), calls=%async_computation.4 | async-start | bytes 524288 | tf_op jit(solution)/shard_map/all_to_all | solution.py:344
Sparse Core Ops, SparseCore 0:
  11.2 41.9 all-gather.6
  58.8 51.3 all-gather.4

commit v10 on v7

--- a/solution.py
+++ b/solution.py
@@ -421,7 +421,7 @@
             pltpu.VMEM((total, 3 * inner), BF16),
             pltpu.SemaphoreType.DMA((12,)),
         ],
-        compiler_params=params(56),
+        compiler_params=params(52),
         cost_estimate=pl.CostEstimate(flops=4 * 10**9, bytes_accessed=10**7, transcendentals=2 * 10**5),
         name="middle",
     )(

time: 198 us -> 197 us (level)
  no operation moved by 1% of the time
where the time goes in v10:
time: 197 us
  blocking collectives  72.9 us (37%)
  waiting for transfers between devices  55.3 us (28%)
  starting transfers between devices  30.2 us (15%)
  Pallas kernels  24.2 us (12%)
  between operations  13.9 us (7%)
    all_to_all x2, blocking collectives, exchange(): return lax.all_to_all(x, axes, split_axis=0, concat_axis=0, tiled=True)  72.9 us
    all_to_all x3, waiting for transfers between devices, exchange(): return lax.all_to_all(x, axes, split_axis=0, concat_axis=0, tiled=True)  55.2 us
    all_to_all x3, starting transfers between devices, exchange(): return lax.all_to_all(x, axes, split_axis=0, concat_axis=0, tiled=True)  30.1 us
    pallas_call x1, Pallas kernels, body(): pl.pallas_call(middle_kernel, out_shape=(shape((total, width), BF16), sha...  12 us
  transfers between devices with their start and end apart: 6, of which 3 were waited for; matrix products, arithmetic and copies ran while one was open for 0% of the time, Pallas kernels for 4%

profile of v10, /device:TPU:8, one launch (start us, length us, event | category | flops | bytes accessed | tf_op | source)
XLA Modules:
  0.0 196.6 jit_solution(2136912838537743622)
XLA Ops:
  7.2 0.0 all-gather.9.cloned.1.call-start
  7.3 2.4 %first.1 = (bf16[16,40,768]{2,1,0:T(8,128)(2,1)}, bf16[8,16,2048]{2,1,0:T(8,128)(2,1)}) custom-call(bf16[6,1024]{1,0:T(8,128)(2,1)} %fc_hbm.1, bf16[6,1024]{1,0:T(8,128)(2,1)} %out_hbm.1, bf16[8,2304]{1,0:T(8,128)(2,1)} %qkv_hbm.1, bf16[1,8,16,1024]{3,2,1,0:T(8,128)(2,1)} %res_hbm.1, bf16[1,8,16,1024]{3,2,1,0:T(8,128)(2,1)} %cot_hbm.1), custom_call_target="tpu_custom_call" | custom-call | tf_op jit(solution)/shard_map/first/pallas_call | solution.py:355
  9.6 0.0 all-gather.9.cloned.1.call-update
  9.6 0.0 all-gather.7.cloned.1.call-start
  9.7 46.1 %all_to_all.25.x_ref = bf16[16,40,768]{2,1,0:T(8,128)(2,1)S(1)} all-to-all(bf16[16,40,768]{2,1,0:T(8,128)(2,1)} %get-tuple-element.16), channel_id=1, replica_groups=mesh['tm'=16,'space'=8,'dp'=4] {'tm'}, dimensions={0} | all-to-all | bytes 1966080 | tf_op jit(solution)/shard_map/all_to_all | solution.py:349
  55.8 1.4 weights_unpack.1
  57.2 0.0 all-gather.7.cloned.1.call-update
  57.3 0.3 pack.1
  57.6 26.8 %all_to_all.26.x_ref = bf16[16,24,768]{2,1,0:T(8,128)(2,1)S(1)} all-to-all(bf16[16,24,768]{2,1,0:T(8,128)(2,1)S(1)} %pack.1), channel_id=1, replica_groups=mesh['tm'=16,'space'=8,'dp'=4] {'tm'}, dimensions={0} | all-to-all | bytes 1179648 | tf_op jit(solution)/shard_map/all_to_all | solution.py:349
  84.4 1.8 temporal_forward.1
  86.2 8.3 %all-to-all-start.2 = ((bf16[128,6,128]{2,1,0:T(8,128)(2,1)}), bf16[128,6,128]{2,1,0:T(8,128)(2,1)S(1)}, u32[]{:S(2)}, u32[]{:S(2)}) async-start(bf16[128,6,128]{2,1,0:T(8,128)(2,1)} %temporal_forward.1), calls=%async_computation.2 | async-start | bytes 524288 | tf_op jit(solution)/shard_map/all_to_all | solution.py:349
  94.6 0.0 all-gather.11.cloned.1.call-start
  94.6 0.1 copy.19.row_ref
  94.8 16.4 %all-to-all-done.2.x_ref = bf16[128,6,128]{2,1,0:T(8,128)(2,1)S(1)} async-done(((bf16[128,6,128]{2,1,0:T(8,128)(2,1)}), bf16[128,6,128]{2,1,0:T(8,128)(2,1)S(1)}, u32[]{:S(2)}, u32[]{:S(2)}) %all-to-all-start.2) | async-done | bytes 196640 | tf_op jit(solution)/shard_map/all_to_all | solution.py:349
  111.2 12.0 %middle.1 = (bf16[128,1024]{1,0:T(8,128)(2,1)}, bf16[128,6,128]{2,1,0:T(8,128)(2,1)}) custom-call(s32[1]{0:T(128)} %bitcast.me_ref, bf16[8,640,768]{2,1,0:T(8,128)(2,1)} %bitcast.8, bf16[128,6,128]{2,1,0:T(8,128)(2,1)S(1)} %all-to-all-done.2.x_ref, bf16[8,8,16,2048]{3,2,1,0:T(8,128)(2,1)} %bitcast.9, f32[1,1024]{1,0:T(1,128)S(1)} %bitcast.7, ...), custom_call_target="tpu_custom_call" | custom-call | flops 4000000000 | bytes 10000000 | tf_op jit(solution)/shard_map/middle/pallas_call | solution.py:407
  123.3 0.0 all-gather.11.cloned.1.call-update
  123.3 14.0 %all-to-all-start.3 = ((bf16[128,6,128]{2,1,0:T(8,128)(2,1)}), bf16[128,6,128]{2,1,0:T(8,128)(2,1)S(1)}, u32[]{:S(2)}, u32[]{:S(2)}) async-start(bf16[128,6,128]{2,1,0:T(8,128)(2,1)} %get-tuple-element.21), calls=%async_computation.3 | async-start | bytes 524288 | tf_op jit(solution)/shard_map/all_to_all | solution.py:349
  137.2 0.7 temporal_probs.1.p_ref
  137.9 17.7 %all-to-all-done.3.g_ref = bf16[128,6,128]{2,1,0:T(8,128)(2,1)S(1)} async-done(((bf16[128,6,128]{2,1,0:T(8,128)(2,1)}), bf16[128,6,128]{2,1,0:T(8,128)(2,1)S(1)}, u32[]{:S(2)}, u32[]{:S(2)}) %all-to-all-start.3) | async-done | bytes 196640 | tf_op jit(solution)/shard_map/all_to_all | solution.py:349
  155.7 2.9 %temporal_backward.1 = bf16[16,24,768]{2,1,0:T(8,128)(2,1)} custom-call(bf16[16,24,768]{2,1,0:T(8,128)(2,1)S(1)} %all_to_all.26.x_ref, f32[6,128,256]{2,1,0:T(8,128)S(1)} %temporal_probs.1.p_ref, bf16[128,6,128]{2,1,0:T(8,128)(2,1)S(1)} %all-to-all-done.3.g_ref), custom_call_target="tpu_custom_call" | custom-call | flops 300000000 | bytes 2000000 | tf_op jit(solution)/shard_map/temporal_backward/pallas_call | solution.py:451
  158.5 7.8 %all-to-all-start.4 = ((bf16[16,24,768]{2,1,0:T(8,128)(2,1)}), bf16[16,24,768]{2,1,0:T(8,128)(2,1)S(1)}, u32[]{:S(2)}, u32[]{:S(2)}) async-start(bf16[16,24,768]{2,1,0:T(8,128)(2,1)} %temporal_backward.1), calls=%async_computation.4 | async-start | bytes 1179648 | tf_op jit(solution)/shard_map/all_to_all | solution.py:349
  166.3 1.7 slice.1
  168.0 21.1 %all-to-all-done.4.x_ref = bf16[16,24,768]{2,1,0:T(8,128)(2,1)S(1)} async-done(((bf16[16,24,768]{2,1,0:T(8,128)(2,1)}), bf16[16,24,768]{2,1,0:T(8,128)(2,1)S(1)}, u32[]{:S(2)}, u32[]{:S(2)}) %all-to-all-start.4) | async-done | bytes 589856 | tf_op jit(solution)/shard_map/all_to_all | solution.py:349
  189.1 1.0 unpack.1
  (19 shorter events, 0.0 us)
Async XLA Ops:
  7.2 50.1 %copy-start.7 = (bf16[128,128]{1,0:T(8,128)(2,1)S(1)}, bf16[128,128]{1,0:T(8,128)(2,1)}, u32[]{:S(2)}) copy-start(bf16[128,128]{1,0:T(8,128)(2,1)} %constant.10.clone.turn_ref) | copy-start | bytes 98308
  7.2 50.1 %copy-start.2 = (bf16[1,8,16,768]{3,2,1,0:T(8,128)(2,1)S(1)}, bf16[1,8,16,768]{3,2,1,0:T(8,128)(2,1)}, u32[]{:S(2)}) copy-start(bf16[1,8,16,768]{3,2,1,0:T(8,128)(2,1)} %q_ref.1) | copy-start | bytes 589828
  7.2 50.1 %copy-start.3 = (bf16[1,8,16,768]{3,2,1,0:T(8,128)(2,1)S(1)}, bf16[1,8,16,768]{3,2,1,0:T(8,128)(2,1)}, u32[]{:S(2)}) copy-start(bf16[1,8,16,768]{3,2,1,0:T(8,128)(2,1)} %k_ref.1) | copy-start | bytes 589828
  7.2 50.1 %copy-start.4 = (bf16[1,8,16,768]{3,2,1,0:T(8,128)(2,1)S(1)}, bf16[1,8,16,768]{3,2,1,0:T(8,128)(2,1)}, u32[]{:S(2)}) copy-start(bf16[1,8,16,768]{3,2,1,0:T(8,128)(2,1)} %v_ref.1) | copy-start | bytes 589828
  7.2 104.0 %all-gather.9.cloned.1.call-start = ((), (), s32[]{:S(2)}) async-start(), calls=%async_computation.6 | async-start | bytes 4718592 | tf_op jit(solution)/shard_map/all_gather | solution.py:369
  9.6 101.6 %all-gather.7.cloned.1.call-start = ((), (), s32[]{:S(2)}) async-start(), calls=%async_computation.5 | async-start | bytes 8847360 | tf_op jit(solution)/shard_map/all_gather | solution.py:390
  55.8 38.8 %copy-start.1 = (s32[1,128]{1,0:T(1,128)S(1)}, s32[1,128]{1,0:T(1,128)}, u32[]{:S(2)}) copy-start(s32[1,128]{1,0:T(1,128)} %col_ref.1) | copy-start | bytes 1540
  55.8 55.4 %copy-start = (bf16[128,128]{1,0:T(8,128)(2,1)S(1)}, bf16[128,128]{1,0:T(8,128)(2,1)}, u32[]{:S(2)}) copy-start(bf16[128,128]{1,0:T(8,128)(2,1)} %constant.11.clone.turn_ref) | copy-start | bytes 98308
  55.8 55.4 %copy-start.5 = (f32[1024]{0:T(1024)S(1)}, f32[1024]{0:T(1024)}, u32[]{:S(2)}) copy-start(f32[1024]{0:T(1024)} %param.19) | copy-start | bytes 12292
  55.8 55.4 %copy-start.6 = (f32[12]{0:T(128)S(1)}, f32[12]{0:T(128)}, u32[]{:S(2)}) copy-start(f32[12]{0:T(128)} %slope_ref.1) | copy-start | bytes 148
  86.2 25.0 %all-to-all-start.2 = ((bf16[128,6,128]{2,1,0:T(8,128)(2,1)}), bf16[128,6,128]{2,1,0:T(8,128)(2,1)S(1)}, u32[]{:S(2)}, u32[]{:S(2)}) async-start(bf16[128,6,128]{2,1,0:T(8,128)(2,1)} %temporal_forward.1), calls=%async_computation.2 | async-start | bytes 524288 | tf_op jit(solution)/shard_map/all_to_all | solution.py:349
  94.6 64.0 %all-gather.11.cloned.1.call-start = ((), (), s32[]{:S(2)}) async-start(), calls=%async_computation.7 | async-start | bytes 2359296 | tf_op jit(solution)/shard_map/all_gather | solution.py:438
  123.3 32.4 %all-to-all-start.3 = ((bf16[128,6,128]{2,1,0:T(8,128)(2,1)}), bf16[128,6,128]{2,1,0:T(8,128)(2,1)S(1)}, u32[]{:S(2)}, u32[]{:S(2)}) async-start(bf16[128,6,128]{2,1,0:T(8,128)(2,1)} %get-tuple-element.21), calls=%async_computation.3 | async-start | bytes 524288 | tf_op jit(solution)/shard_map/all_to_all | solution.py:349
  158.5 30.5 %all-to-all-start.4 = ((bf16[16,24,768]{2,1,0:T(8,128)(2,1)}), bf16[16,24,768]{2,1,0:T(8,128)(2,1)S(1)}, u32[]{:S(2)}, u32[]{:S(2)}) async-start(bf16[16,24,768]{2,1,0:T(8,128)(2,1)} %temporal_backward.1), calls=%async_computation.4 | async-start | bytes 1179648 | tf_op jit(solution)/shard_map/all_to_all | solution.py:349
Sparse Core Ops, SparseCore 0:
  10.2 41.9 all-gather.8
  57.4 51.7 all-gather.6
  123.4 30.8 all-gather.10

commit v11 on v10

--- a/solution.py
+++ b/solution.py
@@ -77,18 +77,15 @@
     return jnp.where(column == source, 1.0, 0.0).astype(BF16)
 
 
-def first_kernel(fc_hbm, out_hbm, qkv_hbm, res_hbm, cot_hbm, o_ref, rest_ref, fc_ref, out_ref, qkv_ref, sem):
-    width = res_hbm.shape[-1]
+def first_kernel(fc_hbm, out_hbm, qkv_hbm, o_ref, fc_ref, out_ref, qkv_ref, sem):
     copies = [
-        pltpu.make_async_copy(res_hbm.at[0], rest_ref.at[:, :, pl.ds(0, width)], sem.at[0]),
-        pltpu.make_async_copy(cot_hbm.at[0], rest_ref.at[:, :, pl.ds(width, width)], sem.at[1]),
-        pltpu.make_async_copy(fc_hbm, fc_ref, sem.at[2]),
-        pltpu.make_async_copy(out_hbm, out_ref, sem.at[3]),
-        pltpu.make_async_copy(qkv_hbm, qkv_ref, sem.at[4]),
+        pltpu.make_async_copy(fc_hbm, fc_ref, sem.at[0]),
+        pltpu.make_async_copy(out_hbm, out_ref, sem.at[1]),
+        pltpu.make_async_copy(qkv_hbm, qkv_ref, sem.at[2]),
     ]
     for c in copies:
         c.start()
-    for c in copies[2:]:
+    for c in copies:
         c.wait()
     both = jnp.concatenate([fc_ref[...].astype(F32), out_ref[...].astype(F32)], axis=0)
     tail = both[:, 768:]
@@ -98,8 +95,6 @@
         [both[:, :768], tail, qkv[:, :768], qkv[:, 768:1536], qkv[:, 1536:]], axis=0
     )
     o_ref[...] = jnp.broadcast_to(block[None], o_ref.shape).astype(BF16)
-    for c in copies[:2]:
-        c.wait()
 
 
 def weights_unpack_kernel(x_ref, o_ref):
@@ -352,20 +347,22 @@
     to_steps = jnp.asarray(transposed_rows(tubes, steps))
     to_order = jnp.asarray(transposed_rows(tm, sp))
     me = lax.axis_index("space").astype(jnp.int32).reshape(1)
-    shards, rest = pl.pallas_call(
+    rest = jnp.concatenate([residual_in[0], cotangent[0]], axis=-1)
+    rest, fc_weight = lax.optimization_barrier((rest, fc_weight))
+    shards = pl.pallas_call(
         first_kernel,
-        out_shape=(shape((tm, 40, inner), BF16), shape((steps, tubes, 2 * width), BF16)),
-        in_specs=[HBM] * 5,
-        out_specs=(VMEM, VMEM),
+        out_shape=shape((tm, 40, inner), BF16),
+        in_specs=[HBM] * 3,
+        out_specs=VMEM,
         scratch_shapes=[
             pltpu.VMEM(fc_weight.shape, BF16),
             pltpu.VMEM(out_weight.shape, BF16),
             pltpu.VMEM(qkv_weight.shape, BF16),
-            pltpu.SemaphoreType.DMA((5,)),
+            pltpu.SemaphoreType.DMA((3,)),
         ],
         compiler_params=params(56),
         name="first",
-    )(fc_weight, out_weight, qkv_weight, residual_in, cotangent)
+    )(fc_weight, out_weight, qkv_weight)
     rest = lax.all_gather(rest, "space", axis=0)
     shards = exchange(shards, "tm")
 

time: 197 us -> 197 us (level)
  other arithmetic: 0 us -> 2.01 us
    concatenate x0 -> x1, other arithmetic: none -> 2.01 us  [body(): rest = jnp.concatenate([residual_in[0], cotangent[0]], axis=-1)]
  transfers between devices with their start and end apart: 6 -> 6, of which waited for: 3 -> 3; matrix products, arithmetic and copies ran while one was open for 0% -> 0% of each run, Pallas kernels for 4% -> 5%
where the time goes in v11:
time: 197 us
  blocking collectives  72.9 us (37%)
  waiting for transfers between devices  55.3 us (28%)
  starting transfers between devices  28.7 us (15%)
  Pallas kernels  23.7 us (12%)
  between operations  13.9 us (7%)
  other arithmetic  2.01 us (1%)
    all_to_all x2, blocking collectives, exchange(): return lax.all_to_all(x, axes, split_axis=0, concat_axis=0, tiled=True)  72.9 us
    all_to_all x3, waiting for transfers between devices, exchange(): return lax.all_to_all(x, axes, split_axis=0, concat_axis=0, tiled=True)  55.2 us
    all_to_all x3, starting transfers between devices, exchange(): return lax.all_to_all(x, axes, split_axis=0, concat_axis=0, tiled=True)  28.5 us
    pallas_call x1, Pallas kernels, body(): pl.pallas_call(middle_kernel, out_shape=(shape((total, width), BF16), sha...  12 us
  transfers between devices with their start and end apart: 6, of which 3 were waited for; matrix products, arithmetic and copies ran while one was open for 0% of the time, Pallas kernels for 5%

profile of v11, /device:TPU:8, one launch (start us, length us, event | category | flops | bytes accessed | tf_op | source)
XLA Modules:
  0.0 196.6 jit_solution(4679462556893818650)
XLA Ops:
  7.2 0.0 all-gather.9.cloned.1.call-start
  7.3 2.0 %pad_maximum_fusion = bf16[8,16,2048]{2,1,0:T(8,128)(2,1)} fusion(bf16[8,16,1024]{2,1,0:T(8,128)(2,1)} %bitcast.10, bf16[8,16,1024]{2,1,0:T(8,128)(2,1)} %bitcast.11), kind=kLoop, calls=%fused_computation | loop fusion | flops 1048576 | bytes 1048576 | tf_op jit(solution)/shard_map/concatenate | solution.py:350
  9.3 0.0 all-gather.9.cloned.1.call-update
  9.3 0.0 all-gather.7.cloned.1.call-start
  9.3 1.9 first.1
  11.2 46.1 %all_to_all.25.x_ref = bf16[16,40,768]{2,1,0:T(8,128)(2,1)S(1)} all-to-all(bf16[16,40,768]{2,1,0:T(8,128)(2,1)} %first.1), channel_id=1, replica_groups=mesh['tm'=16,'space'=8,'dp'=4] {'tm'}, dimensions={0} | all-to-all | bytes 1966080 | tf_op jit(solution)/shard_map/all_to_all | solution.py:344
  57.3 1.4 weights_unpack.1
  58.8 0.3 pack.1
  59.1 26.8 %all_to_all.26.x_ref = bf16[16,24,768]{2,1,0:T(8,128)(2,1)S(1)} all-to-all(bf16[16,24,768]{2,1,0:T(8,128)(2,1)S(1)} %pack.1), channel_id=1, replica_groups=mesh['tm'=16,'space'=8,'dp'=4] {'tm'}, dimensions={0} | all-to-all | bytes 1179648 | tf_op jit(solution)/shard_map/all_to_all | solution.py:344
  85.9 1.8 temporal_forward.1
  87.7 8.3 %all-to-all-start.2 = ((bf16[128,6,128]{2,1,0:T(8,128)(2,1)}), bf16[128,6,128]{2,1,0:T(8,128)(2,1)S(1)}, u32[]{:S(2)}, u32[]{:S(2)}) async-start(bf16[128,6,128]{2,1,0:T(8,128)(2,1)} %temporal_forward.1), calls=%async_computation.2 | async-start | bytes 524288 | tf_op jit(solution)/shard_map/all_to_all | solution.py:344
  96.1 0.0 all-gather.11.cloned.1.call-start
  96.1 0.1 copy.19.row_ref
  96.3 16.4 %all-to-all-done.2.x_ref = bf16[128,6,128]{2,1,0:T(8,128)(2,1)S(1)} async-done(((bf16[128,6,128]{2,1,0:T(8,128)(2,1)}), bf16[128,6,128]{2,1,0:T(8,128)(2,1)S(1)}, u32[]{:S(2)}, u32[]{:S(2)}) %all-to-all-start.2) | async-done | bytes 196640 | tf_op jit(solution)/shard_map/all_to_all | solution.py:344
  112.7 12.0 %middle.1 = (bf16[128,1024]{1,0:T(8,128)(2,1)}, bf16[128,6,128]{2,1,0:T(8,128)(2,1)}) custom-call(s32[1]{0:T(128)} %bitcast.me_ref, bf16[8,640,768]{2,1,0:T(8,128)(2,1)} %bitcast.12, bf16[128,6,128]{2,1,0:T(8,128)(2,1)S(1)} %all-to-all-done.2.x_ref, bf16[8,8,16,2048]{3,2,1,0:T(8,128)(2,1)} %bitcast.13, f32[1,1024]{1,0:T(1,128)S(1)} %bitcast.9, ...), custom_call_target="tpu_custom_call" | custom-call | flops 4000000000 | bytes 10000000 | tf_op jit(solution)/shard_map/middle/pallas_call | solution.py:404
  124.8 0.0 all-gather.11.cloned.1.call-update
  124.8 12.5 %all-to-all-start.3 = ((bf16[128,6,128]{2,1,0:T(8,128)(2,1)}), bf16[128,6,128]{2,1,0:T(8,128)(2,1)S(1)}, u32[]{:S(2)}, u32[]{:S(2)}) async-start(bf16[128,6,128]{2,1,0:T(8,128)(2,1)} %get-tuple-element.21), calls=%async_computation.3 | async-start | bytes 524288 | tf_op jit(solution)/shard_map/all_to_all | solution.py:344
  137.2 0.7 temporal_probs.1.p_ref
  138.0 17.7 %all-to-all-done.3.g_ref = bf16[128,6,128]{2,1,0:T(8,128)(2,1)S(1)} async-done(((bf16[128,6,128]{2,1,0:T(8,128)(2,1)}), bf16[128,6,128]{2,1,0:T(8,128)(2,1)S(1)}, u32[]{:S(2)}, u32[]{:S(2)}) %all-to-all-start.3) | async-done | bytes 196640 | tf_op jit(solution)/shard_map/all_to_all | solution.py:344
  155.7 2.9 %temporal_backward.1 = bf16[16,24,768]{2,1,0:T(8,128)(2,1)} custom-call(bf16[16,24,768]{2,1,0:T(8,128)(2,1)S(1)} %all_to_all.26.x_ref, f32[6,128,256]{2,1,0:T(8,128)S(1)} %temporal_probs.1.p_ref, bf16[128,6,128]{2,1,0:T(8,128)(2,1)S(1)} %all-to-all-done.3.g_ref), custom_call_target="tpu_custom_call" | custom-call | flops 300000000 | bytes 2000000 | tf_op jit(solution)/shard_map/temporal_backward/pallas_call | solution.py:448
  158.5 7.8 %all-to-all-start.4 = ((bf16[16,24,768]{2,1,0:T(8,128)(2,1)}), bf16[16,24,768]{2,1,0:T(8,128)(2,1)S(1)}, u32[]{:S(2)}, u32[]{:S(2)}) async-start(bf16[16,24,768]{2,1,0:T(8,128)(2,1)} %temporal_backward.1), calls=%async_computation.4 | async-start | bytes 1179648 | tf_op jit(solution)/shard_map/all_to_all | solution.py:344
  166.3 1.7 slice.1
  168.0 21.1 %all-to-all-done.4.x_ref = bf16[16,24,768]{2,1,0:T(8,128)(2,1)S(1)} async-done(((bf16[16,24,768]{2,1,0:T(8,128)(2,1)}), bf16[16,24,768]{2,1,0:T(8,128)(2,1)S(1)}, u32[]{:S(2)}, u32[]{:S(2)}) %all-to-all-start.4) | async-done | bytes 589856 | tf_op jit(solution)/shard_map/all_to_all | solution.py:344
  189.1 1.0 unpack.1
  (20 shorter events, 0.1 us)
Async XLA Ops:
  7.2 51.6 %copy-start.7 = (bf16[128,128]{1,0:T(8,128)(2,1)S(1)}, bf16[128,128]{1,0:T(8,128)(2,1)}, u32[]{:S(2)}) copy-start(bf16[128,128]{1,0:T(8,128)(2,1)} %constant.10.clone.turn_ref) | copy-start | bytes 98308
  7.2 51.6 %copy-start.2 = (bf16[1,8,16,768]{3,2,1,0:T(8,128)(2,1)S(1)}, bf16[1,8,16,768]{3,2,1,0:T(8,128)(2,1)}, u32[]{:S(2)}) copy-start(bf16[1,8,16,768]{3,2,1,0:T(8,128)(2,1)} %q_ref.1) | copy-start | bytes 589828
  7.2 51.6 %copy-start.3 = (bf16[1,8,16,768]{3,2,1,0:T(8,128)(2,1)S(1)}, bf16[1,8,16,768]{3,2,1,0:T(8,128)(2,1)}, u32[]{:S(2)}) copy-start(bf16[1,8,16,768]{3,2,1,0:T(8,128)(2,1)} %k_ref.1) | copy-start | bytes 589828
  7.2 51.6 %copy-start.4 = (bf16[1,8,16,768]{3,2,1,0:T(8,128)(2,1)S(1)}, bf16[1,8,16,768]{3,2,1,0:T(8,128)(2,1)}, u32[]{:S(2)}) copy-start(bf16[1,8,16,768]{3,2,1,0:T(8,128)(2,1)} %v_ref.1) | copy-start | bytes 589828
  7.2 105.5 %all-gather.9.cloned.1.call-start = ((), (), s32[]{:S(2)}) async-start(), calls=%async_computation.6 | async-start | bytes 4718592 | tf_op jit(solution)/shard_map/all_gather | solution.py:366
  9.3 103.4 %all-gather.7.cloned.1.call-start = ((), (), s32[]{:S(2)}) async-start(), calls=%async_computation.5 | async-start | bytes 8847360 | tf_op jit(solution)/shard_map/all_gather | solution.py:387
  57.3 38.8 %copy-start.1 = (s32[1,128]{1,0:T(1,128)S(1)}, s32[1,128]{1,0:T(1,128)}, u32[]{:S(2)}) copy-start(s32[1,128]{1,0:T(1,128)} %col_ref.1) | copy-start | bytes 1540
  57.3 55.4 %copy-start = (bf16[128,128]{1,0:T(8,128)(2,1)S(1)}, bf16[128,128]{1,0:T(8,128)(2,1)}, u32[]{:S(2)}) copy-start(bf16[128,128]{1,0:T(8,128)(2,1)} %constant.11.clone.turn_ref) | copy-start | bytes 98308
  57.3 55.4 %copy-start.5 = (f32[1024]{0:T(1024)S(1)}, f32[1024]{0:T(1024)}, u32[]{:S(2)}) copy-start(f32[1024]{0:T(1024)} %param.19) | copy-start | bytes 12292
  57.3 55.4 %copy-start.6 = (f32[12]{0:T(128)S(1)}, f32[12]{0:T(128)}, u32[]{:S(2)}) copy-start(f32[12]{0:T(128)} %slope_ref.1) | copy-start | bytes 148
  87.7 25.0 %all-to-all-start.2 = ((bf16[128,6,128]{2,1,0:T(8,128)(2,1)}), bf16[128,6,128]{2,1,0:T(8,128)(2,1)S(1)}, u32[]{:S(2)}, u32[]{:S(2)}) async-start(bf16[128,6,128]{2,1,0:T(8,128)(2,1)} %temporal_forward.1), calls=%async_computation.2 | async-start | bytes 524288 | tf_op jit(solution)/shard_map/all_to_all | solution.py:344
  96.1 62.5 %all-gather.11.cloned.1.call-start = ((), (), s32[]{:S(2)}) async-start(), calls=%async_computation.7 | async-start | bytes 2359296 | tf_op jit(solution)/shard_map/all_gather | solution.py:435
  124.8 30.9 %all-to-all-start.3 = ((bf16[128,6,128]{2,1,0:T(8,128)(2,1)}), bf16[128,6,128]{2,1,0:T(8,128)(2,1)S(1)}, u32[]{:S(2)}, u32[]{:S(2)}) async-start(bf16[128,6,128]{2,1,0:T(8,128)(2,1)} %get-tuple-element.21), calls=%async_computation.3 | async-start | bytes 524288 | tf_op jit(solution)/shard_map/all_to_all | solution.py:344
  158.5 30.5 %all-to-all-start.4 = ((bf16[16,24,768]{2,1,0:T(8,128)(2,1)}), bf16[16,24,768]{2,1,0:T(8,128)(2,1)S(1)}, u32[]{:S(2)}, u32[]{:S(2)}) async-start(bf16[16,24,768]{2,1,0:T(8,128)(2,1)} %temporal_backward.1), calls=%async_computation.4 | async-start | bytes 1179648 | tf_op jit(solution)/shard_map/all_to_all | solution.py:344
Sparse Core Ops, SparseCore 0:
  10.2 41.9 all-gather.8
  58.9 49.9 all-gather.6
  124.9 29.3 all-gather.10

commit v12 on v11

--- a/solution.py
+++ b/solution.py
@@ -75,6 +75,26 @@
     source = jnp.where((g >> 2) == src, a * 16 + 12 + (g & 3), -1)
     column = lax.broadcasted_iota(jnp.int32, (2 * third, 16 * tm), 1)
     return jnp.where(column == source, 1.0, 0.0).astype(BF16)
+
+
+def join_kernel(res_hbm, cot_hbm, o_hbm, both, sem):
+    width = res_hbm.shape[-1]
+    part = both.shape[0] // 4
+    loads, stores = [], []
+    for i in range(4):
+        at = pl.ds(i * part, part)
+        for j, src in enumerate((res_hbm, cot_hbm)):
+            dst = both.at[at, :, pl.ds(j * width, width)]
+            loads.append(pltpu.make_async_copy(src.at[0, at], dst, sem.at[0, i, j]))
+            loads[-1].start()
+    for i in range(4):
+        at = pl.ds(i * part, part)
+        loads[2 * i].wait()
+        loads[2 * i + 1].wait()
+        stores.append(pltpu.make_async_copy(both.at[at], o_hbm.at[at], sem.at[1, i, 0]))
+        stores[-1].start()
+    for c in stores:
+        c.wait()
 
 
 def first_kernel(fc_hbm, out_hbm, qkv_hbm, o_ref, fc_ref, out_ref, qkv_ref, sem):
@@ -347,7 +367,15 @@
     to_steps = jnp.asarray(transposed_rows(tubes, steps))
     to_order = jnp.asarray(transposed_rows(tm, sp))
     me = lax.axis_index("space").astype(jnp.int32).reshape(1)
-    rest = jnp.concatenate([residual_in[0], cotangent[0]], axis=-1)
+    rest = pl.pallas_call(
+        join_kernel,
+        out_shape=shape((steps, tubes, 2 * width), BF16),
+        in_specs=[HBM] * 2,
+        out_specs=HBM,
+        scratch_shapes=[pltpu.VMEM((steps, tubes, 2 * width), BF16), pltpu.SemaphoreType.DMA((2, 4, 2))],
+        compiler_params=params(56),
+        name="join",
+    )(residual_in, cotangent)
     rest, fc_weight = lax.optimization_barrier((rest, fc_weight))
     shards = pl.pallas_call(
         first_kernel,

time: 197 us -> 197 us (level)
  other arithmetic: 2.01 us -> 0 us
  Pallas kernels: 23.7 us -> 25.7 us
    concatenate x1 -> x0, other arithmetic: 2.01 us -> none  [body(): rest = jnp.concatenate([residual_in[0], cotangent[0]], axis=-1)]
where the time goes in v12:
time: 197 us
  blocking collectives  72.9 us (37%)
  waiting for transfers between devices  55.3 us (28%)
  starting transfers between devices  28.7 us (15%)
  Pallas kernels  25.7 us (13%)
  between operations  13.9 us (7%)
    all_to_all x2, blocking collectives, exchange(): return lax.all_to_all(x, axes, split_axis=0, concat_axis=0, tiled=True)  72.9 us
    all_to_all x3, waiting for transfers between devices, exchange(): return lax.all_to_all(x, axes, split_axis=0, concat_axis=0, tiled=True)  55.2 us
    all_to_all x3, starting transfers between devices, exchange(): return lax.all_to_all(x, axes, split_axis=0, concat_axis=0, tiled=True)  28.6 us
    pallas_call x1, Pallas kernels, body(): pl.pallas_call(middle_kernel, out_shape=(shape((total, width), BF16), sha...  12 us
  transfers between devices with their start and end apart: 6, of which 3 were waited for; matrix products, arithmetic and copies ran while one was open for 0% of the time, Pallas kernels for 5%

profile of v12, /device:TPU:8, one launch (start us, length us, event | category | flops | bytes accessed | tf_op | source)
XLA Modules:
  0.0 196.6 jit_solution(567221605103957053)
XLA Ops:
  7.2 0.0 all-gather.9.cloned.1.call-start
  7.3 2.0 join.1
  9.2 0.0 all-gather.9.cloned.1.call-update
  9.2 0.0 all-gather.7.cloned.1.call-start
  9.3 1.9 first.1
  11.2 46.1 %all_to_all.25.x_ref = bf16[16,40,768]{2,1,0:T(8,128)(2,1)S(1)} all-to-all(bf16[16,40,768]{2,1,0:T(8,128)(2,1)} %first.1), channel_id=1, replica_groups=mesh['tm'=16,'space'=8,'dp'=4] {'tm'}, dimensions={0} | all-to-all | bytes 1966080 | tf_op jit(solution)/shard_map/all_to_all | solution.py:364
  57.3 1.4 weights_unpack.1
  58.8 0.3 pack.1
  59.1 26.8 %all_to_all.26.x_ref = bf16[16,24,768]{2,1,0:T(8,128)(2,1)S(1)} all-to-all(bf16[16,24,768]{2,1,0:T(8,128)(2,1)S(1)} %pack.1), channel_id=1, replica_groups=mesh['tm'=16,'space'=8,'dp'=4] {'tm'}, dimensions={0} | all-to-all | bytes 1179648 | tf_op jit(solution)/shard_map/all_to_all | solution.py:364
  85.9 1.8 temporal_forward.1
  87.7 8.3 %all-to-all-start.2 = ((bf16[128,6,128]{2,1,0:T(8,128)(2,1)}), bf16[128,6,128]{2,1,0:T(8,128)(2,1)S(1)}, u32[]{:S(2)}, u32[]{:S(2)}) async-start(bf16[128,6,128]{2,1,0:T(8,128)(2,1)} %temporal_forward.1), calls=%async_computation.2 | async-start | bytes 524288 | tf_op jit(solution)/shard_map/all_to_all | solution.py:364
  96.0 0.0 all-gather.11.cloned.1.call-start
  96.1 0.1 copy.19.row_ref
  96.2 16.4 %all-to-all-done.2.x_ref = bf16[128,6,128]{2,1,0:T(8,128)(2,1)S(1)} async-done(((bf16[128,6,128]{2,1,0:T(8,128)(2,1)}), bf16[128,6,128]{2,1,0:T(8,128)(2,1)S(1)}, u32[]{:S(2)}, u32[]{:S(2)}) %all-to-all-start.2) | async-done | bytes 196640 | tf_op jit(solution)/shard_map/all_to_all | solution.py:364
  112.7 12.0 %middle.1 = (bf16[128,1024]{1,0:T(8,128)(2,1)}, bf16[128,6,128]{2,1,0:T(8,128)(2,1)}) custom-call(s32[1]{0:T(128)} %bitcast.me_ref, bf16[8,640,768]{2,1,0:T(8,128)(2,1)} %bitcast.8, bf16[128,6,128]{2,1,0:T(8,128)(2,1)S(1)} %all-to-all-done.2.x_ref, bf16[8,8,16,2048]{3,2,1,0:T(8,128)(2,1)} %bitcast.9, f32[1,1024]{1,0:T(1,128)S(1)} %bitcast.7, ...), custom_call_target="tpu_custom_call" | custom-call | flops 4000000000 | bytes 10000000 | tf_op jit(solution)/shard_map/middle/pallas_call | solution.py:432
  124.7 0.0 all-gather.11.cloned.1.call-update
  124.7 12.5 %all-to-all-start.3 = ((bf16[128,6,128]{2,1,0:T(8,128)(2,1)}), bf16[128,6,128]{2,1,0:T(8,128)(2,1)S(1)}, u32[]{:S(2)}, u32[]{:S(2)}) async-start(bf16[128,6,128]{2,1,0:T(8,128)(2,1)} %get-tuple-element.21), calls=%async_computation.3 | async-start | bytes 524288 | tf_op jit(solution)/shard_map/all_to_all | solution.py:364
  137.2 0.7 temporal_probs.1.p_ref
  138.0 17.7 %all-to-all-done.3.g_ref = bf16[128,6,128]{2,1,0:T(8,128)(2,1)S(1)} async-done(((bf16[128,6,128]{2,1,0:T(8,128)(2,1)}), bf16[128,6,128]{2,1,0:T(8,128)(2,1)S(1)}, u32[]{:S(2)}, u32[]{:S(2)}) %all-to-all-start.3) | async-done | bytes 196640 | tf_op jit(solution)/shard_map/all_to_all | solution.py:364
  155.7 2.9 %temporal_backward.1 = bf16[16,24,768]{2,1,0:T(8,128)(2,1)} custom-call(bf16[16,24,768]{2,1,0:T(8,128)(2,1)S(1)} %all_to_all.26.x_ref, f32[6,128,256]{2,1,0:T(8,128)S(1)} %temporal_probs.1.p_ref, bf16[128,6,128]{2,1,0:T(8,128)(2,1)S(1)} %all-to-all-done.3.g_ref), custom_call_target="tpu_custom_call" | custom-call | flops 300000000 | bytes 2000000 | tf_op jit(solution)/shard_map/temporal_backward/pallas_call | solution.py:476
  158.5 7.8 %all-to-all-start.4 = ((bf16[16,24,768]{2,1,0:T(8,128)(2,1)}), bf16[16,24,768]{2,1,0:T(8,128)(2,1)S(1)}, u32[]{:S(2)}, u32[]{:S(2)}) async-start(bf16[16,24,768]{2,1,0:T(8,128)(2,1)} %temporal_backward.1), calls=%async_computation.4 | async-start | bytes 1179648 | tf_op jit(solution)/shard_map/all_to_all | solution.py:364
  166.3 1.7 slice.1
  168.0 21.1 %all-to-all-done.4.x_ref = bf16[16,24,768]{2,1,0:T(8,128)(2,1)S(1)} async-done(((bf16[16,24,768]{2,1,0:T(8,128)(2,1)}), bf16[16,24,768]{2,1,0:T(8,128)(2,1)S(1)}, u32[]{:S(2)}, u32[]{:S(2)}) %all-to-all-start.4) | async-done | bytes 589856 | tf_op jit(solution)/shard_map/all_to_all | solution.py:364
  189.1 1.0 unpack.1
  (20 shorter events, 0.1 us)
Async XLA Ops:
  7.2 51.6 %copy-start.7 = (bf16[128,128]{1,0:T(8,128)(2,1)S(1)}, bf16[128,128]{1,0:T(8,128)(2,1)}, u32[]{:S(2)}) copy-start(bf16[128,128]{1,0:T(8,128)(2,1)} %constant.10.clone.turn_ref) | copy-start | bytes 98308
  7.2 51.6 %copy-start.2 = (bf16[1,8,16,768]{3,2,1,0:T(8,128)(2,1)S(1)}, bf16[1,8,16,768]{3,2,1,0:T(8,128)(2,1)}, u32[]{:S(2)}) copy-start(bf16[1,8,16,768]{3,2,1,0:T(8,128)(2,1)} %q_ref.1) | copy-start | bytes 589828
  7.2 51.6 %copy-start.3 = (bf16[1,8,16,768]{3,2,1,0:T(8,128)(2,1)S(1)}, bf16[1,8,16,768]{3,2,1,0:T(8,128)(2,1)}, u32[]{:S(2)}) copy-start(bf16[1,8,16,768]{3,2,1,0:T(8,128)(2,1)} %k_ref.1) | copy-start | bytes 589828
  7.2 51.6 %copy-start.4 = (bf16[1,8,16,768]{3,2,1,0:T(8,128)(2,1)S(1)}, bf16[1,8,16,768]{3,2,1,0:T(8,128)(2,1)}, u32[]{:S(2)}) copy-start(bf16[1,8,16,768]{3,2,1,0:T(8,128)(2,1)} %v_ref.1) | copy-start | bytes 589828
  7.2 105.4 %all-gather.9.cloned.1.call-start = ((), (), s32[]{:S(2)}) async-start(), calls=%async_computation.6 | async-start | bytes 4718592 | tf_op jit(solution)/shard_map/all_gather | solution.py:394
  9.2 103.4 %all-gather.7.cloned.1.call-start = ((), (), s32[]{:S(2)}) async-start(), calls=%async_computation.5 | async-start | bytes 8847360 | tf_op jit(solution)/shard_map/all_gather | solution.py:415
  57.3 38.8 %copy-start.1 = (s32[1,128]{1,0:T(1,128)S(1)}, s32[1,128]{1,0:T(1,128)}, u32[]{:S(2)}) copy-start(s32[1,128]{1,0:T(1,128)} %col_ref.1) | copy-start | bytes 1540
  57.3 55.4 %copy-start = (bf16[128,128]{1,0:T(8,128)(2,1)S(1)}, bf16[128,128]{1,0:T(8,128)(2,1)}, u32[]{:S(2)}) copy-start(bf16[128,128]{1,0:T(8,128)(2,1)} %constant.11.clone.turn_ref) | copy-start | bytes 98308
  57.3 55.4 %copy-start.5 = (f32[1024]{0:T(1024)S(1)}, f32[1024]{0:T(1024)}, u32[]{:S(2)}) copy-start(f32[1024]{0:T(1024)} %param.19) | copy-start | bytes 12292
  57.3 55.4 %copy-start.6 = (f32[12]{0:T(128)S(1)}, f32[12]{0:T(128)}, u32[]{:S(2)}) copy-start(f32[12]{0:T(128)} %slope_ref.1) | copy-start | bytes 148
  87.7 24.9 %all-to-all-start.2 = ((bf16[128,6,128]{2,1,0:T(8,128)(2,1)}), bf16[128,6,128]{2,1,0:T(8,128)(2,1)S(1)}, u32[]{:S(2)}, u32[]{:S(2)}) async-start(bf16[128,6,128]{2,1,0:T(8,128)(2,1)} %temporal_forward.1), calls=%async_computation.2 | async-start | bytes 524288 | tf_op jit(solution)/shard_map/all_to_all | solution.py:364
  96.0 62.5 %all-gather.11.cloned.1.call-start = ((), (), s32[]{:S(2)}) async-start(), calls=%async_computation.7 | async-start | bytes 2359296 | tf_op jit(solution)/shard_map/all_gather | solution.py:463
  124.7 30.9 %all-to-all-start.3 = ((bf16[128,6,128]{2,1,0:T(8,128)(2,1)}), bf16[128,6,128]{2,1,0:T(8,128)(2,1)S(1)}, u32[]{:S(2)}, u32[]{:S(2)}) async-start(bf16[128,6,128]{2,1,0:T(8,128)(2,1)} %get-tuple-element.21), calls=%async_computation.3 | async-start | bytes 524288 | tf_op jit(solution)/shard_map/all_to_all | solution.py:364
  158.5 30.5 %all-to-all-start.4 = ((bf16[16,24,768]{2,1,0:T(8,128)(2,1)}), bf16[16,24,768]{2,1,0:T(8,128)(2,1)S(1)}, u32[]{:S(2)}, u32[]{:S(2)}) async-start(bf16[16,24,768]{2,1,0:T(8,128)(2,1)} %temporal_backward.1), calls=%async_computation.4 | async-start | bytes 1179648 | tf_op jit(solution)/shard_map/all_to_all | solution.py:364
Sparse Core Ops, SparseCore 0:
  10.2 41.9 all-gather.8
  58.9 49.9 all-gather.6
  124.9 29.3 all-gather.10
